TPU v7x, 32 devices: a whole 2x2x4 slice. The times are simulated.
32 devices in a mesh: groups: 2 (over y), ctx: 4 (over z), chan: 2 (over x), grp: 2 (over core).
Axes of the slice: x: 2, y: 2, z: 4, core: 2. Of those that a mesh axis runs over, the one named last changes fastest.
Arguments:
- events: bfloat16 [4, 1024, 2048], P('groups', 'ctx', 'chan'), parts along dimension 0, may hold values from -6 to 6
- gap_bins: int32 [4, 1024], P('groups', 'ctx'), parts along dimension 0, may hold values from 0 to 63
- lengths: int32 [4], P('groups'), parts along dimension 0, may hold values from 128 to 1024, as said below
- gap_table: float32 [64], replicated, may hold values from 0.5 to 1024, as said below
- decay_rate: float32 [2048], P(('chan', 'grp')), may hold values from 0 to 1, as said below
- frequency: float32 [2048], P(('chan', 'grp')), may hold values from -3.140625 to 3.140625
- in_proj: bfloat16 [2048, 2, 2048], P(None, None, ('chan', 'grp')), may hold values from -0.125 to 0.125
- out_proj: bfloat16 [2, 2048, 2048], P(None, ('chan', 'grp')), may hold values from -0.09375 to 0.09375
- skip_gain: float32 [2048], P(('chan', 'grp')), may hold values from -4 to 4
Outputs:
- layer_out: bfloat16 [4, 1024, 2048], P('groups', 'ctx', ('chan', 'grp')), parts along dimension 0
There are 2 independent parts, one for each index of `groups`. A program takes and returns all parts, laid end to end along the dimension named above; an argument that names none is the same for every part. Nothing has to cross between parts.
Inputs may be any that keep to these rules, and one draw needn't show every extreme that they name: `lengths`: some user has 1024. `gap_table`: positive. `decay_rate`: positive.
All inputs are finite; a program needn't handle non-finite values.
Results may differ from a plain program's by a relative error of at most 0.0035.
Values may be sent and summed in bfloat16 or wider, within the bound.
No kernel may reach another device: no remote copies, remote signals or barrier semaphores. Data moves between devices by JAX's collectives and lax.ppermute only.
A program may use at most 128 MiB of HBM per device.

v0:
```python
import jax
import jax.numpy as jnp
from jax import lax
from jax.sharding import PartitionSpec as P


def entering(array, axis, combine, identity):
    size, position = (lax.axis_size(axis), lax.axis_index(axis))
    everything = jax.tree.map(lambda part: lax.all_gather(part, axis), array)
    start = jax.tree.map(
        lambda part, zero: jnp.broadcast_to(jnp.asarray(zero, part.dtype), part.shape),
        array,
        identity,
    )

    def hop(k, before):
        reached = k < position
        new = combine(before, jax.tree.map(lambda part: part[k], everything))
        return jax.tree.map(lambda a, b: jnp.where(reached, a, b), new, before)

    return lax.fori_loop(0, size, hop, start)


def combine(earlier, later):
    first_re, first_im, base_re, base_im = earlier
    second_re, second_im, extra_re, extra_im = later
    return (
        first_re * second_re - first_im * second_im,
        first_re * second_im + first_im * second_re,
        second_re * base_re - second_im * base_im + extra_re,
        second_re * base_im + second_im * base_re + extra_im,
    )


def local(
    events, gap_bins, lengths, gap_table, decay_rate, frequency, in_proj, out_proj, skip_gain
):
    user_count, seg_rows, chan_width = events.shape
    model_width = in_proj.shape[0]
    local_states = decay_rate.shape[0]
    drive = jnp.einsum(
        "ush,hcq->scuq",
        lax.all_gather(events, "chan", axis=2, tiled=True),
        in_proj,
        preferred_element_type=jnp.float32,
    )
    bins_first = jnp.transpose(gap_bins)
    bin_range = jnp.arange(gap_table.shape[0], dtype=jnp.int32)
    hits = bins_first[..., None] == bin_range
    gaps = jnp.sum(jnp.where(hits, gap_table, 0.0), axis=-1)
    scaled = gaps[..., None] * decay_rate
    magnitude = jnp.exp(-scaled)
    turned = gaps[..., None] * frequency
    decay_re = magnitude * jnp.cos(turned)
    decay_im = magnitude * jnp.sin(turned)
    norm_in = jnp.sqrt(-jnp.expm1(-2.0 * scaled))
    drive_re = norm_in * drive[:, 0]
    drive_im = norm_in * drive[:, 1]
    running = lax.associative_scan(combine, (decay_re, decay_im, drive_re, drive_im), axis=0)
    summary = tuple((item[-1] for item in running))
    ones_part = jnp.ones((user_count, local_states), jnp.float32)
    zeroed_portion = jnp.zeros((user_count, local_states), jnp.float32)
    incoming = entering(
        summary, "ctx", combine, (ones_part, zeroed_portion, zeroed_portion, zeroed_portion)
    )
    carry_re = incoming[2][None]
    carry_im = incoming[3][None]
    first_re = decay_re[:1] * carry_re - decay_im[:1] * carry_im + drive_re[:1]
    first_im = decay_re[:1] * carry_im + decay_im[:1] * carry_re + drive_im[:1]
    start_re = jnp.concatenate([first_re, drive_re[1:]], axis=0)
    start_im = jnp.concatenate([first_im, drive_im[1:]], axis=0)
    again = lax.associative_scan(combine, (decay_re, decay_im, start_re, start_im), axis=0)
    state_re = again[2]
    state_im = again[3]
    states = jnp.stack([state_re, state_im], 1).astype(jnp.bfloat16)
    chan_count = lax.axis_size("chan")
    grp_count = lax.axis_size("grp")
    part_width = model_width // (chan_count * grp_count)
    blocked = out_proj.reshape(2, local_states, chan_count * grp_count, part_width)
    terms = jnp.einsum("scuq,cqkh->kush", states, blocked, preferred_element_type=jnp.float32)
    summed = lax.psum_scatter(terms, ("chan", "grp"), scatter_dimension=0, tiled=True)[0]
    own_events = lax.dynamic_slice_in_dim(
        events, lax.axis_index("grp") * part_width, part_width, 2
    ).astype(jnp.float32)
    before = summed + skip_gain * own_events
    result = jax.nn.gelu(before)
    target_positions = lax.axis_index("ctx") * seg_rows + jnp.arange(seg_rows, dtype=jnp.int32)
    valid = target_positions[None, :] < lengths[:, None]
    return jnp.where(valid[..., None], result, 0.0).astype(jnp.bfloat16)


def solution(mesh):
    return jax.shard_map(
        local,
        mesh=mesh,
        in_specs=(
            P("groups", "ctx", "chan"),
            P("groups", "ctx"),
            P("groups"),
            P(),
            P(("chan", "grp")),
            P(("chan", "grp")),
            P(None, None, ("chan", "grp")),
            P(None, ("chan", "grp"), None),
            P(("chan", "grp")),
        ),
        out_specs=P("groups", "ctx", ("chan", "grp")),
        check_vma=False,
    )
```

profile of v0, /device:TPU:1, one launch (start us, length us, event | category | flops | bytes accessed | tf_op | source)
XLA Modules:
  0.0 544.0 jit_solution(16143298024461174301)
XLA Ops:
  8.1 36.0 %all-gather.2.cloned.1.call-done = bf16[2,256,2048]{2,1,0:T(8,128)(2,1)} async-done(((bf16[2,256,1024]{2,1,0:T(8,128)(2,1)}), bf16[2,256,2048]{2,1,0:T(8,128)(2,1)}) %all-gather.2.cloned.1.call-update) | async-done | bytes 2097168 | tf_op jit(solution)/shard_map/all_gather | solution.py:43
  44.1 5.2 fusion.10
  49.4 5.9 %fusion.22 = (f32[256,2,512]{2,0,1:T(8,128)S(1)}, f32[256,2,512]{2,0,1:T(8,128)S(1)}, f32[256,2,512]{2,0,1:T(8,128)S(1)}, f32[256,2,512]{2,0,1:T(8,128)}) fusion(f32[256,2,2,512]{3,0,2,1:T(8,128)S(1)} %fusion.10, f32[512]{0:T(512)S(1)} %copy-done.45, f32[256,2]{0,1:T(2,128)S(1)} %select_reduce_fusion, f32[512]{0:T(512)S(1)} %copy-done.46), kind=kLoop, calls=%fused_computation.32 | loop fusion | flops 2359296 | bytes 6297600 | tf_op jit(solution)/shard_map/mul | solution.py:57
  55.3 2.3 slice.839
  70.5 4.1 slice.760
  74.6 4.1 slice.827
  78.7 4.1 slice.759
  82.9 3.4 add_add_fusion.3
  134.4 4.1 slice.984
  138.5 4.1 slice.916
  271.2 2.3 pad.348
  283.5 2.3 pad.316
  301.7 2.6 pad.350
  306.0 2.5 pad.318
  310.2 2.6 pad.320
  312.8 2.5 pad.319
  315.3 2.5 pad.321
  319.6 2.6 pad.352
  322.2 2.6 pad.351
  324.8 2.6 pad.353
  329.5 3.0 pad.687
  333.3 10.8 %all_gather.19 = f32[4,2,512]{2,1,0:T(2,128)} all-gather(f32[1,2,512]{2,1,0:T(2,128)S(1)} %copy.30), channel_id=1, replica_groups=mesh['groups'=2,'ctx'=4,'chan'=2,'grp'=2] {'ctx'}, dimensions={0}, use_global_device_ids=true | all-gather | bytes 20480 | tf_op jit(solution)/shard_map/all_gather | solution.py:9
  346.1 3.0 pad.685
  349.9 10.8 %all_gather.18 = f32[4,2,512]{2,1,0:T(2,128)} all-gather(f32[1,2,512]{2,1,0:T(2,128)S(1)} %copy.29), channel_id=1, replica_groups=mesh['groups'=2,'ctx'=4,'chan'=2,'grp'=2] {'ctx'}, dimensions={0}, use_global_device_ids=true | all-gather | bytes 20480 | tf_op jit(solution)/shard_map/all_gather | solution.py:9
  362.8 3.0 pad.683
  366.6 10.9 %all_gather.16 = f32[4,2,512]{2,1,0:T(2,128)} all-gather(f32[1,2,512]{2,1,0:T(2,128)S(1)} %copy.27), channel_id=1, replica_groups=mesh['groups'=2,'ctx'=4,'chan'=2,'grp'=2] {'ctx'}, dimensions={0}, use_global_device_ids=true | all-gather | bytes 20480 | tf_op jit(solution)/shard_map/all_gather | solution.py:9
  379.6 3.0 pad.681
  383.4 10.9 %all_gather.15 = f32[4,2,512]{2,1,0:T(2,128)} all-gather(f32[1,2,512]{2,1,0:T(2,128)S(1)} %copy.26), channel_id=1, replica_groups=mesh['groups'=2,'ctx'=4,'chan'=2,'grp'=2] {'ctx'}, dimensions={0}, use_global_device_ids=true | all-gather | bytes 20480 | tf_op jit(solution)/shard_map/all_gather | solution.py:9
  394.3 5.3 while.16
  432.5 4.4 fusion.8
  438.3 95.8 %all-reduce.99.cloned.1.call-done = f32[4,2,256,512]{3,2,0,1:T(8,128)} async-done(((f32[4,2,256,512]{3,2,0,1:T(8,128)}), f32[4,2,256,512]{3,2,0,1:T(8,128)}) %all-reduce.99.cloned.1.call-update) | async-done | bytes 4194320
  534.1 3.1 fusion.31
  (452 shorter events, 271.7 us)
Async XLA Ops:
  6.5 37.6 %all-gather.2.cloned.1.call-start = ((), (), s32[]{:S(2)}) async-start(), calls=%async_computation | async-start | bytes 3145728 | tf_op jit(solution)/shard_map/all_gather | solution.py:43
  7.3 526.8 %all-reduce.99.cloned.1.call-start = ((), (), s32[]{:S(2)}) async-start(), calls=%async_computation.1 | async-start | bytes 8388608
  44.1 5.2 copy-start.45
  44.1 5.2 copy-start.46
  55.3 19.3 %copy-start = (f32[256,2,512]{2,0,1:T(8,128)}, f32[256,2,512]{2,0,1:T(8,128)S(1)}, u32[]{:S(2)}) copy-start(f32[256,2,512]{2,0,1:T(8,128)S(1)} %get-tuple-element.315) | copy-start | bytes 3145732
  109.9 22.5 %copy-start.18 = (f32[32,2,512]{2,0,1:T(8,128)}, f32[32,2,512]{2,0,1:T(8,128)S(1)}, u32[]{:S(2)}) copy-start(f32[32,2,512]{2,0,1:T(8,128)S(1)} %slice.770) | copy-start | bytes 393220
  117.8 14.6 %copy-start.24 = (f32[16,2,512]{2,0,1:T(8,128)}, f32[16,2,512]{2,0,1:T(8,128)S(1)}, u32[]{:S(2)}) copy-start(f32[16,2,512]{2,0,1:T(8,128)S(1)} %slice.777) | copy-start | bytes 196612
  117.8 14.6 %copy-start.25 = (f32[16,2,512]{2,0,1:T(8,128)}, f32[16,2,512]{2,0,1:T(8,128)S(1)}, u32[]{:S(2)}) copy-start(f32[16,2,512]{2,0,1:T(8,128)S(1)} %slice.775) | copy-start | bytes 196612
  123.0 9.4 %copy-start.28 = (f32[8,2,512]{2,0,1:T(8,128)}, f32[8,2,512]{2,0,1:T(8,128)S(1)}, u32[]{:S(2)}) copy-start(f32[8,2,512]{2,0,1:T(8,128)S(1)} %slice.782) | copy-start | bytes 98308
  123.1 9.4 %copy-start.29 = (f32[8,2,512]{2,0,1:T(8,128)}, f32[8,2,512]{2,0,1:T(8,128)S(1)}, u32[]{:S(2)}) copy-start(f32[8,2,512]{2,0,1:T(8,128)S(1)} %slice.780) | copy-start | bytes 98308
  127.5 4.9 copy-start.33
  127.6 4.9 copy-start.34
  290.4 9.5 %copy-start.3 = (f32[63,2,512]{2,0,1:T(8,128)S(1)}, f32[63,2,512]{2,0,1:T(8,128)}, u32[]{:S(2)}) copy-start(f32[63,2,512]{2,0,1:T(8,128)} %slice.822) | copy-start | bytes 774148
  290.4 9.5 %copy-start.6 = (f32[64,2,512]{2,0,1:T(8,128)S(1)}, f32[64,2,512]{2,0,1:T(8,128)}, u32[]{:S(2)}) copy-start(f32[64,2,512]{2,0,1:T(8,128)} %pad.346) | copy-start | bytes 786436
  290.4 9.5 %copy-start.7 = (f32[64,2,512]{2,0,1:T(8,128)S(1)}, f32[64,2,512]{2,0,1:T(8,128)}, u32[]{:S(2)}) copy-start(f32[64,2,512]{2,0,1:T(8,128)} %pad.348) | copy-start | bytes 786436
  290.4 9.5 %copy-start.8 = (f32[64,2,512]{2,0,1:T(8,128)S(1)}, f32[64,2,512]{2,0,1:T(8,128)}, u32[]{:S(2)}) copy-start(f32[64,2,512]{2,0,1:T(8,128)} %pad.347) | copy-start | bytes 786436
  290.4 9.5 %copy-start.9 = (f32[64,2,512]{2,0,1:T(8,128)S(1)}, f32[64,2,512]{2,0,1:T(8,128)}, u32[]{:S(2)}) copy-start(f32[64,2,512]{2,0,1:T(8,128)} %pad.349) | copy-start | bytes 786436
  290.4 9.5 %copy-start.20 = (f32[63,2,512]{2,0,1:T(8,128)S(1)}, f32[63,2,512]{2,0,1:T(8,128)}, u32[]{:S(2)}) copy-start(f32[63,2,512]{2,0,1:T(8,128)} %slice.905) | copy-start | bytes 774148
  290.5 9.5 %copy-start.21 = (f32[63,2,512]{2,0,1:T(8,128)S(1)}, f32[63,2,512]{2,0,1:T(8,128)}, u32[]{:S(2)}) copy-start(f32[63,2,512]{2,0,1:T(8,128)} %slice.902) | copy-start | bytes 774148
  290.5 10.5 %copy-start.42 = (f32[1,2,512]{2,0,1:T(1,128)S(1)}, f32[1,2,512]{2,0,1:T(1,128)}, u32[]{:S(2)}) copy-start(f32[1,2,512]{2,0,1:T(1,128)} %slice.1037) | copy-start | bytes 12292
  401.0 5.6 %copy-start.1 = (f32[128,2,512]{2,0,1:T(8,128)S(1)}, f32[128,2,512]{2,0,1:T(8,128)}, u32[]{:S(2)}) copy-start(f32[128,2,512]{2,0,1:T(8,128)} %slice.762) | copy-start | bytes 1572868
  401.0 5.6 %copy-start.2 = (f32[128,2,512]{2,0,1:T(8,128)S(1)}, f32[128,2,512]{2,0,1:T(8,128)}, u32[]{:S(2)}) copy-start(f32[128,2,512]{2,0,1:T(8,128)} %slice.760) | copy-start | bytes 1572868
  405.9 5.2 copy-start.11
  406.0 5.2 copy-start.12
  411.2 7.2 %copy-start.30 = (f32[3,2,512]{2,0,1:T(4,128)S(1)}, f32[3,2,512]{2,0,1:T(4,128)}, u32[]{:S(2)}) copy-start(f32[3,2,512]{2,0,1:T(4,128)} %slice.802) | copy-start | bytes 36868
  411.2 7.5 %copy-start.26 = (f32[7,2,512]{2,0,1:T(8,128)S(1)}, f32[7,2,512]{2,0,1:T(8,128)}, u32[]{:S(2)}) copy-start(f32[7,2,512]{2,0,1:T(8,128)} %slice.810) | copy-start | bytes 86020
  411.2 7.5 %copy-start.27 = (f32[7,2,512]{2,0,1:T(8,128)S(1)}, f32[7,2,512]{2,0,1:T(8,128)}, u32[]{:S(2)}) copy-start(f32[7,2,512]{2,0,1:T(8,128)} %slice.807) | copy-start | bytes 86020
  412.4 6.6 %copy-start.22 = (f32[15,2,512]{2,0,1:T(8,128)S(1)}, f32[15,2,512]{2,0,1:T(8,128)}, u32[]{:S(2)}) copy-start(f32[15,2,512]{2,0,1:T(8,128)} %slice.815) | copy-start | bytes 184324
  412.4 6.6 %copy-start.23 = (f32[15,2,512]{2,0,1:T(8,128)S(1)}, f32[15,2,512]{2,0,1:T(8,128)}, u32[]{:S(2)}) copy-start(f32[15,2,512]{2,0,1:T(8,128)} %slice.812) | copy-start | bytes 184324
  412.8 6.5 %copy-start.16 = (f32[31,2,512]{2,0,1:T(8,128)S(1)}, f32[31,2,512]{2,0,1:T(8,128)}, u32[]{:S(2)}) copy-start(f32[31,2,512]{2,0,1:T(8,128)} %slice.817) | copy-start | bytes 380932
  436.9 97.2 %copy-start.10 = (bf16[2,256,1024]{2,1,0:T(8,128)(2,1)S(1)}, bf16[2,256,1024]{2,1,0:T(8,128)(2,1)}, u32[]{:S(2)}) copy-start(bf16[2,256,1024]{2,1,0:T(8,128)(2,1)} %param.11) | copy-start | bytes 3145732
  436.9 97.2 %copy-start.47 = (f32[512]{0:T(512)S(1)}, f32[512]{0:T(512)}, u32[]{:S(2)}) copy-start(f32[512]{0:T(512)} %param.19) | copy-start | bytes 6148
  (21 other events, 46.9 us)
Sparse Core Ops, SparseCore 0:
  8.9 35.1 all-gather.1
  437.1 96.9 all-reduce.98
where the time goes:
time: 551 us; the launch traced here: 544 us
  local copies, waits for them, and re-layouts  215 us (39%)
  waiting for transfers between devices  133 us (24%)
  other arithmetic  129 us (23%)
  blocking collectives  43.3 us (8%)
  between operations  14.9 us (3%)
  matrix products  9.6 us (2%)
    pad x48, local copies, waits for them, and re-layouts, local(): lax.associative_scan(combine, (decay_re, decay_im, drive_re, drive_im), a...  102 us
    unnamed x3, waiting for transfers between devices  96.5 us
    slice x101, local copies, waits for them, and re-layouts, local(): lax.associative_scan(combine, (decay_re, decay_im, drive_re, drive_im), a...  67.6 us
    all_gather x4, blocking collectives, entering(): everything = jax.tree.map(lambda part: lax.all_gather(part, axis), array)  43.3 us
    add x26, other arithmetic, local(): lax.associative_scan(combine, (decay_re, decay_im, drive_re, drive_im), a...  40.4 us
    all_gather x1, waiting for transfers between devices, local(): lax.all_gather(events, 'chan', axis=2, tiled=True)  36 us
    concatenate x22, other arithmetic, local(): lax.associative_scan(combine, (decay_re, decay_im, drive_re, drive_im), a...  31.1 us
    add x26, other arithmetic, combine(): second_re * base_im + second_im * base_re + extra_im  21.3 us
  transfers between devices with their start and end apart: 2, of which 2 were waited for; matrix products, arithmetic and copies ran while one was open for 0% of the time, Pallas kernels for 0%

commit v1 on v0

v1 whole, which is shorter than its diff:
```python
import functools

import jax
import jax.numpy as jnp
from jax import lax
from jax.experimental import pallas as pl
from jax.experimental.pallas import tpu as pltpu
from jax.sharding import PartitionSpec as P

F32 = jnp.float32
BF16 = jnp.bfloat16
SEGS = 8
VMEM = 48 * 1024 * 1024


def dot(a, b):
    return jnp.dot(a, b, preferred_element_type=F32)


def cmul(ar, ai, br, bi):
    return ar * br - ai * bi, ar * bi + ai * br


def order_matrix(tokens):
    steps = tokens // SEGS
    r = lax.broadcasted_iota(jnp.int32, (tokens, tokens), 0)
    t = lax.broadcasted_iota(jnp.int32, (tokens, tokens), 1)
    return (t == (r % SEGS) * steps + r // SEGS).astype(F32).astype(BF16)


def run_starts(ar, ai, er, ei):
    cr, ci = jnp.zeros_like(er[:1]), jnp.zeros_like(ei[:1])
    rows_r, rows_i = [], []
    for i in range(SEGS):
        rows_r.append(cr)
        rows_i.append(ci)
        xr, xi = cmul(ar[i : i + 1], ai[i : i + 1], cr, ci)
        cr, ci = xr + er[i : i + 1], xi + ei[i : i + 1]
    return jnp.concatenate(rows_r, 0), jnp.concatenate(rows_i, 0), cr, ci


def run_products(ar, ai):
    cr, ci = jnp.ones_like(ar[:1]), jnp.zeros_like(ai[:1])
    rows_r, rows_i = [], []
    for i in range(SEGS):
        rows_r.append(cr)
        rows_i.append(ci)
        cr, ci = cmul(ar[i : i + 1], ai[i : i + 1], cr, ci)
    return jnp.concatenate(rows_r, 0), jnp.concatenate(rows_i, 0), cr, ci


def decay_kernel(users, tokens, ids, bins, table, dec, cum, prod, runs):
    grp = ids[1]
    half = pl.program_id(0)
    place = jnp.where(half == 0, grp, 1 - grp)
    count = table.shape[2]
    order = order_matrix(tokens)
    steps = tokens // SEGS
    pieces = []
    for k in range(3):
        full = table[0, k]
        high = full.astype(BF16)
        rest = full - high.astype(F32)
        mid = rest.astype(BF16)
        low = (rest - mid.astype(F32)).astype(BF16)
        pieces.append((high, mid, low))
    for u in range(users):
        row = bins[u : u + 1, pl.ds(pl.multiple_of(grp * tokens, tokens), tokens)]
        hit = (lax.broadcasted_iota(jnp.int32, (count, tokens), 0) == row).astype(F32).astype(BF16)
        pick = lax.dot_general(
            order, hit, (((1,), (1,)), ((), ())), preferred_element_type=F32
        ).astype(BF16)
        for k in range(3):
            high, mid, low = pieces[k]
            dec[k, 0, u * tokens : (u + 1) * tokens, :] = (
                dot(pick, high) + dot(pick, mid)
            ) + dot(pick, low)
        base = u * tokens

        def at(s):
            rows = slice(base + s * SEGS, base + (s + 1) * SEGS)
            return dec[0, 0, rows, :], dec[1, 0, rows, :]

        pr, pi = at(0)
        for s in range(1, steps):
            dr, di = at(s)
            pr, pi = cmul(dr, di, pr, pi)
        runs[0, 0, u * SEGS : (u + 1) * SEGS, :] = pr
        runs[1, 0, u * SEGS : (u + 1) * SEGS, :] = pi
        cr, ci, tr, ti = run_products(pr, pi)
        prod[place, u : u + 1, :] = tr
        prod[2 + place, u : u + 1, :] = ti
        for s in range(steps):
            dr, di = at(s)
            cr, ci = cmul(dr, di, cr, ci)
            rows = slice(base + s * SEGS, base + (s + 1) * SEGS)
            cum[0, 0, rows, :] = cr
            cum[1, 0, rows, :] = ci


def weight_kernel(xor, ids, prods, out):
    me = ids[2]
    blocks = prods.shape[0]
    half = prods.shape[1] // 2
    one = jnp.ones(prods.shape[2:], F32)
    zero = jnp.zeros(prods.shape[2:], F32)

    def step(n, carry):
        j = blocks - 1 - n
        before = j < me
        new = []
        for h in range(half):
            r, i = carry[2 * h], carry[2 * h + 1]
            where = (j ^ me) if xor else j
            out[where, h] = jnp.where(before, r, 0.0)
            out[where, half + h] = jnp.where(before, i, 0.0)
            xr, xi = cmul(prods[j, h], prods[j, half + h], r, i)
            new += [jnp.where(before, xr, r), jnp.where(before, xi, i)]
        return tuple(new)

    lax.fori_loop(0, blocks, step, (one, zero) * half)


def into_order(users, tokens, source, target):
    order = order_matrix(tokens)
    for u in range(users):
        target[u * tokens : (u + 1) * tokens, :] = dot(order, source[u]).astype(BF16)


def own_kernel(users, tokens, ids, events, w_own, w_oth, out, rows):
    @pl.when(pl.program_id(0) == 0)
    def _():
        into_order(users, tokens, events, rows)

    for h, w in enumerate((w_own, w_oth)):
        for c in range(2):
            out[c, h] = dot(rows[...], w[c])


def scan_kernel(users, tokens, peers, ids, *refs):
    events = refs[:peers]
    weights = refs[peers : 3 * peers]
    part, dec, runs, state, ends, rows, drive = refs[3 * peers :]
    grp = ids[1]
    steps = tokens // SEGS

    @pl.when(pl.program_id(0) == 0)
    def _():
        for n in range(peers):
            into_order(users, tokens, events[n], rows.at[n])

    for h in range(2):
        place = grp if h == 0 else 1 - grp
        for c in range(2):
            total = part[c, h]
            for n in range(peers):
                total = total + dot(rows[n], weights[2 * n + h][c])
            drive[c] = dec[2, h] * total
        for u in range(users):
            base = u * tokens

            def at(s):
                sl = slice(base + s * SEGS, base + (s + 1) * SEGS)
                return dec[0, h, sl, :], dec[1, h, sl, :], drive[0, sl, :], drive[1, sl, :]

            _, _, sr, si = at(0)
            for s in range(1, steps):
                dr, di, vr, vi = at(s)
                xr, xi = cmul(dr, di, sr, si)
                sr, si = xr + vr, xi + vi
            ar = runs[0, h, u * SEGS : (u + 1) * SEGS, :]
            ai = runs[1, h, u * SEGS : (u + 1) * SEGS, :]
            sr, si, er, ei = run_starts(ar, ai, sr, si)
            ends[place, u : u + 1, :] = er
            ends[2 + place, u : u + 1, :] = ei
            for s in range(steps):
                dr, di, vr, vi = at(s)
                xr, xi = cmul(dr, di, sr, si)
                sr, si = xr + vr, xi + vi
                sl = slice(base + s * SEGS, base + (s + 1) * SEGS)
                state[0, h, sl, :] = sr
                state[1, h, sl, :] = si


def carry_kernel(users, tokens, firsts, ids, *refs):
    given = refs[: len(firsts)]
    weights, state, cum, out = refs[len(firsts) :]
    grp = ids[1]
    order = order_matrix(tokens)
    for h in range(2):
        place = grp if h == 0 else 1 - grp
        cr = jnp.zeros(weights.shape[2:], F32)
        ci = jnp.zeros(weights.shape[2:], F32)
        for first, ref in zip(firsts, given):
            for n in range(ref.shape[0]):
                xr, xi = cmul(
                    weights[first + n, place],
                    weights[first + n, 2 + place],
                    ref[n, place],
                    ref[n, 2 + place],
                )
                cr, ci = cr + xr, ci + xi
        for u in range(users):
            sl = slice(u * tokens, (u + 1) * tokens)
            xr, xi = cmul(cum[0, h, sl, :], cum[1, h, sl, :], cr[u : u + 1], ci[u : u + 1])
            for c, value in ((0, state[0, h, sl, :] + xr), (1, state[1, h, sl, :] + xi)):
                moved = lax.dot_general(
                    order, value.astype(BF16), (((0,), (0,)), ((), ())), preferred_element_type=F32
                )
                out[c, h, sl, :] = moved.astype(BF16)


def mix_kernel(ids, states, w_own, w_oth, out):
    total = None
    for h, w in enumerate((w_own, w_oth)):
        for c in range(2):
            term = dot(states[c, h], w[c])
            total = term if total is None else total + term
    out[...] = total.astype(out.dtype)


def final_kernel(users, tokens, same, cross, ids, lengths, *refs):
    mine, other = refs[:same], refs[same : same + cross]
    events, gain, out = refs[same + cross :]
    grp = ids[1]
    for u in range(users):
        sl = slice(u * tokens, (u + 1) * tokens)
        for where, parts in ((grp, mine), (1 - grp, other)):
            start = pl.multiple_of(where * tokens, tokens)
            total = parts[0][sl, :].astype(F32)
            for part in parts[1:]:
                total = total + part[sl, :].astype(F32)
            own = events[u, pl.ds(start, tokens), :].astype(F32)
            result = jax.nn.gelu(total + gain[...] * own)
            position = (
                ids[3] + start + lax.broadcasted_iota(jnp.int32, result.shape, 0)
            )
            result = jnp.where(position < lengths[u], result, 0.0)
            out[u, pl.ds(start, tokens), :] = result.astype(BF16)


def call(body, name, ids, args, in_specs, out_shape, out_specs, grid=(1,), scratch=(), flops=0, bytes_=0):
    return pl.pallas_call(
        body,
        name=name,
        out_shape=out_shape,
        grid_spec=pltpu.PrefetchScalarGridSpec(
            num_scalar_prefetch=len(ids),
            grid=grid,
            in_specs=in_specs,
            out_specs=out_specs,
            scratch_shapes=list(scratch),
        ),
        compiler_params=pltpu.CompilerParams(vmem_limit_bytes=VMEM),
        cost_estimate=pl.CostEstimate(flops=flops, bytes_accessed=bytes_, transcendentals=0),
    )(*ids, *args)


def whole(array):
    rank = array.ndim
    return pl.BlockSpec(array.shape, lambda *_: (0,) * rank)


def shape(dims, kind):
    return jax.ShapeDtypeStruct(dims, kind)


def local(
    events, gap_bins, lengths, gap_table, decay_rate, frequency, in_proj, out_proj, skip_gain
):
    users, seg_rows, width = events.shape
    model_width = in_proj.shape[0]
    q = decay_rate.shape[0]
    grps, chans, ctxs = (lax.axis_size(a) for a in ("grp", "chan", "ctx"))
    assert grps == 2
    tokens = seg_rows // grps
    rows = users * tokens
    count = gap_table.shape[0]
    devices, blocks = chans * grps, ctxs * grps
    part_width = model_width // devices

    chan, grp, ctx = (lax.axis_index(a) for a in ("chan", "grp", "ctx"))
    ids = jnp.stack(
        [chan, grp, ctx * grps + grp, ctx * seg_rows, chan * grps + grp]
    ).astype(jnp.int32)

    def swap(array, axes, size, k):
        return lax.ppermute(array, axes, [(i, i ^ k) for i in range(size)])

    own_rows = lax.dynamic_slice_in_dim(events, grp * tokens, tokens, 1)
    peer_rows = [swap(own_rows, "chan", chans, k) for k in range(1, chans)]

    w_own = jnp.transpose(in_proj, (1, 0, 2))
    w_oth = swap(w_own, "grp", grps, 1)
    rates = jnp.stack([decay_rate, frequency])
    rates_oth = swap(rates, "grp", grps, 1)
    o_oth = swap(out_proj, "grp", grps, 1)

    both = jnp.stack([rates, rates_oth])
    scaled = gap_table[None, :, None] * both[:, 0][:, None, :]
    turned = gap_table[None, :, None] * both[:, 1][:, None, :]
    magnitude = jnp.exp(-scaled)
    table = jnp.stack(
        [
            magnitude * jnp.cos(turned),
            magnitude * jnp.sin(turned),
            jnp.sqrt(-jnp.expm1(-2.0 * scaled)),
        ],
        1,
    )

    dec, cum, prod, runs = call(
        functools.partial(decay_kernel, users, tokens),
        "decays",
        (ids,),
        (gap_bins, table),
        [
            whole(gap_bins),
            pl.BlockSpec((1, 3, count, q), lambda i, ids: (i, 0, 0, 0)),
        ],
        (
            shape((3, 2, rows, q), F32),
            shape((2, 2, rows, q), F32),
            shape((4, users, q), F32),
            shape((2, 2, users * SEGS, q), F32),
        ),
        (
            pl.BlockSpec((3, 1, rows, q), lambda i, ids: (0, i, 0, 0)),
            pl.BlockSpec((2, 1, rows, q), lambda i, ids: (0, i, 0, 0)),
            pl.BlockSpec((4, users, q), lambda i, ids: (0, 0, 0)),
            pl.BlockSpec((2, 1, users * SEGS, q), lambda i, ids: (0, i, 0, 0)),
        ),
        grid=(2,),
        flops=2 * rows * q * 2 * 9 * count,
        bytes_=5 * 2 * rows * q * 4,
    )

    prods = lax.all_gather(prod, ("ctx", "grp"))
    xor = blocks <= 8
    weights = call(
        functools.partial(weight_kernel, xor),
        "between",
        (ids,),
        (prods,),
        [whole(prods)],
        shape(prods.shape, F32),
        whole(prods),
        bytes_=2 * prods.size * 4,
    )

    step = min(q, 256)
    part = call(
        functools.partial(own_kernel, users, tokens),
        "own_drive",
        (ids,),
        (own_rows, w_own, w_oth),
        [whole(own_rows)]
        + [pl.BlockSpec((2, width, step), lambda i, ids: (0, ids[0], i))] * 2,
        shape((2, 2, rows, q), F32),
        pl.BlockSpec((2, 2, rows, step), lambda i, ids: (0, 0, 0, i)),
        grid=(q // step,),
        scratch=[pltpu.VMEM((rows, width), BF16)],
        flops=2 * rows * width * 4 * q,
        bytes_=4 * width * q * 2 + 4 * rows * q * 4,
    )

    peers = chans - 1
    w_specs = []
    for k in range(1, chans):
        w_specs += [
            pl.BlockSpec((2, width, step), lambda i, ids, k=k: (0, ids[0] ^ k, i))
        ] * 2
    state, ends = call(
        functools.partial(scan_kernel, users, tokens, peers),
        "drive_scan",
        (ids,),
        (*peer_rows, *((w_own, w_oth) * peers), part, dec, runs),
        [whole(p) for p in peer_rows]
        + w_specs
        + [
            pl.BlockSpec((2, 2, rows, step), lambda i, ids: (0, 0, 0, i)),
            pl.BlockSpec((3, 2, rows, step), lambda i, ids: (0, 0, 0, i)),
            pl.BlockSpec((2, 2, users * SEGS, step), lambda i, ids: (0, 0, 0, i)),
        ],
        (shape((2, 2, rows, q), F32), shape((4, users, q), F32)),
        (
            pl.BlockSpec((2, 2, rows, step), lambda i, ids: (0, 0, 0, i)),
            pl.BlockSpec((4, users, step), lambda i, ids: (0, 0, i)),
        ),
        grid=(q // step,),
        scratch=[
            pltpu.VMEM((peers, rows, width), BF16),
            pltpu.VMEM((2, rows, step), F32),
        ],
        flops=2 * rows * width * 4 * q * peers,
        bytes_=4 * width * q * 2 * peers + 4 * rows * q * 12,
    )

    if xor:
        given = [swap(ends, ("ctx", "grp"), blocks, k)[None] for k in range(1, blocks)]
        firsts = tuple(range(1, blocks))
    else:
        given = [lax.all_gather(ends, ("ctx", "grp"))]
        firsts = (0,)

    states = call(
        functools.partial(carry_kernel, users, tokens, firsts),
        "carry_in",
        (ids,),
        (*given, weights, state, cum),
        [whole(g) for g in given] + [whole(weights), whole(state), whole(cum)],
        shape((2, 2, rows, q), BF16),
        pl.BlockSpec((2, 2, rows, q), lambda i, ids: (0, 0, 0, 0)),
        flops=2 * rows * tokens * 4 * q,
        bytes_=rows * q * 4 * 10,
    )

    cols = min(part_width, 256)

    def mixed(d, kind):
        def spec(i, ids):
            return (0, 0, (ids[4] ^ d) * (part_width // cols) + i)

        return call(
            mix_kernel,
            "mix_%d" % d,
            (ids,),
            (states, out_proj, o_oth),
            [whole(states)] + [pl.BlockSpec((2, q, cols), spec)] * 2,
            shape((rows, part_width), kind),
            pl.BlockSpec((rows, cols), lambda i, ids: (0, i)),
            grid=(part_width // cols,),
            flops=2 * rows * part_width * 4 * q,
            bytes_=4 * q * part_width * 2 + rows * part_width * 2 + 4 * rows * q * 2,
        )

    order = list(range(2, devices)) + [1]
    received = {
        d: swap(mixed(d, F32 if d == 1 else BF16), ("chan", "grp"), devices, d) for d in order
    }
    received[0] = mixed(0, F32)
    same = [received[d] for d in range(0, devices, 2)]
    cross = [received[d] for d in range(1, devices, 2)]

    own_events = lax.dynamic_slice_in_dim(events, grp * part_width, part_width, 2)
    gain = skip_gain[None]
    return call(
        functools.partial(final_kernel, users, tokens, len(same), len(cross)),
        "final",
        (ids, lengths),
        (*same, *cross, own_events, gain),
        [whole(a) for a in (*same, *cross, own_events, gain)],
        shape((users, seg_rows, part_width), BF16),
        pl.BlockSpec((users, seg_rows, part_width), lambda i, ids, lengths: (0, 0, 0)),
        bytes_=rows * part_width * 12,
    )


def solution(mesh):
    return jax.shard_map(
        local,
        mesh=mesh,
        in_specs=(
            P("groups", "ctx", "chan"),
            P("groups", "ctx"),
            P("groups"),
            P(),
            P(("chan", "grp")),
            P(("chan", "grp")),
            P(None, None, ("chan", "grp")),
            P(None, ("chan", "grp"), None),
            P(("chan", "grp")),
        ),
        out_specs=P("groups", "ctx", ("chan", "grp")),
        check_vma=False,
    )
```

time: 551 us -> 74.9 us (0.14); the launches traced: 544 us -> 74.4 us
  local copies, waits for them, and re-layouts: 215 us -> 5.16 us
  other arithmetic: 129 us -> 1.24 us
  waiting for transfers between devices: 133 us -> 9.31 us
  Pallas kernels: 0 us -> 29.1 us
  blocking collectives: 43.3 us -> 14.2 us
  starting transfers between devices: 0.04 us -> 15.2 us
  between operations: 14.9 us -> 0.24 us
  matrix products: 9.6 us -> 0 us
    pad x76 -> x0, local copies, waits for them, and re-layouts: 108 us -> none  [the longest x48 102 us: local(): lax.associative_scan(combine, (decay_re, decay_im, drive_re, drive_im), a...]
    unnamed x3 -> x0, waiting for transfers between devices: 96.5 us -> none
    slice x161 -> x0, local copies, waits for them, and re-layouts: 90.9 us -> none  [the longest x101 67.6 us: local(): lax.associative_scan(combine, (decay_re, decay_im, drive_re, drive_im), a...]
    add x77 -> x0, other arithmetic: 78.3 us -> none  [the longest x26 40.4 us: local(): lax.associative_scan(combine, (decay_re, decay_im, drive_re, drive_im), a...]
    all_gather x1 -> x0, waiting for transfers between devices: 36 us -> none  [local(): lax.all_gather(events, 'chan', axis=2, tiled=True)]
    concatenate x38 -> x0, other arithmetic: 33.6 us -> none  [the longest x22 31.1 us: local(): lax.associative_scan(combine, (decay_re, decay_im, drive_re, drive_im), a...]
    all_gather x4 -> x1, blocking collectives: 43.3 us -> 14.2 us  [local(): prods = lax.all_gather(prod, ('ctx', 'grp'))]
    pallas_call x0 -> x10, Pallas kernels: none -> 29.1 us  [call(): pl.pallas_call(body, name=name, out_shape=out_shape, grid_spec=pltpu.Pref...]
  transfers between devices with their start and end apart: 2 -> 14, of which waited for: 2 -> 2; matrix products, arithmetic and copies ran while one was open for 0% -> 2% of each run, Pallas kernels for 0% -> 32%
where the time goes in v1:
time: 74.9 us; the launch traced here: 74.4 us
  Pallas kernels  29.1 us (39%)
  starting transfers between devices  15.2 us (20%)
  blocking collectives  14.2 us (19%)
  waiting for transfers between devices  9.31 us (12%)
  local copies, waits for them, and re-layouts  5.16 us (7%)
  other arithmetic  1.24 us (2%)
    pallas_call x10, Pallas kernels, call(): pl.pallas_call(body, name=name, out_shape=out_shape, grid_spec=pltpu.Pref...  29.1 us
    ppermute x14, starting transfers between devices, swap(): return lax.ppermute(array, axes, [(i, i ^ k) for i in range(size)])  15.2 us
    all_gather x1, blocking collectives, local(): prods = lax.all_gather(prod, ('ctx', 'grp'))  14.2 us
    ppermute x14, waiting for transfers between devices, swap(): return lax.ppermute(array, axes, [(i, i ^ k) for i in range(size)])  9.31 us
    unnamed x17, local copies, waits for them, and re-layouts  5 us
  transfers between devices with their start and end apart: 14, of which 2 were waited for; matrix products, arithmetic and copies ran while one was open for 2% of the time, Pallas kernels for 32%

profile of v1, /device:TPU:1, one launch (start us, length us, event | category | flops | bytes accessed | tf_op | source)
XLA Modules:
  0.0 74.4 jit_solution(4678393961624006256)
XLA Ops:
  0.0 5.0 %copy.15 = bf16[2048,2,512]{2,0,1:T(8,128)(2,1)} copy(bf16[2048,2,512]{2,1,0:T(2,128)(2,1)} %param.15) | data formatting | bytes 8388608 | tf_op args[6]
  5.0 0.1 collective-permute-start.1
  5.0 0.5 collective-permute-start.10
  5.5 0.1 collective-permute-start.2
  5.7 2.7 %collective-permute-start = (bf16[2,128,1024]{2,1,0:T(8,128)(2,1)S(1)}, bf16[2,128,1024]{2,1,0:T(8,128)(2,1)S(1)}, u32[]{:S(2)}, u32[]{:S(2)}) collective-permute-start(bf16[2,128,1024]{2,1,0:T(8,128)(2,1)S(1)} %constant_dynamic-slice_fusion.1.events), channel_id=1, source_target_pairs={{0,2},{2,0},{1,3},{3,1},{4,6},{6,4},{5,7},{7,5},{8,10},{10,8},{9,1... | collective-permute-start | bytes 1572872 | tf_op jit(solution)/shard_map/ppermute | solution.py:288
  8.4 0.1 stack.47.ids
  8.5 3.6 %collective-permute-done.2 = f32[2,512]{1,0:T(2,128)S(1)} collective-permute-done((f32[2,512]{1,0:T(2,128)S(1)}, f32[2,512]{1,0:T(2,128)S(1)}, u32[]{:S(2)}, u32[]{:S(2)}) %collective-permute-start.2) | collective-permute-done | bytes 4128 | tf_op jit(solution)/shard_map/ppermute | solution.py:288
  12.1 1.2 %fusion.2 = (f32[2,1,64,512]{3,2,1,0:T(8,128)S(1)}, f32[2,1,64,512]{3,2,1,0:T(8,128)S(1)}, f32[2,1,64,512]{3,2,1,0:T(8,128)S(1)}) fusion(f32[2,512]{1,0:T(2,128)S(1)} %get-tuple-element.19, f32[2,512]{1,0:T(2,128)S(1)} %get-tuple-element.20, f32[64]{0:T(128)S(1)} %copy-done.7), kind=kLoop, calls=%fused_computation.8 | loop fusion | flops 458752 | bytes 794880 | tf_op jit(solution)/shard_map/mul | solution.py:305
  13.3 0.1 pad_maximum_fusion.table
  13.4 3.0 %decays.1 = (f32[3,2,256,512]{3,2,1,0:T(8,128)S(1)}, f32[2,2,256,512]{3,2,1,0:T(8,128)S(1)}, f32[4,2,512]{2,1,0:T(2,128)S(1)}, f32[2,2,16,512]{3,2,1,0:T(8,128)S(1)}) custom-call(s32[5]{0:T(128)S(1)} %stack.47.ids, s32[2,256]{1,0:T(2,128)S(1)} %copy-done.4, f32[2,3,64,512]{3,2,1,0:T(8,128)S(1)} %pad_maximum_fusion.table), custom_call_target="tpu_custom_call" | custom-call | flops 301989888 | bytes 5242880 | tf_op jit(solution)/shard_map/decays/pallas_call | solution.py:243
  16.5 4.6 %own_drive.1.refs_3_ = f32[2,2,256,512]{3,2,1,0:T(8,128)S(1)} custom-call(s32[5]{0:T(128)S(1)} %stack.47.ids, bf16[2,128,1024]{2,1,0:T(8,128)(2,1)S(1)} %constant_dynamic-slice_fusion.1.events, bf16[2,2048,512]{2,1,0:T(8,128)(2,1)} %bitcast.24.w_own.refs_1_, bf16[2,2048,512]{2,1,0:T(8,128)(2,1)} %collective-permute-done.1.w_oth.refs_2_), custom_call_target="tpu_custom_call" | custom-call | flops 1073741824 | bytes 6291456 | tf_op jit(solution)/shard_map/own_drive/pallas_call | solution.py:243
  21.0 5.3 %drive_scan.1 = (f32[2,2,256,512]{3,2,1,0:T(8,128)S(1)}, f32[4,2,512]{2,1,0:T(2,128)S(1)}) custom-call(s32[5]{0:T(128)S(1)} %stack.47.ids, bf16[2,128,1024]{2,1,0:T(8,128)(2,1)S(1)} %collective-permute-done.refs_0_, bf16[2,2048,512]{2,1,0:T(8,128)(2,1)} %bitcast.24.w_own.refs_1_, bf16[2,2048,512]{2,1,0:T(8,128)(2,1)} %collective-permute-done.1.w_oth.refs_2_, ...), custom_call_target="tpu_custom_call" | custom-call | flops 1073741824 | bytes 10485760 | tf_op jit(solution)/shard_map/drive_scan/pallas_call | solution.py:243
  26.4 0.3 collective-permute-start.3
  26.7 2.6 %collective-permute-start.4 = (f32[4,2,512]{2,1,0:T(2,128)S(1)}, f32[4,2,512]{2,1,0:T(2,128)S(1)}, u32[]{:S(2)}, u32[]{:S(2)}) collective-permute-start(f32[4,2,512]{2,1,0:T(2,128)S(1)} %get-tuple-element.13), channel_id=1, source_target_pairs={{0,4},{1,5},{4,0},{5,1},{8,12},{9,13},{12,8},{13,9},{2,6},{3,7},{6... | collective-permute-start | bytes 49160 | tf_op jit(solution)/shard_map/ppermute | solution.py:288
  29.3 0.1 collective-permute-start.5
  29.3 2.7 %collective-permute-start.6 = (f32[4,2,512]{2,1,0:T(2,128)S(1)}, f32[4,2,512]{2,1,0:T(2,128)S(1)}, u32[]{:S(2)}, u32[]{:S(2)}) collective-permute-start(f32[4,2,512]{2,1,0:T(2,128)S(1)} %get-tuple-element.13), channel_id=1, source_target_pairs={{0,8},{1,9},{4,12},{5,13},{8,0},{9,1},{12,4},{13,5},{2,10},{3,11},... | collective-permute-start | bytes 49160 | tf_op jit(solution)/shard_map/ppermute | solution.py:288
  32.1 0.2 collective-permute-start.7
  32.2 3.4 %collective-permute-start.8 = (f32[4,2,512]{2,1,0:T(2,128)S(1)}, f32[4,2,512]{2,1,0:T(2,128)S(1)}, u32[]{:S(2)}, u32[]{:S(2)}) collective-permute-start(f32[4,2,512]{2,1,0:T(2,128)S(1)} %get-tuple-element.13), channel_id=1, source_target_pairs={{0,12},{1,13},{4,8},{5,9},{8,4},{9,5},{12,0},{13,1},{2,14},{3,15},... | collective-permute-start | bytes 49160 | tf_op jit(solution)/shard_map/ppermute | solution.py:288
  35.7 0.2 collective-permute-start.9
  35.9 14.2 %all-gather = f32[32,2,512]{2,1,0:T(2,128)S(1)} all-gather(f32[4,2,512]{2,1,0:T(2,128)S(1)} %get-tuple-element.14), channel_id=2, replica_groups=mesh['groups'=2,'ctx'=4,'chan'=2,'grp'=2] {'ctx','grp'}, dimensions={0}, use_global_device_ids=true | all-gather | bytes 147456 | tf_op jit(solution)/shard_map/all_gather | solution.py:338
  50.1 0.6 between.1.refs_7_
  50.8 1.2 %carry_in.1.states = bf16[2,2,256,512]{3,2,1,0:T(8,128)(2,1)S(1)} custom-call(s32[5]{0:T(128)S(1)} %stack.47.ids, f32[1,4,2,512]{3,2,1,0:T(2,128)S(1)} %bitcast.26, f32[1,4,2,512]{3,2,1,0:T(2,128)S(1)} %bitcast.27, f32[1,4,2,512]{3,2,1,0:T(2,128)S(1)} %bitcast.28, f32[1,4,2,512]{3,2,1,0:T(2,128)S(1)} %bitcast.29, f32[1,4,2,512]{3,2,1,0:T(2,128)S(1)} %bitcast.30, ...), custom_call_target="tpu_custom_call" | custom-call | flops 134217728 | bytes 5242880 | tf_op jit(solution)/shard_map/carry_in/pallas_call | solution.py:243
  52.0 2.7 %mix_1.1 = f32[256,512]{1,0:T(8,128)S(1)} custom-call(s32[5]{0:T(128)S(1)} %stack.47.ids, bf16[2,2,256,512]{3,2,1,0:T(8,128)(2,1)S(1)} %carry_in.1.states, bf16[2,512,2048]{2,1,0:T(8,128)(2,1)} %w_own.7, bf16[2,512,2048]{2,1,0:T(8,128)(2,1)} %collective-permute-done.10.w_oth), custom_call_target="tpu_custom_call" | custom-call | flops 536870912 | bytes 3407872 | tf_op jit(solution)/shard_map/mix_1/pallas_call | solution.py:243
  54.7 0.2 collective-permute-start.12
  54.9 2.7 %mix_2.1 = bf16[256,512]{1,0:T(8,128)(2,1)S(1)} custom-call(s32[5]{0:T(128)S(1)} %stack.47.ids, bf16[2,2,256,512]{3,2,1,0:T(8,128)(2,1)S(1)} %carry_in.1.states, bf16[2,512,2048]{2,1,0:T(8,128)(2,1)} %w_own.7, bf16[2,512,2048]{2,1,0:T(8,128)(2,1)} %collective-permute-done.10.w_oth), custom_call_target="tpu_custom_call" | custom-call | flops 536870912 | bytes 3407872 | tf_op jit(solution)/shard_map/mix_2/pallas_call | solution.py:243
  57.6 1.2 %collective-permute-start.11 = (bf16[256,512]{1,0:T(8,128)(2,1)S(1)}, bf16[256,512]{1,0:T(8,128)(2,1)}, u32[]{:S(2)}, u32[]{:S(2)}) collective-permute-start(bf16[256,512]{1,0:T(8,128)(2,1)S(1)} %mix_2.1), channel_id=1, source_target_pairs={{0,2},{1,3},{2,0},{3,1},{4,6},{5,7},{6,4},{7,5},{8,10},{9,11},{10,... | collective-permute-start | bytes 786440 | tf_op jit(solution)/shard_map/ppermute | solution.py:288
  58.8 3.3 %mix_3.1 = bf16[256,512]{1,0:T(8,128)(2,1)} custom-call(s32[5]{0:T(128)S(1)} %stack.47.ids, bf16[2,2,256,512]{3,2,1,0:T(8,128)(2,1)S(1)} %carry_in.1.states, bf16[2,512,2048]{2,1,0:T(8,128)(2,1)} %w_own.7, bf16[2,512,2048]{2,1,0:T(8,128)(2,1)} %collective-permute-done.10.w_oth), custom_call_target="tpu_custom_call" | custom-call | flops 536870912 | bytes 3407872 | tf_op jit(solution)/shard_map/mix_3/pallas_call | solution.py:243
  62.1 0.9 %collective-permute-start.13 = (bf16[256,512]{1,0:T(8,128)(2,1)}, bf16[256,512]{1,0:T(8,128)(2,1)}, u32[]{:S(2)}, u32[]{:S(2)}) collective-permute-start(bf16[256,512]{1,0:T(8,128)(2,1)} %mix_3.1), channel_id=1, source_target_pairs={{0,3},{1,2},{2,1},{3,0},{4,7},{5,6},{6,5},{7,4},{8,11},{9,10},{10,... | collective-permute-start | bytes 786440 | tf_op jit(solution)/shard_map/ppermute | solution.py:288
  63.0 0.0 copy-start.2
  63.1 2.7 %mix_0.1.refs_0_ = f32[256,512]{1,0:T(8,128)S(1)} custom-call(s32[5]{0:T(128)S(1)} %stack.47.ids, bf16[2,2,256,512]{3,2,1,0:T(8,128)(2,1)S(1)} %carry_in.1.states, bf16[2,512,2048]{2,1,0:T(8,128)(2,1)} %w_own.7, bf16[2,512,2048]{2,1,0:T(8,128)(2,1)} %collective-permute-done.10.w_oth), custom_call_target="tpu_custom_call" | custom-call | flops 536870912 | bytes 3407872 | tf_op jit(solution)/shard_map/mix_0/pallas_call | solution.py:243
  65.8 5.7 %collective-permute-done.13.refs_3_ = bf16[256,512]{1,0:T(8,128)(2,1)} collective-permute-done((bf16[256,512]{1,0:T(8,128)(2,1)}, bf16[256,512]{1,0:T(8,128)(2,1)}, u32[]{:S(2)}, u32[]{:S(2)}) %collective-permute-start.13) | collective-permute-done | bytes 262176 | tf_op jit(solution)/shard_map/ppermute | solution.py:288
  71.5 2.9 %final.1 = bf16[2,256,512]{2,1,0:T(8,128)(2,1)} custom-call(s32[5]{0:T(128)S(1)} %stack.47.ids, s32[2]{0:T(128)S(1)} %copy-done.3, f32[256,512]{1,0:T(8,128)S(1)} %mix_0.1.refs_0_, bf16[256,512]{1,0:T(8,128)(2,1)} %collective-permute-done.11.refs_1_, f32[256,512]{1,0:T(8,128)S(1)} %collective-permute-done.12.refs_2_, ...), custom_call_target="tpu_custom_call" | custom-call | bytes 1572864 | tf_op jit(solution)/shard_map/final/pallas_call | solution.py:243
  (33 shorter events, 0.2 us)
Async XLA Ops:
  0.0 5.6 %copy-start = (bf16[2,256,1024]{2,1,0:T(8,128)(2,1)S(1)}, bf16[2,256,1024]{2,1,0:T(8,128)(2,1)}, u32[]{:S(2)}) copy-start(bf16[2,256,1024]{2,1,0:T(8,128)(2,1)} %param.9) | copy-start | bytes 3145732
  0.0 5.5 %copy-start.6 = (f32[512]{0:T(512)S(1)}, f32[512]{0:T(512)}, u32[]{:S(2)}) copy-start(f32[512]{0:T(512)} %param.13) | copy-start | bytes 6148
  0.0 5.5 %copy-start.5 = (f32[512]{0:T(512)S(1)}, f32[512]{0:T(512)}, u32[]{:S(2)}) copy-start(f32[512]{0:T(512)} %param.14) | copy-start | bytes 6148
  0.0 12.1 %copy-start.7 = (f32[64]{0:T(128)S(1)}, f32[64]{0:T(128)}, u32[]{:S(2)}) copy-start(f32[64]{0:T(128)} %param.12) | copy-start | bytes 772
  0.0 13.4 %copy-start.4 = (s32[2,256]{1,0:T(2,128)S(1)}, s32[2,256]{1,0:T(2,128)}, u32[]{:S(2)}) copy-start(s32[2,256]{1,0:T(2,128)} %bins.1) | copy-start | bytes 6148
  5.0 11.5 %collective-permute-start.1 = (bf16[2,2048,512]{2,1,0:T(8,128)(2,1)}, bf16[2,2048,512]{2,1,0:T(8,128)(2,1)}, u32[]{:S(2)}, u32[]{:S(2)}) collective-permute-start(bf16[2,2048,512]{2,1,0:T(8,128)(2,1)} %bitcast.24.w_own.refs_1_), channel_id=1, source_target_pairs={{0,1},{1,0},{2,3},{3,2},{4,5},{5,4},{6,7},{7,6},{8,9},{9,8},{10,11... | collective-permute-start | bytes 12582920 | tf_op jit(solution)/shard_map/ppermute | solution.py:288
  5.0 46.9 %collective-permute-start.10 = (bf16[2,512,2048]{2,1,0:T(8,128)(2,1)}, bf16[2,512,2048]{2,1,0:T(8,128)(2,1)}, u32[]{:S(2)}, u32[]{:S(2)}) collective-permute-start(bf16[2,512,2048]{2,1,0:T(8,128)(2,1)} %w_own.7), channel_id=1, source_target_pairs={{0,1},{1,0},{2,3},{3,2},{4,5},{5,4},{6,7},{7,6},{8,9},{9,8},{10,11... | collective-permute-start | bytes 12582920 | tf_op jit(solution)/shard_map/ppermute | solution.py:288
  5.5 6.6 %collective-permute-start.2 = (f32[2,512]{1,0:T(2,128)S(1)}, f32[2,512]{1,0:T(2,128)S(1)}, u32[]{:S(2)}, u32[]{:S(2)}) collective-permute-start(f32[2,512]{1,0:T(2,128)S(1)} %get-tuple-element.22), channel_id=1, source_target_pairs={{0,1},{1,0},{2,3},{3,2},{4,5},{5,4},{6,7},{7,6},{8,9},{9,8},{10,11... | collective-permute-start | bytes 12296 | tf_op jit(solution)/shard_map/ppermute | solution.py:288
  5.7 15.4 %collective-permute-start = (bf16[2,128,1024]{2,1,0:T(8,128)(2,1)S(1)}, bf16[2,128,1024]{2,1,0:T(8,128)(2,1)S(1)}, u32[]{:S(2)}, u32[]{:S(2)}) collective-permute-start(bf16[2,128,1024]{2,1,0:T(8,128)(2,1)S(1)} %constant_dynamic-slice_fusion.1.events), channel_id=1, source_target_pairs={{0,2},{2,0},{1,3},{3,1},{4,6},{6,4},{5,7},{7,5},{8,10},{10,8},{9,1... | collective-permute-start | bytes 1572872 | tf_op jit(solution)/shard_map/ppermute | solution.py:288
  16.4 4.6 %copy-start.1 = (f32[3,2,256,512]{3,2,1,0:T(8,128)}, f32[3,2,256,512]{3,2,1,0:T(8,128)S(1)}, u32[]{:S(2)}) copy-start(f32[3,2,256,512]{3,2,1,0:T(8,128)S(1)} %get-tuple-element.11.refs_4_) | copy-start | bytes 9437188
  26.4 5.7 %collective-permute-start.3 = (f32[4,2,512]{2,1,0:T(2,128)S(1)}, f32[4,2,512]{2,1,0:T(2,128)S(1)}, u32[]{:S(2)}, u32[]{:S(2)}) collective-permute-start(f32[4,2,512]{2,1,0:T(2,128)S(1)} %get-tuple-element.13), channel_id=1, source_target_pairs={{0,1},{1,0},{4,5},{5,4},{8,9},{9,8},{12,13},{13,12},{2,3},{3,2},{6... | collective-permute-start | bytes 49160 | tf_op jit(solution)/shard_map/ppermute | solution.py:288
  26.7 5.5 %collective-permute-start.4 = (f32[4,2,512]{2,1,0:T(2,128)S(1)}, f32[4,2,512]{2,1,0:T(2,128)S(1)}, u32[]{:S(2)}, u32[]{:S(2)}) collective-permute-start(f32[4,2,512]{2,1,0:T(2,128)S(1)} %get-tuple-element.13), channel_id=1, source_target_pairs={{0,4},{1,5},{4,0},{5,1},{8,12},{9,13},{12,8},{13,9},{2,6},{3,7},{6... | collective-permute-start | bytes 49160 | tf_op jit(solution)/shard_map/ppermute | solution.py:288
  29.3 6.4 %collective-permute-start.5 = (f32[4,2,512]{2,1,0:T(2,128)S(1)}, f32[4,2,512]{2,1,0:T(2,128)S(1)}, u32[]{:S(2)}, u32[]{:S(2)}) collective-permute-start(f32[4,2,512]{2,1,0:T(2,128)S(1)} %get-tuple-element.13), channel_id=1, source_target_pairs={{0,5},{1,4},{4,1},{5,0},{8,13},{9,12},{12,9},{13,8},{2,7},{3,6},{6... | collective-permute-start | bytes 49160 | tf_op jit(solution)/shard_map/ppermute | solution.py:288
  29.3 21.4 %collective-permute-start.6 = (f32[4,2,512]{2,1,0:T(2,128)S(1)}, f32[4,2,512]{2,1,0:T(2,128)S(1)}, u32[]{:S(2)}, u32[]{:S(2)}) collective-permute-start(f32[4,2,512]{2,1,0:T(2,128)S(1)} %get-tuple-element.13), channel_id=1, source_target_pairs={{0,8},{1,9},{4,12},{5,13},{8,0},{9,1},{12,4},{13,5},{2,10},{3,11},... | collective-permute-start | bytes 49160 | tf_op jit(solution)/shard_map/ppermute | solution.py:288
  32.1 18.6 %collective-permute-start.7 = (f32[4,2,512]{2,1,0:T(2,128)S(1)}, f32[4,2,512]{2,1,0:T(2,128)S(1)}, u32[]{:S(2)}, u32[]{:S(2)}) collective-permute-start(f32[4,2,512]{2,1,0:T(2,128)S(1)} %get-tuple-element.13), channel_id=1, source_target_pairs={{0,9},{1,8},{4,13},{5,12},{8,1},{9,0},{12,5},{13,4},{2,11},{3,10},... | collective-permute-start | bytes 49160 | tf_op jit(solution)/shard_map/ppermute | solution.py:288
  32.2 18.5 %collective-permute-start.8 = (f32[4,2,512]{2,1,0:T(2,128)S(1)}, f32[4,2,512]{2,1,0:T(2,128)S(1)}, u32[]{:S(2)}, u32[]{:S(2)}) collective-permute-start(f32[4,2,512]{2,1,0:T(2,128)S(1)} %get-tuple-element.13), channel_id=1, source_target_pairs={{0,12},{1,13},{4,8},{5,9},{8,4},{9,5},{12,0},{13,1},{2,14},{3,15},... | collective-permute-start | bytes 49160 | tf_op jit(solution)/shard_map/ppermute | solution.py:288
  35.7 15.1 %collective-permute-start.9 = (f32[4,2,512]{2,1,0:T(2,128)S(1)}, f32[4,2,512]{2,1,0:T(2,128)S(1)}, u32[]{:S(2)}, u32[]{:S(2)}) collective-permute-start(f32[4,2,512]{2,1,0:T(2,128)S(1)} %get-tuple-element.13), channel_id=1, source_target_pairs={{0,13},{1,12},{4,9},{5,8},{8,5},{9,4},{12,1},{13,0},{2,15},{3,14},... | collective-permute-start | bytes 49160 | tf_op jit(solution)/shard_map/ppermute | solution.py:288
  54.7 16.8 %collective-permute-start.12 = (f32[256,512]{1,0:T(8,128)S(1)}, f32[256,512]{1,0:T(8,128)S(1)}, u32[]{:S(2)}, u32[]{:S(2)}) collective-permute-start(f32[256,512]{1,0:T(8,128)S(1)} %mix_1.1), channel_id=1, source_target_pairs={{0,1},{1,0},{2,3},{3,2},{4,5},{5,4},{6,7},{7,6},{8,9},{9,8},{10,11... | collective-permute-start | bytes 1572872 | tf_op jit(solution)/shard_map/ppermute | solution.py:288
  57.6 8.1 %collective-permute-start.11 = (bf16[256,512]{1,0:T(8,128)(2,1)S(1)}, bf16[256,512]{1,0:T(8,128)(2,1)}, u32[]{:S(2)}, u32[]{:S(2)}) collective-permute-start(bf16[256,512]{1,0:T(8,128)(2,1)S(1)} %mix_2.1), channel_id=1, source_target_pairs={{0,2},{1,3},{2,0},{3,1},{4,6},{5,7},{6,4},{7,5},{8,10},{9,11},{10,... | collective-permute-start | bytes 786440 | tf_op jit(solution)/shard_map/ppermute | solution.py:288
  62.1 9.3 %collective-permute-start.13 = (bf16[256,512]{1,0:T(8,128)(2,1)}, bf16[256,512]{1,0:T(8,128)(2,1)}, u32[]{:S(2)}, u32[]{:S(2)}) collective-permute-start(bf16[256,512]{1,0:T(8,128)(2,1)} %mix_3.1), channel_id=1, source_target_pairs={{0,3},{1,2},{2,1},{3,0},{4,7},{5,6},{6,5},{7,4},{8,11},{9,10},{10,... | collective-permute-start | bytes 786440 | tf_op jit(solution)/shard_map/ppermute | solution.py:288
  63.0 8.4 %copy-start.2 = (f32[512]{0:T(512)S(1)}, f32[512]{0:T(512)}, u32[]{:S(2)}) copy-start(f32[512]{0:T(512)} %param.17) | copy-start | bytes 6148
  63.0 8.4 %copy-start.3 = (s32[2]{0:T(128)S(1)}, s32[2]{0:T(128)}, u32[]{:S(2)}) copy-start(s32[2]{0:T(128)} %lengths.1) | copy-start | bytes 28

commit v2 on v1

v2 whole, which is shorter than its diff:
```python
import functools

import jax
import jax.numpy as jnp
from jax import lax
from jax.experimental import pallas as pl
from jax.experimental.layout import Layout, with_layout_constraint
from jax.experimental.pallas import tpu as pltpu
from jax.sharding import PartitionSpec as P

F32 = jnp.float32
BF16 = jnp.bfloat16
SEGS = 8
VMEM = 16 * 1024 * 1024
HERE = pl.BlockSpec(memory_space=pltpu.VMEM)


def dot(a, b):
    return jnp.dot(a, b, preferred_element_type=F32)


def cmul(ar, ai, br, bi):
    return ar * br - ai * bi, ar * bi + ai * br


def order_matrix(tokens):
    steps = tokens // SEGS
    r = lax.broadcasted_iota(jnp.int32, (tokens, tokens), 0)
    t = lax.broadcasted_iota(jnp.int32, (tokens, tokens), 1)
    return (t == (r % SEGS) * steps + r // SEGS).astype(F32).astype(BF16)


def run_starts(ar, ai, er, ei):
    cr, ci = jnp.zeros_like(er[:1]), jnp.zeros_like(ei[:1])
    rows_r, rows_i = [], []
    for i in range(SEGS):
        rows_r.append(cr)
        rows_i.append(ci)
        xr, xi = cmul(ar[i : i + 1], ai[i : i + 1], cr, ci)
        cr, ci = xr + er[i : i + 1], xi + ei[i : i + 1]
    return jnp.concatenate(rows_r, 0), jnp.concatenate(rows_i, 0), cr, ci


def run_products(ar, ai):
    cr, ci = jnp.ones_like(ar[:1]), jnp.zeros_like(ai[:1])
    rows_r, rows_i = [], []
    for i in range(SEGS):
        rows_r.append(cr)
        rows_i.append(ci)
        cr, ci = cmul(ar[i : i + 1], ai[i : i + 1], cr, ci)
    return jnp.concatenate(rows_r, 0), jnp.concatenate(rows_i, 0), cr, ci


def decay_kernel(tokens, bins, table, dec, cum, prod, runs, later):
    grp = lax.axis_index("grp")
    users = bins.shape[0]
    count = table.shape[2]
    me = lax.axis_index("ctx") * lax.axis_size("grp") + grp
    for k in range(later.shape[0]):
        later[k] = jnp.full(later.shape[1:], (me >> k) & 1, jnp.int32)
    order = order_matrix(tokens)
    steps = tokens // SEGS
    picks = []
    for u in range(users):
        row = bins[u : u + 1, pl.ds(pl.multiple_of(grp * tokens, tokens), tokens)]
        hit = (lax.broadcasted_iota(jnp.int32, (count, tokens), 0) == row).astype(F32).astype(BF16)
        picks.append(
            lax.dot_general(
                order, hit, (((1,), (1,)), ((), ())), preferred_element_type=F32
            ).astype(BF16)
        )
    pick = jnp.concatenate(picks, 0)
    pick = jnp.concatenate([pick] * 3, 1)
    for h in range(2):
        place = grp if h == 0 else 1 - grp
        for k in range(3):
            full = table[h, k]
            high = full.astype(BF16)
            rest = full - high.astype(F32)
            mid = rest.astype(BF16)
            low = (rest - mid.astype(F32)).astype(BF16)
            dec[k, h] = dot(pick, jnp.concatenate([high, mid, low], 0))
        for u in range(users):
            base = u * tokens

            def at(s):
                rows = slice(base + s * SEGS, base + (s + 1) * SEGS)
                return dec[0, h, rows, :], dec[1, h, rows, :]

            pr, pi = at(0)
            for s in range(1, steps):
                dr, di = at(s)
                pr, pi = cmul(dr, di, pr, pi)
            runs[0, h, u * SEGS : (u + 1) * SEGS, :] = pr
            runs[1, h, u * SEGS : (u + 1) * SEGS, :] = pi
            cr, ci, tr, ti = run_products(pr, pi)
            prod[place, u : u + 1, :] = tr
            prod[2 + place, u : u + 1, :] = ti
            for s in range(steps):
                dr, di = at(s)
                cr, ci = cmul(dr, di, cr, ci)
                rows = slice(base + s * SEGS, base + (s + 1) * SEGS)
                cum[0, h, rows, :] = cr
                cum[1, h, rows, :] = ci


def own_kernel(tokens, events, w, out):
    chan = lax.axis_index("chan")
    users, _, width = events.shape
    order = order_matrix(tokens)
    rows = jnp.concatenate([dot(order, events[u]).astype(BF16) for u in range(users)], 0)
    start = pl.ds(pl.multiple_of(chan * width, width), width)
    for c in range(2):
        out[c] = dot(rows, w[c, start, :])


def scan_kernel(tokens, peers, *refs):
    events = refs[:peers]
    weights = refs[peers : peers + 2]
    parts = refs[peers + 2 : peers + 4]
    dec, runs, state, ends, drive = refs[peers + 4 :]
    chan, grp = lax.axis_index("chan"), lax.axis_index("grp")
    users, _, width = events[0].shape
    steps = tokens // SEGS
    order = order_matrix(tokens)
    rows = [
        jnp.concatenate([dot(order, ev[u]).astype(BF16) for u in range(users)], 0) for ev in events
    ]
    for h in range(2):
        place = grp if h == 0 else 1 - grp
        for c in range(2):
            total = parts[h][c]
            for n in range(peers):
                start = pl.multiple_of((chan ^ (n + 1)) * width, width)
                total = total + dot(rows[n], weights[h][c, pl.ds(start, width), :])
            drive[c] = dec[2, h] * total
        for u in range(users):
            base = u * tokens

            def at(s):
                sl = slice(base + s * SEGS, base + (s + 1) * SEGS)
                return dec[0, h, sl, :], dec[1, h, sl, :], drive[0, sl, :], drive[1, sl, :]

            _, _, sr, si = at(0)
            for s in range(1, steps):
                dr, di, vr, vi = at(s)
                xr, xi = cmul(dr, di, sr, si)
                sr, si = xr + vr, xi + vi
            ar = runs[0, h, u * SEGS : (u + 1) * SEGS, :]
            ai = runs[1, h, u * SEGS : (u + 1) * SEGS, :]
            sr, si, er, ei = run_starts(ar, ai, sr, si)
            ends[place, u : u + 1, :] = er
            ends[2 + place, u : u + 1, :] = ei
            for s in range(steps):
                dr, di, vr, vi = at(s)
                xr, xi = cmul(dr, di, sr, si)
                sr, si = xr + vr, xi + vi
                sl = slice(base + s * SEGS, base + (s + 1) * SEGS)
                state[0, h, sl, :] = sr
                state[1, h, sl, :] = si


def carry_kernel(tokens, carry, state, cum, out):
    grp = lax.axis_index("grp")
    users = carry.shape[1]
    order = order_matrix(tokens)
    for h in range(2):
        place = grp if h == 0 else 1 - grp
        cr, ci = carry[place], carry[2 + place]
        for u in range(users):
            sl = slice(u * tokens, (u + 1) * tokens)
            xr, xi = cmul(cum[0, h, sl, :], cum[1, h, sl, :], cr[u : u + 1], ci[u : u + 1])
            for c, value in ((0, state[0, h, sl, :] + xr), (1, state[1, h, sl, :] + xi)):
                moved = lax.dot_general(
                    order, value.astype(BF16), (((0,), (0,)), ((), ())), preferred_element_type=F32
                )
                out[c, h, sl, :] = moved.astype(BF16)


def mix(d, states, w_own, w_oth, width):
    at = (lax.axis_index("chan") * lax.axis_size("grp") + lax.axis_index("grp")) ^ d
    cols = pl.ds(pl.multiple_of(at * width, width), width)
    total = None
    for h, w in enumerate((w_own, w_oth)):
        for c in range(2):
            term = dot(states[c, h], w[c, :, cols])
            total = term if total is None else total + term
    return total


def first_mix_kernel(tokens, d, carry, state, cum, w_own, w_oth, states, out):
    carry_kernel(tokens, carry, state, cum, states)
    out[...] = mix(d, states, w_own, w_oth, out.shape[1]).astype(out.dtype)


def mix_kernel(d, states, w_own, w_oth, out):
    out[...] = mix(d, states, w_own, w_oth, out.shape[1]).astype(out.dtype)


def hold_kernel(source, target, sem):
    copy = pltpu.make_async_copy(source, target, sem)
    copy.start()
    copy.wait()


def final_kernel(tokens, same, cross, lengths, *refs):
    mine, other = refs[:same], refs[same : same + cross]
    events, gain, out = refs[same + cross :]
    users, seg_rows, _ = out.shape
    grp = lax.axis_index("grp")
    first = lax.axis_index("ctx") * seg_rows
    for u in range(users):
        sl = slice(u * tokens, (u + 1) * tokens)
        for where, parts in ((grp, mine), (1 - grp, other)):
            start = pl.multiple_of(where * tokens, tokens)
            total = parts[0][sl, :].astype(F32)
            for part in parts[1:]:
                total = total + part[sl, :].astype(F32)
            own = events[u, pl.ds(start, tokens), :].astype(F32)
            result = jax.nn.gelu(total + gain[...] * own)
            position = first + start + lax.broadcasted_iota(jnp.int32, result.shape, 0)
            result = jnp.where(position < lengths[u], result, 0.0)
            out[u, pl.ds(start, tokens), :] = result.astype(BF16)


def call(body, name, args, out_shape, scratch=(), flops=0, bytes_=0, in_specs=None, out_specs=None):
    single = not isinstance(out_shape, tuple)
    return pl.pallas_call(
        body,
        name=name,
        out_shape=out_shape,
        in_specs=in_specs or [HERE] * len(args),
        out_specs=out_specs or (HERE if single else (HERE,) * len(out_shape)),
        scratch_shapes=list(scratch),
        compiler_params=pltpu.CompilerParams(vmem_limit_bytes=VMEM),
        cost_estimate=pl.CostEstimate(flops=flops, bytes_accessed=bytes_, transcendentals=0),
    )(*args)


def shape(dims, kind):
    return jax.ShapeDtypeStruct(dims, kind)


def join(first, second):
    ar, ai, br, bi = first[0][:2], first[0][2:], second[0][:2], second[0][2:]
    er, ei, fr, fi = first[1][:2], first[1][2:], second[1][:2], second[1][2:]
    pr, pi = cmul(br, bi, ar, ai)
    xr, xi = cmul(br, bi, er, ei)
    return jnp.concatenate([pr, pi]), jnp.concatenate([xr + fr, xi + fi])


def local(
    events, gap_bins, lengths, gap_table, decay_rate, frequency, in_proj, out_proj, skip_gain
):
    users, seg_rows, width = events.shape
    model_width = in_proj.shape[0]
    q = decay_rate.shape[0]
    grps, chans, ctxs = (lax.axis_size(a) for a in ("grp", "chan", "ctx"))
    assert grps == 2
    tokens = seg_rows // grps
    rows = users * tokens
    devices, blocks = chans * grps, ctxs * grps
    part_width = model_width // devices
    grp = lax.axis_index("grp")

    def swap(array, axes, size, k):
        return lax.ppermute(array, axes, [(i, i ^ k) for i in range(size)])

    own_rows = lax.dynamic_slice_in_dim(events, grp * tokens, tokens, 1)
    own_events = lax.dynamic_slice_in_dim(events, grp * part_width, part_width, 2)
    own_rows, own_events = lax.optimization_barrier((own_rows, own_events))
    peer_rows = [swap(own_rows, "chan", chans, k) for k in range(1, chans)]

    rates = jnp.stack([decay_rate, frequency])
    groups = lax.axis_size("groups")
    by = 3 if groups == 2 else 1
    stored = Layout((0, 1, 2))
    raw_oth = swap(with_layout_constraint(in_proj, stored), "grp", grps, 1)
    raw_oth = with_layout_constraint(raw_oth, stored)
    o_oth = swap(out_proj, "grp", grps, 1)
    w_own = jnp.transpose(in_proj, (1, 0, 2))
    w_oth = jnp.transpose(raw_oth, (1, 0, 2))

    parts = [
        call(
            functools.partial(own_kernel, tokens),
            "own_drive_%d" % h,
            (own_rows, w),
            shape((2, rows, q), F32),
            flops=2 * rows * width * 2 * q,
            bytes_=2 * width * q * 2 + 2 * rows * q * 4,
        )
        for h, w in enumerate((w_own, w_oth))
    ]

    rates_oth = swap(rates, ("groups", "grp"), groups * grps, by)
    rates_oth, _ = lax.optimization_barrier((rates_oth, parts[1]))
    both = jnp.stack([rates, rates_oth])
    scaled = gap_table[None, :, None] * both[:, 0][:, None, :]
    turned = gap_table[None, :, None] * both[:, 1][:, None, :]
    magnitude = jnp.exp(-scaled)
    table = jnp.stack(
        [
            magnitude * jnp.cos(turned),
            magnitude * jnp.sin(turned),
            jnp.sqrt(-jnp.expm1(-2.0 * scaled)),
        ],
        1,
    )

    rounds = blocks.bit_length() - 1
    dec, cum, prod, runs, later = call(
        functools.partial(decay_kernel, tokens),
        "decays",
        (gap_bins, table),
        (
            shape((3, 2, rows, q), F32),
            shape((2, 2, rows, q), F32),
            shape((4, users, q), F32),
            shape((2, 2, users * SEGS, q), F32),
            shape((rounds, users, q), jnp.int32),
        ),
        flops=2 * rows * q * 2 * 9 * gap_table.shape[0],
        bytes_=5 * 2 * rows * q * 4,
    )

    peers = chans - 1
    state, ends = call(
        functools.partial(scan_kernel, tokens, peers),
        "drive_scan",
        (*peer_rows, w_own, w_oth, *parts, dec, runs),
        (shape((2, 2, rows, q), F32), shape((4, users, q), F32)),
        scratch=[pltpu.VMEM((2, rows, q), F32)],
        flops=2 * rows * width * 4 * q * peers,
        bytes_=4 * width * q * 2 * peers + 4 * rows * q * 12,
    )

    o_oth = call(hold_kernel, "hold", (o_oth,), shape(o_oth.shape, BF16),
        scratch=[pltpu.SemaphoreType.DMA(())],
        in_specs=[pl.BlockSpec(memory_space=pl.ANY)],
        bytes_=4 * o_oth.size,
    )
    group = (prod, ends)
    before = (jnp.concatenate([jnp.ones_like(prod[:2]), jnp.zeros_like(prod[2:])]), jnp.zeros_like(ends))
    for k in range(rounds):
        theirs = swap(jnp.concatenate(group), ("ctx", "grp"), blocks, 1 << k)
        theirs = (theirs[:4], theirs[4:])
        second = later[k] > 0
        longer = join(theirs, before)
        before = tuple(jnp.where(second, a, b) for a, b in zip(longer, before))
        group = tuple(
            jnp.where(second, a, b) for a, b in zip(join(theirs, group), join(group, theirs))
        )
    carry = before[1]

    order = list(range(2, devices)) + [1]
    received = {}
    states, piece = call(
        functools.partial(first_mix_kernel, tokens, order[0]),
        "carry_mix",
        (carry, state, cum, out_proj, o_oth),
        (shape((2, 2, rows, q), BF16), shape((rows, part_width), BF16)),
        flops=2 * rows * part_width * 4 * q,
        bytes_=4 * q * part_width * 2 + 6 * rows * q * 4,
    )
    received[order[0]] = swap(piece, ("chan", "grp"), devices, order[0])
    for d in order[1:] + [0]:
        piece = call(
            functools.partial(mix_kernel, d),
            "mix_%d" % d,
            (states, out_proj, o_oth),
            shape((rows, part_width), F32 if d < 2 else BF16),
            flops=2 * rows * part_width * 4 * q,
            bytes_=4 * q * part_width * 2 + rows * part_width * 2 + 4 * rows * q * 2,
        )
        received[d] = swap(piece, ("chan", "grp"), devices, d) if d else piece
    same = [received[d] for d in range(0, devices, 2)]
    cross = [received[d] for d in range(1, devices, 2)]

    gain = skip_gain[None]
    given = (lengths, *same, *cross, own_events, gain)
    return call(
        functools.partial(final_kernel, tokens, len(same), len(cross)),
        "final",
        given,
        shape((users, seg_rows, part_width), BF16),
        in_specs=[pl.BlockSpec(memory_space=pltpu.SMEM)] + [HERE] * (len(given) - 1),
        out_specs=HERE,
        bytes_=rows * part_width * 12,
    )


def solution(mesh):
    return jax.shard_map(
        local,
        mesh=mesh,
        in_specs=(
            P("groups", "ctx", "chan"),
            P("groups", "ctx"),
            P("groups"),
            P(),
            P(("chan", "grp")),
            P(("chan", "grp")),
            P(None, None, ("chan", "grp")),
            P(None, ("chan", "grp"), None),
            P(("chan", "grp")),
        ),
        out_specs=P("groups", "ctx", ("chan", "grp")),
        check_vma=False,
    )
```

time: 74.9 us -> 50.3 us (0.67)
  the two profiles are of different devices: /device:TPU:1 before, /device:TPU:0 now
where the time goes in v2:
time: 50.3 us; the launch traced here: 50.1 us
  waiting for transfers between devices  17.7 us (35%)
  Pallas kernels  12.6 us (25%)
  starting transfers between devices  11.4 us (23%)
  local copies, waits for them, and re-layouts  5.85 us (12%)
  other arithmetic  2.24 us (4%)
    ppermute x10, waiting for transfers between devices, swap(): return lax.ppermute(array, axes, [(i, i ^ k) for i in range(size)])  17.7 us
    pallas_call x10, Pallas kernels, call(): pl.pallas_call(body, name=name, out_shape=out_shape, in_specs=in_specs or...  12.6 us
    ppermute x10, starting transfers between devices, swap(): return lax.ppermute(array, axes, [(i, i ^ k) for i in range(size)])  11.4 us
    unnamed x15, local copies, waits for them, and re-layouts  2.9 us
    another operation x1, local copies, waits for them, and re-layouts, local(): raw_oth = with_layout_constraint(raw_oth, stored)  2.86 us
    mul x1, other arithmetic, local(): magnitude * jnp.cos(turned)  1.17 us
  transfers between devices with their start and end apart: 10, of which 5 were waited for; matrix products, arithmetic and copies ran while one was open for 16% of the time, Pallas kernels for 18%

profile of v2, /device:TPU:0, one launch (start us, length us, event | category | flops | bytes accessed | tf_op | source)
XLA Modules:
  0.0 50.1 jit_solution(2428960203523262176)
XLA Ops:
  0.0 0.5 collective-permute-start.1
  0.5 0.1 collective-permute-start.6
  0.5 0.7 %pad_maximum_fusion.5 = (f32[2,512]{1,0:T(2,128)S(1)}, f32[1,2,512]{2,1,0:T(2,128)S(1)}) fusion(f32[1,512]{1,0:T(1,128)} %bitcast.26, f32[1,512]{1,0:T(1,128)} %bitcast.27), kind=kLoop, calls=%fused_computation.54 | loop fusion | flops 1024 | bytes 12288 | tf_op jit(solution)/shard_map/stack | solution.py:274
  1.2 2.7 %collective-permute-start = (f32[2,512]{1,0:T(2,128)S(1)}, f32[2,512]{1,0:T(2,128)S(1)}, u32[]{:S(2)}, u32[]{:S(2)}) collective-permute-start(f32[2,512]{1,0:T(2,128)S(1)} %get-tuple-element.58), channel_id=1, source_target_pairs={{0,17},{1,16},{16,1},{17,0},{2,19},{3,18},{18,3},{19,2},{4,21},{5,... | collective-permute-start | bytes 12296 | tf_op jit(solution)/shard_map/ppermute | solution.py:267
  4.0 1.6 %collective-permute-start.2 = (bf16[2,128,1024]{2,1,0:T(8,128)(2,1)S(1)}, bf16[2,128,1024]{2,1,0:T(8,128)(2,1)S(1)}, u32[]{:S(2)}, u32[]{:S(2)}) collective-permute-start(bf16[2,128,1024]{2,1,0:T(8,128)(2,1)S(1)} %constant_dynamic-slice_fusion.1.events), channel_id=1, source_target_pairs={{0,2},{2,0},{1,3},{3,1},{4,6},{6,4},{5,7},{7,5},{8,10},{10,8},{9,1... | collective-permute-start | bytes 1572872 | tf_op jit(solution)/shard_map/ppermute | solution.py:267
  5.6 2.9 %copy.15 = bf16[2048,2,512]{2,0,1:T(8,128)(2,1)S(1)} copy(bf16[2048,2,512]{2,1,0:T(2,128)(2,1)} %param.15) | data formatting | bytes 8388608 | tf_op args[6]
  8.5 0.9 %own_drive_0.1.refs_3_ = f32[2,256,512]{2,1,0:T(8,128)S(1)} custom-call(bf16[2,128,1024]{2,1,0:T(8,128)(2,1)S(1)} %constant_dynamic-slice_fusion.1.events, bf16[2,2048,512]{2,1,0:T(8,128)(2,1)S(1)} %bitcast.21), custom_call_target="tpu_custom_call" | custom-call | flops 536870912 | bytes 3145728 | tf_op jit(solution)/shard_map/own_drive_0/pallas_call | solution.py:228
  9.3 2.9 %copy.16 = bf16[2048,2,512]{2,0,1:T(8,128)(2,1)S(1)} copy(bf16[2048,2,512]{2,1,0:T(2,128)(2,1)} %collective-permute-done.1) | data formatting | bytes 8388608 | tf_op jit(solution)/shard_map/layout_constraint | solution.py:279
  12.2 0.0 copy-start.6
  12.2 0.9 %own_drive_1.1.refs_4_ = f32[2,256,512]{2,1,0:T(8,128)S(1)} custom-call(bf16[2,128,1024]{2,1,0:T(8,128)(2,1)S(1)} %constant_dynamic-slice_fusion.1.events, bf16[2,2048,512]{2,1,0:T(8,128)(2,1)S(1)} %bitcast.23), custom_call_target="tpu_custom_call" | custom-call | flops 536870912 | bytes 3145728 | tf_op jit(solution)/shard_map/own_drive_1/pallas_call | solution.py:228
  13.2 1.2 %fusion.2 = (f32[2,1,64,512]{3,2,1,0:T(8,128)S(1)}, f32[2,1,64,512]{3,2,1,0:T(8,128)S(1)}, f32[2,1,64,512]{3,2,1,0:T(8,128)S(1)}) fusion(f32[2,512]{1,0:T(2,128)S(1)} %get-tuple-element.55, f32[2,512]{1,0:T(2,128)S(1)} %get-tuple-element.56, f32[64]{0:T(128)S(1)} %copy-done.6), kind=kLoop, calls=%fused_computation.9 | loop fusion | flops 458752 | bytes 794880 | tf_op jit(solution)/shard_map/mul | solution.py:304
  14.3 0.1 pad_maximum_fusion.table
  14.4 1.2 %decays.1 = (f32[3,2,256,512]{3,2,1,0:T(8,128)S(1)}, f32[2,2,256,512]{3,2,1,0:T(8,128)S(1)}, f32[4,2,512]{2,1,0:T(2,128)S(1)}, f32[2,2,16,512]{3,2,1,0:T(8,128)S(1)}, s32[3,2,512]{2,1,0:T(2,128)S(1)}) custom-call(s32[2,256]{1,0:T(2,128)S(1)} %copy-done.4, f32[2,3,64,512]{3,2,1,0:T(8,128)S(1)} %pad_maximum_fusion.table), custom_call_target="tpu_custom_call" | custom-call | flops 301989888 | bytes 5242880 | tf_op jit(solution)/shard_map/decays/pallas_call | solution.py:228
  15.6 2.8 %collective-permute-done.2.refs_0_ = bf16[2,128,1024]{2,1,0:T(8,128)(2,1)S(1)} collective-permute-done((bf16[2,128,1024]{2,1,0:T(8,128)(2,1)S(1)}, bf16[2,128,1024]{2,1,0:T(8,128)(2,1)S(1)}, u32[]{:S(2)}, u32[]{:S(2)}) %collective-permute-start.2) | collective-permute-done | bytes 524320 | tf_op jit(solution)/shard_map/ppermute | solution.py:267
  18.4 2.3 %drive_scan.1 = (f32[2,2,256,512]{3,2,1,0:T(8,128)S(1)}, f32[4,2,512]{2,1,0:T(2,128)S(1)}) custom-call(bf16[2,128,1024]{2,1,0:T(8,128)(2,1)S(1)} %collective-permute-done.2.refs_0_, bf16[2,2048,512]{2,1,0:T(8,128)(2,1)S(1)} %bitcast.22, bf16[2,2048,512]{2,1,0:T(8,128)(2,1)S(1)} %bitcast.24, f32[2,256,512]{2,1,0:T(8,128)S(1)} %own_drive_0.1.refs_3_, ...), custom_call_target="tpu_custom_call" | custom-call | flops 1073741824 | bytes 10485760 | tf_op jit(solution)/shard_map/drive_scan/pallas_call | solution.py:228
  20.7 0.1 collective-permute-start.3
  20.8 1.2 %collective-permute-done.3 = f32[8,2,512]{2,1,0:T(2,128)S(1)} collective-permute-done((f32[8,2,512]{2,1,0:T(2,128)S(1)}, f32[8,2,512]{2,1,0:T(2,128)S(1)}, u32[]{:S(2)}, u32[]{:S(2)}) %collective-permute-start.3) | collective-permute-done | bytes 32800 | tf_op jit(solution)/shard_map/ppermute | solution.py:267
  22.2 1.6 %collective-permute-start.4 = (f32[8,2,512]{2,1,0:T(2,128)S(1)}, f32[8,2,512]{2,1,0:T(2,128)S(1)}, u32[]{:S(2)}, u32[]{:S(2)}) collective-permute-start(f32[8,2,512]{2,1,0:T(2,128)S(1)} %pad_maximum_fusion.2), channel_id=1, source_target_pairs={{0,4},{1,5},{4,0},{5,1},{8,12},{9,13},{12,8},{13,9},{2,6},{3,7},{6... | collective-permute-start | bytes 98312 | tf_op jit(solution)/shard_map/ppermute | solution.py:267
  23.8 2.3 %collective-permute-done.4 = f32[8,2,512]{2,1,0:T(2,128)S(1)} collective-permute-done((f32[8,2,512]{2,1,0:T(2,128)S(1)}, f32[8,2,512]{2,1,0:T(2,128)S(1)}, u32[]{:S(2)}, u32[]{:S(2)}) %collective-permute-start.4) | collective-permute-done | bytes 32800 | tf_op jit(solution)/shard_map/ppermute | solution.py:267
  26.3 2.7 %collective-permute-start.5 = (f32[8,2,512]{2,1,0:T(2,128)S(1)}, f32[8,2,512]{2,1,0:T(2,128)S(1)}, u32[]{:S(2)}, u32[]{:S(2)}) collective-permute-start(f32[8,2,512]{2,1,0:T(2,128)S(1)} %pad_maximum_fusion.3), channel_id=1, source_target_pairs={{0,8},{1,9},{4,12},{5,13},{8,0},{9,1},{12,4},{13,5},{2,10},{3,11},... | collective-permute-start | bytes 98312 | tf_op jit(solution)/shard_map/ppermute | solution.py:267
  29.0 2.2 %hold.1.w_oth = bf16[2,512,2048]{2,1,0:T(8,128)(2,1)S(1)} custom-call(bf16[2,512,2048]{2,1,0:T(8,128)(2,1)} %collective-permute-done.6.source), custom_call_target="tpu_custom_call" | custom-call | bytes 8388608 | tf_op jit(solution)/shard_map/hold/pallas_call | solution.py:228
  31.2 0.0 collective-permute-done.5
  31.2 1.1 %carry_mix.1 = (bf16[2,2,256,512]{3,2,1,0:T(8,128)(2,1)S(1)}, bf16[256,512]{1,0:T(8,128)(2,1)S(1)}) custom-call(f32[4,2,512]{2,1,0:T(2,128)S(1)} %maximum_select_fusion.6.carry, f32[2,2,256,512]{3,2,1,0:T(8,128)S(1)} %get-tuple-element.24.state, f32[2,2,256,512]{3,2,1,0:T(8,128)S(1)} %get-tuple-element.25.cum, bf16[2,512,2048]{2,1,0:T(8,128)(2,1)S(1)} %copy-done.1, ...), custom_call_target="tpu_custom_call" | custom-call | flops 536870912 | bytes 5242880 | tf_op jit(solution)/shard_map/carry_mix/pallas_call | solution.py:228
  32.4 0.7 %mix_1.1 = f32[256,512]{1,0:T(8,128)S(1)} custom-call(bf16[2,2,256,512]{3,2,1,0:T(8,128)(2,1)S(1)} %get-tuple-element.26.states, bf16[2,512,2048]{2,1,0:T(8,128)(2,1)S(1)} %copy-done.1, bf16[2,512,2048]{2,1,0:T(8,128)(2,1)S(1)} %hold.1.w_oth), custom_call_target="tpu_custom_call" | custom-call | flops 536870912 | bytes 3407872 | tf_op jit(solution)/shard_map/mix_1/pallas_call | solution.py:228
  33.1 0.1 collective-permute-start.8
  33.2 0.7 %mix_3.1 = bf16[256,512]{1,0:T(8,128)(2,1)S(1)} custom-call(bf16[2,2,256,512]{3,2,1,0:T(8,128)(2,1)S(1)} %get-tuple-element.26.states, bf16[2,512,2048]{2,1,0:T(8,128)(2,1)S(1)} %copy-done.1, bf16[2,512,2048]{2,1,0:T(8,128)(2,1)S(1)} %hold.1.w_oth), custom_call_target="tpu_custom_call" | custom-call | flops 536870912 | bytes 3407872 | tf_op jit(solution)/shard_map/mix_3/pallas_call | solution.py:228
  33.9 1.6 %collective-permute-start.9 = (bf16[256,512]{1,0:T(8,128)(2,1)S(1)}, bf16[256,512]{1,0:T(8,128)(2,1)S(1)}, u32[]{:S(2)}, u32[]{:S(2)}) collective-permute-start(bf16[256,512]{1,0:T(8,128)(2,1)S(1)} %mix_3.1), channel_id=1, source_target_pairs={{0,3},{1,2},{2,1},{3,0},{4,7},{5,6},{6,5},{7,4},{8,11},{9,10},{10,... | collective-permute-start | bytes 786440 | tf_op jit(solution)/shard_map/ppermute | solution.py:267
  35.5 0.5 %collective-permute-start.7 = (bf16[256,512]{1,0:T(8,128)(2,1)S(1)}, bf16[256,512]{1,0:T(8,128)(2,1)S(1)}, u32[]{:S(2)}, u32[]{:S(2)}) collective-permute-start(bf16[256,512]{1,0:T(8,128)(2,1)S(1)} %get-tuple-element.27), channel_id=1, source_target_pairs={{0,2},{1,3},{2,0},{3,1},{4,6},{5,7},{6,4},{7,5},{8,10},{9,11},{10,... | collective-permute-start | bytes 786440 | tf_op jit(solution)/shard_map/ppermute | solution.py:267
  36.1 0.7 %mix_0.1.refs_0_ = f32[256,512]{1,0:T(8,128)S(1)} custom-call(bf16[2,2,256,512]{3,2,1,0:T(8,128)(2,1)S(1)} %get-tuple-element.26.states, bf16[2,512,2048]{2,1,0:T(8,128)(2,1)S(1)} %copy-done.1, bf16[2,512,2048]{2,1,0:T(8,128)(2,1)S(1)} %hold.1.w_oth), custom_call_target="tpu_custom_call" | custom-call | flops 536870912 | bytes 3407872 | tf_op jit(solution)/shard_map/mix_0/pallas_call | solution.py:228
  36.8 5.4 %collective-permute-done.9.refs_3_ = bf16[256,512]{1,0:T(8,128)(2,1)S(1)} collective-permute-done((bf16[256,512]{1,0:T(8,128)(2,1)S(1)}, bf16[256,512]{1,0:T(8,128)(2,1)S(1)}, u32[]{:S(2)}, u32[]{:S(2)}) %collective-permute-start.9) | collective-permute-done | bytes 262176 | tf_op jit(solution)/shard_map/ppermute | solution.py:267
  42.2 6.0 %collective-permute-done.7.refs_1_ = bf16[256,512]{1,0:T(8,128)(2,1)S(1)} collective-permute-done((bf16[256,512]{1,0:T(8,128)(2,1)S(1)}, bf16[256,512]{1,0:T(8,128)(2,1)S(1)}, u32[]{:S(2)}, u32[]{:S(2)}) %collective-permute-start.7) | collective-permute-done | bytes 262176 | tf_op jit(solution)/shard_map/ppermute | solution.py:267
  48.2 1.9 %final.1 = bf16[2,256,512]{2,1,0:T(8,128)(2,1)} custom-call(s32[2]{0:T(128)S(1)} %copy-done.3, f32[256,512]{1,0:T(8,128)S(1)} %mix_0.1.refs_0_, bf16[256,512]{1,0:T(8,128)(2,1)S(1)} %collective-permute-done.7.refs_1_, f32[256,512]{1,0:T(8,128)S(1)} %collective-permute-done.8.refs_2_, bf16[256,512]{1,0:T(8,128)(2,1)S(1)} %collective-permute-done.9.refs_3_, ...), custom_call_target="tpu_custom_call" | custom-call | bytes 1572864 | tf_op jit(solution)/shard_map/final/pallas_call | solution.py:228
  (35 shorter events, 0.4 us)
Async XLA Ops:
  0.0 3.9 %copy-start = (bf16[2,256,1024]{2,1,0:T(8,128)(2,1)S(1)}, bf16[2,256,1024]{2,1,0:T(8,128)(2,1)}, u32[]{:S(2)}) copy-start(bf16[2,256,1024]{2,1,0:T(8,128)(2,1)} %param.9) | copy-start | bytes 3145732
  0.0 9.3 %collective-permute-start.1 = (bf16[2048,2,512]{2,1,0:T(2,128)(2,1)}, bf16[2048,2,512]{2,1,0:T(2,128)(2,1)}, u32[]{:S(2)}, u32[]{:S(2)}) collective-permute-start(bf16[2048,2,512]{2,1,0:T(2,128)(2,1)} %param.15), channel_id=1, source_target_pairs={{0,1},{1,0},{2,3},{3,2},{4,5},{5,4},{6,7},{7,6},{8,9},{9,8},{10,11... | collective-permute-start | bytes 12582920 | tf_op jit(solution)/shard_map/ppermute | solution.py:267
  0.5 28.5 %collective-permute-start.6 = (bf16[2,512,2048]{2,1,0:T(8,128)(2,1)}, bf16[2,512,2048]{2,1,0:T(8,128)(2,1)}, u32[]{:S(2)}, u32[]{:S(2)}) collective-permute-start(bf16[2,512,2048]{2,1,0:T(8,128)(2,1)} %w_own.7), channel_id=1, source_target_pairs={{0,1},{1,0},{2,3},{3,2},{4,5},{5,4},{6,7},{7,6},{8,9},{9,8},{10,11... | collective-permute-start | bytes 12582920 | tf_op jit(solution)/shard_map/ppermute | solution.py:267
  1.2 11.9 %collective-permute-start = (f32[2,512]{1,0:T(2,128)S(1)}, f32[2,512]{1,0:T(2,128)S(1)}, u32[]{:S(2)}, u32[]{:S(2)}) collective-permute-start(f32[2,512]{1,0:T(2,128)S(1)} %get-tuple-element.58), channel_id=1, source_target_pairs={{0,17},{1,16},{16,1},{17,0},{2,19},{3,18},{18,3},{19,2},{4,21},{5,... | collective-permute-start | bytes 12296 | tf_op jit(solution)/shard_map/ppermute | solution.py:267
  4.0 14.3 %collective-permute-start.2 = (bf16[2,128,1024]{2,1,0:T(8,128)(2,1)S(1)}, bf16[2,128,1024]{2,1,0:T(8,128)(2,1)S(1)}, u32[]{:S(2)}, u32[]{:S(2)}) collective-permute-start(bf16[2,128,1024]{2,1,0:T(8,128)(2,1)S(1)} %constant_dynamic-slice_fusion.1.events), channel_id=1, source_target_pairs={{0,2},{2,0},{1,3},{3,1},{4,6},{6,4},{5,7},{7,5},{8,10},{10,8},{9,1... | collective-permute-start | bytes 1572872 | tf_op jit(solution)/shard_map/ppermute | solution.py:267
  12.2 0.9 %copy-start.6 = (f32[64]{0:T(128)S(1)}, f32[64]{0:T(128)}, u32[]{:S(2)}) copy-start(f32[64]{0:T(128)} %param.12) | copy-start | bytes 772
  12.2 2.2 %copy-start.4 = (s32[2,256]{1,0:T(2,128)S(1)}, s32[2,256]{1,0:T(2,128)}, u32[]{:S(2)}) copy-start(s32[2,256]{1,0:T(2,128)} %bins.1) | copy-start | bytes 6148
  18.4 3.7 %copy-start.5 = (f32[4,2,512]{2,1,0:T(2,128)S(1)}, f32[4,2,512]{2,1,0:T(2,128)}, u32[]{:S(2)}) copy-start(f32[4,2,512]{2,1,0:T(2,128)} %constant.6.clone.1) | copy-start | bytes 49156
  20.7 1.3 %collective-permute-start.3 = (f32[8,2,512]{2,1,0:T(2,128)S(1)}, f32[8,2,512]{2,1,0:T(2,128)S(1)}, u32[]{:S(2)}, u32[]{:S(2)}) collective-permute-start(f32[8,2,512]{2,1,0:T(2,128)S(1)} %pad_maximum_fusion.1), channel_id=1, source_target_pairs={{0,1},{1,0},{4,5},{5,4},{8,9},{9,8},{12,13},{13,12},{2,3},{3,2},{6... | collective-permute-start | bytes 98312 | tf_op jit(solution)/shard_map/ppermute | solution.py:267
  22.2 4.0 %collective-permute-start.4 = (f32[8,2,512]{2,1,0:T(2,128)S(1)}, f32[8,2,512]{2,1,0:T(2,128)S(1)}, u32[]{:S(2)}, u32[]{:S(2)}) collective-permute-start(f32[8,2,512]{2,1,0:T(2,128)S(1)} %pad_maximum_fusion.2), channel_id=1, source_target_pairs={{0,4},{1,5},{4,0},{5,1},{8,12},{9,13},{12,8},{13,9},{2,6},{3,7},{6... | collective-permute-start | bytes 98312 | tf_op jit(solution)/shard_map/ppermute | solution.py:267
  26.3 4.9 %copy-start.1 = (bf16[2,512,2048]{2,1,0:T(8,128)(2,1)S(1)}, bf16[2,512,2048]{2,1,0:T(8,128)(2,1)}, u32[]{:S(2)}) copy-start(bf16[2,512,2048]{2,1,0:T(8,128)(2,1)} %w_own.7) | copy-start | bytes 12582916
  26.3 4.9 %collective-permute-start.5 = (f32[8,2,512]{2,1,0:T(2,128)S(1)}, f32[8,2,512]{2,1,0:T(2,128)S(1)}, u32[]{:S(2)}, u32[]{:S(2)}) collective-permute-start(f32[8,2,512]{2,1,0:T(2,128)S(1)} %pad_maximum_fusion.3), channel_id=1, source_target_pairs={{0,8},{1,9},{4,12},{5,13},{8,0},{9,1},{12,4},{13,5},{2,10},{3,11},... | collective-permute-start | bytes 98312 | tf_op jit(solution)/shard_map/ppermute | solution.py:267
  33.1 15.1 %collective-permute-start.8 = (f32[256,512]{1,0:T(8,128)S(1)}, f32[256,512]{1,0:T(8,128)S(1)}, u32[]{:S(2)}, u32[]{:S(2)}) collective-permute-start(f32[256,512]{1,0:T(8,128)S(1)} %mix_1.1), channel_id=1, source_target_pairs={{0,1},{1,0},{2,3},{3,2},{4,5},{5,4},{6,7},{7,6},{8,9},{9,8},{10,11... | collective-permute-start | bytes 1572872 | tf_op jit(solution)/shard_map/ppermute | solution.py:267
  33.9 8.3 %collective-permute-start.9 = (bf16[256,512]{1,0:T(8,128)(2,1)S(1)}, bf16[256,512]{1,0:T(8,128)(2,1)S(1)}, u32[]{:S(2)}, u32[]{:S(2)}) collective-permute-start(bf16[256,512]{1,0:T(8,128)(2,1)S(1)} %mix_3.1), channel_id=1, source_target_pairs={{0,3},{1,2},{2,1},{3,0},{4,7},{5,6},{6,5},{7,4},{8,11},{9,10},{10,... | collective-permute-start | bytes 786440 | tf_op jit(solution)/shard_map/ppermute | solution.py:267
  35.5 12.6 %copy-start.2 = (f32[512]{0:T(512)S(1)}, f32[512]{0:T(512)}, u32[]{:S(2)}) copy-start(f32[512]{0:T(512)} %param.17) | copy-start | bytes 6148
  35.5 12.6 %copy-start.3 = (s32[2]{0:T(128)S(1)}, s32[2]{0:T(128)}, u32[]{:S(2)}) copy-start(s32[2]{0:T(128)} %lengths.1) | copy-start | bytes 28
  35.5 12.6 %collective-permute-start.7 = (bf16[256,512]{1,0:T(8,128)(2,1)S(1)}, bf16[256,512]{1,0:T(8,128)(2,1)S(1)}, u32[]{:S(2)}, u32[]{:S(2)}) collective-permute-start(bf16[256,512]{1,0:T(8,128)(2,1)S(1)} %get-tuple-element.27), channel_id=1, source_target_pairs={{0,2},{1,3},{2,0},{3,1},{4,6},{5,7},{6,4},{7,5},{8,10},{9,11},{10,... | collective-permute-start | bytes 786440 | tf_op jit(solution)/shard_map/ppermute | solution.py:267

commit v3 on v2

v3 whole, which is shorter than its diff:
```python
import functools

import jax
import jax.numpy as jnp
from jax import lax
from jax.experimental import pallas as pl
from jax.experimental.layout import Layout, with_layout_constraint
from jax.experimental.pallas import tpu as pltpu
from jax.sharding import PartitionSpec as P

F32 = jnp.float32
BF16 = jnp.bfloat16
SEGS = 8
VMEM = 16 * 1024 * 1024
HERE = pl.BlockSpec(memory_space=pltpu.VMEM)


def dot(a, b):
    return jnp.dot(a, b, preferred_element_type=F32)


def cmul(ar, ai, br, bi):
    return ar * br - ai * bi, ar * bi + ai * br


def order_matrix(tokens):
    steps = tokens // SEGS
    r = lax.broadcasted_iota(jnp.int32, (tokens, tokens), 0)
    t = lax.broadcasted_iota(jnp.int32, (tokens, tokens), 1)
    return (t == (r % SEGS) * steps + r // SEGS).astype(F32).astype(BF16)


def run_starts(ar, ai, er, ei):
    cr, ci = jnp.zeros_like(er[:1]), jnp.zeros_like(ei[:1])
    rows_r, rows_i = [], []
    for i in range(SEGS):
        rows_r.append(cr)
        rows_i.append(ci)
        xr, xi = cmul(ar[i : i + 1], ai[i : i + 1], cr, ci)
        cr, ci = xr + er[i : i + 1], xi + ei[i : i + 1]
    return jnp.concatenate(rows_r, 0), jnp.concatenate(rows_i, 0), cr, ci


def run_products(ar, ai):
    cr, ci = jnp.ones_like(ar[:1]), jnp.zeros_like(ai[:1])
    rows_r, rows_i = [], []
    for i in range(SEGS):
        rows_r.append(cr)
        rows_i.append(ci)
        cr, ci = cmul(ar[i : i + 1], ai[i : i + 1], cr, ci)
    return jnp.concatenate(rows_r, 0), jnp.concatenate(rows_i, 0), cr, ci


def decay_kernel(tokens, bins, *refs):
    tables, (dec, cum, prod, runs, later) = refs[:6], refs[6:]
    grp = lax.axis_index("grp")
    users = bins.shape[0]
    count = tables[0].shape[0]
    me = lax.axis_index("ctx") * lax.axis_size("grp") + grp
    for k in range(later.shape[0]):
        later[k] = jnp.full(later.shape[1:], (me >> k) & 1, jnp.int32)
    order = order_matrix(tokens)
    steps = tokens // SEGS
    picks = []
    for u in range(users):
        row = bins[u : u + 1, pl.ds(pl.multiple_of(grp * tokens, tokens), tokens)]
        hit = (lax.broadcasted_iota(jnp.int32, (count, tokens), 0) == row).astype(F32).astype(BF16)
        picks.append(
            lax.dot_general(
                order, hit, (((1,), (1,)), ((), ())), preferred_element_type=F32
            ).astype(BF16)
        )
    pick = jnp.concatenate(picks, 0)
    pick = jnp.concatenate([pick] * 3, 1)
    for h in range(2):
        place = grp if h == 0 else 1 - grp
        for k in range(3):
            full = tables[3 * h + k][...]
            high = full.astype(BF16)
            rest = full - high.astype(F32)
            mid = rest.astype(BF16)
            low = (rest - mid.astype(F32)).astype(BF16)
            dec[k, h] = dot(pick, jnp.concatenate([high, mid, low], 0))
        for u in range(users):
            base = u * tokens

            def at(s):
                rows = slice(base + s * SEGS, base + (s + 1) * SEGS)
                return dec[0, h, rows, :], dec[1, h, rows, :]

            pr, pi = at(0)
            for s in range(1, steps):
                dr, di = at(s)
                pr, pi = cmul(dr, di, pr, pi)
            runs[0, h, u * SEGS : (u + 1) * SEGS, :] = pr
            runs[1, h, u * SEGS : (u + 1) * SEGS, :] = pi
            cr, ci, tr, ti = run_products(pr, pi)
            prod[place, u : u + 1, :] = tr
            prod[2 + place, u : u + 1, :] = ti
            for s in range(steps):
                dr, di = at(s)
                cr, ci = cmul(dr, di, cr, ci)
                rows = slice(base + s * SEGS, base + (s + 1) * SEGS)
                cum[0, h, rows, :] = cr
                cum[1, h, rows, :] = ci


def own_kernel(tokens, events, w, out):
    chan = lax.axis_index("chan")
    users, _, width = events.shape
    order = order_matrix(tokens)
    rows = jnp.concatenate([dot(order, events[u]).astype(BF16) for u in range(users)], 0)
    start = pl.ds(pl.multiple_of(chan * width, width), width)
    for c in range(2):
        out[c] = dot(rows, w[c, start, :])


def scan_kernel(tokens, peers, user, *refs):
    events = refs[:peers]
    weights = refs[peers : peers + 2]
    parts = refs[peers + 2 : peers + 4]
    dec, runs, state, ends, drive = refs[peers + 4 :]
    chan, grp = lax.axis_index("chan"), lax.axis_index("grp")
    width = events[0].shape[1]
    steps = tokens // SEGS
    base = user * tokens
    order = order_matrix(tokens)
    rows = [dot(order, ev[...]).astype(BF16) for ev in events]
    for h in range(2):
        place = grp if h == 0 else 1 - grp
        for c in range(2):
            total = parts[h][c, base : base + tokens, :]
            for n in range(peers):
                start = pl.multiple_of((chan ^ (n + 1)) * width, width)
                total = total + dot(rows[n], weights[h][c, pl.ds(start, width), :])
            drive[c] = dec[2, h, base : base + tokens, :] * total

        def at(s):
            sl = slice(base + s * SEGS, base + (s + 1) * SEGS)
            to = slice(s * SEGS, (s + 1) * SEGS)
            return dec[0, h, sl, :], dec[1, h, sl, :], drive[0, to, :], drive[1, to, :]

        _, _, sr, si = at(0)
        for s in range(1, steps):
            dr, di, vr, vi = at(s)
            xr, xi = cmul(dr, di, sr, si)
            sr, si = xr + vr, xi + vi
        ar = runs[0, h, user * SEGS : (user + 1) * SEGS, :]
        ai = runs[1, h, user * SEGS : (user + 1) * SEGS, :]
        sr, si, er, ei = run_starts(ar, ai, sr, si)
        ends[place] = er
        ends[2 + place] = ei
        for s in range(steps):
            dr, di, vr, vi = at(s)
            xr, xi = cmul(dr, di, sr, si)
            sr, si = xr + vr, xi + vi
            to = slice(s * SEGS, (s + 1) * SEGS)
            state[0, h, to, :] = sr
            state[1, h, to, :] = si


def carry_in(tokens, carry, states, cum, out):
    grp = lax.axis_index("grp")
    order = order_matrix(tokens)
    for h in range(2):
        place = grp if h == 0 else 1 - grp
        cr, ci = carry[place], carry[2 + place]
        for u, state in enumerate(states):
            sl = slice(u * tokens, (u + 1) * tokens)
            xr, xi = cmul(cum[0, h, sl, :], cum[1, h, sl, :], cr[u : u + 1], ci[u : u + 1])
            for c, value in ((0, state[0, h] + xr), (1, state[1, h] + xi)):
                moved = lax.dot_general(
                    order, value.astype(BF16), (((0,), (0,)), ((), ())), preferred_element_type=F32
                )
                out[c, h, sl, :] = moved.astype(BF16)


def mix(d, states, w_own, w_oth, *outs):
    at = (lax.axis_index("chan") * lax.axis_size("grp") + lax.axis_index("grp")) ^ d
    count, width = outs[0].shape
    cols = pl.ds(pl.multiple_of(at * width, width), width)
    total = None
    for h, w in enumerate((w_own, w_oth)):
        for c in range(2):
            term = dot(states[c, h], w[c, :, cols])
            total = term if total is None else total + term
    for i, out in enumerate(outs):
        out[...] = total[i * count : (i + 1) * count].astype(out.dtype)


def far_kernel(tokens, users, far, carry, *refs):
    states, (cum, w_own, w_oth) = refs[:users], refs[users : users + 3]
    rounded, outs = refs[users + 3], refs[users + 4 :]
    carry_in(tokens, carry, states, cum, rounded)
    for d, out in zip(far, outs):
        mix(d, rounded, w_own, w_oth, out)


def near_kernel(states, w_own, w_oth, same, *cross):
    mix(1, states, w_own, w_oth, *cross)
    mix(0, states, w_own, w_oth, same)


def hold_kernel(source, target, sem):
    copy = pltpu.make_async_copy(source, target, sem)
    copy.start()
    copy.wait()


def finish(place, seg_rows, lengths, sums, events, gain, put):
    users = events.shape[0]
    tokens = seg_rows // 2
    start = pl.multiple_of(place * tokens, tokens)
    first = lax.axis_index("ctx") * seg_rows + start
    for u in range(users):
        total = gain[...] * events[u, pl.ds(start, tokens), :].astype(F32)
        for parts in sums:
            if len(parts) == users:
                total = total + parts[u][...].astype(F32)
            else:
                total = total + parts[0][u * tokens : (u + 1) * tokens, :].astype(F32)
        result = jax.nn.gelu(total)
        position = first + lax.broadcasted_iota(jnp.int32, result.shape, 0)
        put(u, start, jnp.where(position < lengths[u], result, 0.0).astype(BF16))


def store(u, start, value, held, out, sems):
    held[u] = value
    copy = pltpu.make_async_copy(
        held.at[u], out.at[u, pl.ds(start, value.shape[0]), :], sems.at[u]
    )
    copy.start()
    return copy


def same_kernel(lengths, events, gain, *refs):
    sums, (out, held, sems) = refs[:-3], refs[-3:]
    copies = []

    def put(u, start, value):
        copies.append(store(u, start, value, held, out, sems))

    finish(lax.axis_index("grp"), events.shape[1], lengths, [(r,) for r in sums], events, gain, put)
    for copy in copies:
        copy.wait()


def final_kernel(users, lengths, events, gain, done, *refs):
    cross, sums, (out, held, sems) = refs[:users], refs[users:-3], refs[-3:]
    copies = []

    def put(u, start, value):
        copies.append(store(u, start, value, held, out, sems))

    sums = [cross] + [(r,) for r in sums]
    finish(1 - lax.axis_index("grp"), events.shape[1], lengths, sums, events, gain, put)
    for copy in copies:
        copy.wait()


def call(body, name, args, out_shape, scratch=(), flops=0, bytes_=0, in_specs=None, out_specs=None, aliases=None):
    single = not isinstance(out_shape, tuple)
    return pl.pallas_call(
        body,
        name=name,
        out_shape=out_shape,
        in_specs=in_specs or [HERE] * len(args),
        out_specs=out_specs or (HERE if single else (HERE,) * len(out_shape)),
        scratch_shapes=list(scratch),
        input_output_aliases=aliases or {},
        compiler_params=pltpu.CompilerParams(vmem_limit_bytes=VMEM),
        cost_estimate=pl.CostEstimate(flops=flops, bytes_accessed=bytes_, transcendentals=0),
    )(*args)


def shape(dims, kind):
    return jax.ShapeDtypeStruct(dims, kind)


def join(first, second):
    ar, ai, br, bi = first[0][:2], first[0][2:], second[0][:2], second[0][2:]
    er, ei, fr, fi = first[1][:2], first[1][2:], second[1][:2], second[1][2:]
    pr, pi = cmul(br, bi, ar, ai)
    xr, xi = cmul(br, bi, er, ei)
    return jnp.concatenate([pr, pi]), jnp.concatenate([xr + fr, xi + fi])


def local(
    events, gap_bins, lengths, gap_table, decay_rate, frequency, in_proj, out_proj, skip_gain
):
    users, seg_rows, width = events.shape
    model_width = in_proj.shape[0]
    q = decay_rate.shape[0]
    grps, chans, ctxs = (lax.axis_size(a) for a in ("grp", "chan", "ctx"))
    assert grps == 2
    tokens = seg_rows // grps
    rows = users * tokens
    devices, blocks = chans * grps, ctxs * grps
    part_width = model_width // devices
    grp = lax.axis_index("grp")

    def swap(array, axes, size, k):
        return lax.ppermute(array, axes, [(i, i ^ k) for i in range(size)])

    own_rows = lax.dynamic_slice_in_dim(events, grp * tokens, tokens, 1)
    own_events = lax.dynamic_slice_in_dim(events, grp * part_width, part_width, 2)
    own_rows, own_events = lax.optimization_barrier((own_rows, own_events))
    peer_rows = [
        [swap(own_rows[u], "chan", chans, k) for k in range(1, chans)] for u in range(users)
    ]

    decay_oth = swap(decay_rate, "grp", grps, 1)
    freq_oth = swap(frequency, "grp", grps, 1)
    in_proj, decay_oth, freq_oth = lax.optimization_barrier((in_proj, decay_oth, freq_oth))
    stored = Layout((0, 1, 2))
    raw_oth = swap(with_layout_constraint(in_proj, stored), "grp", grps, 1)
    raw_oth = with_layout_constraint(raw_oth, stored)
    o_oth = swap(out_proj, "grp", grps, 1)
    w_own = jnp.transpose(in_proj, (1, 0, 2))
    w_oth = jnp.transpose(raw_oth, (1, 0, 2))

    parts = [
        call(
            functools.partial(own_kernel, tokens),
            "own_drive_%d" % h,
            (own_rows, w),
            shape((2, rows, q), F32),
            flops=2 * rows * width * 2 * q,
            bytes_=2 * width * q * 2 + 2 * rows * q * 4,
        )
        for h, w in enumerate((w_own, w_oth))
    ]
    def tables(decay, turn):
        scaled = gap_table[:, None] * decay
        turned = gap_table[:, None] * turn
        magnitude = jnp.exp(-scaled)
        return (
            magnitude * jnp.cos(turned),
            magnitude * jnp.sin(turned),
            jnp.sqrt(-jnp.expm1(-2.0 * scaled)),
        )

    rounds = blocks.bit_length() - 1
    dec, cum, prod, runs, later = call(
        functools.partial(decay_kernel, tokens),
        "decays",
        (gap_bins, *tables(decay_rate, frequency), *tables(decay_oth, freq_oth)),
        (
            shape((3, 2, rows, q), F32),
            shape((2, 2, rows, q), F32),
            shape((4, users, q), F32),
            shape((2, 2, users * SEGS, q), F32),
            shape((rounds, users, q), jnp.int32),
        ),
        flops=2 * rows * q * 2 * 9 * gap_table.shape[0],
        bytes_=5 * 2 * rows * q * 4,
    )

    peers = chans - 1
    states, ends = [], []
    for u in range(users):
        state, end = call(
            functools.partial(scan_kernel, tokens, peers, u),
            "drive_scan_%d" % u,
            (*peer_rows[u], w_own, w_oth, *parts, dec, runs),
            (shape((2, 2, tokens, q), F32), shape((4, 1, q), F32)),
            scratch=[pltpu.VMEM((2, tokens, q), F32)],
            flops=2 * tokens * width * 4 * q * peers,
            bytes_=4 * width * q * 2 * peers + 4 * tokens * q * 12,
        )
        states.append(state)
        ends.append(end)
    ends = jnp.concatenate(ends, 1)
    o_oth = call(
        hold_kernel,
        "hold",
        (o_oth,),
        shape(o_oth.shape, BF16),
        scratch=[pltpu.SemaphoreType.DMA(())],
        in_specs=[pl.BlockSpec(memory_space=pl.ANY)],
        bytes_=4 * o_oth.size,
    )

    group = (prod, ends)
    before = (jnp.concatenate([jnp.ones_like(prod[:2]), jnp.zeros_like(prod[2:])]), jnp.zeros_like(ends))

    def send(k):
        got = swap(jnp.concatenate(group), ("ctx", "grp"), blocks, k)
        return got[:4], got[4:]

    def choose(second, a, b):
        return tuple(jnp.where(second, x, y) for x, y in zip(a, b))

    for k in range(rounds):
        bit = later[k] > 0
        near = send(1 << k)
        before = choose(bit, join(near, before), before)
        group = choose(bit, join(near, group), join(group, near))
    carry = before[1]

    far = list(range(2, devices))
    rounded, *pieces = call(
        functools.partial(far_kernel, tokens, users, far),
        "carry_far",
        (carry, *states, cum, out_proj, o_oth),
        (shape((2, 2, rows, q), BF16),) + (shape((rows, part_width), BF16),) * len(far),
        flops=2 * rows * part_width * 4 * q * len(far),
        bytes_=4 * q * part_width * 2 + 6 * rows * q * 4,
    )
    received = {d: swap(p, ("chan", "grp"), devices, d) for d, p in zip(far, pieces)}
    received[0], *cross = call(
        near_kernel,
        "near",
        (rounded, out_proj, o_oth),
        (shape((rows, part_width), F32),) + (shape((tokens, part_width), BF16),) * users,
        flops=2 * rows * part_width * 8 * q,
        bytes_=8 * q * part_width * 2 + 4 * rows * q * 2,
    )
    cross = [swap(c, ("chan", "grp"), devices, 1) for c in cross]

    common = (lengths, own_events, skip_gain[None])
    kinds = [pl.BlockSpec(memory_space=pltpu.SMEM), HERE, HERE]
    evens = [received[d] for d in range(0, devices, 2)]
    odds = [received[d] for d in range(3, devices, 2)]
    whole = shape((users, seg_rows, part_width), BF16)
    room = [
        pltpu.VMEM((users, tokens, part_width), BF16),
        pltpu.SemaphoreType.DMA((users,)),
    ]
    anywhere = pl.BlockSpec(memory_space=pl.ANY)
    done = call(
        same_kernel,
        "same",
        (*common, *evens),
        whole,
        scratch=room,
        in_specs=kinds + [HERE] * len(evens),
        out_specs=anywhere,
        bytes_=rows * part_width * 8,
    )
    return call(
        functools.partial(final_kernel, users),
        "final",
        (*common, done, *cross, *odds),
        whole,
        scratch=room,
        in_specs=kinds + [anywhere] + [HERE] * (users + len(odds)),
        out_specs=anywhere,
        aliases={3: 0},
        bytes_=rows * part_width * 8,
    )


def solution(mesh):
    return jax.shard_map(
        local,
        mesh=mesh,
        in_specs=(
            P("groups", "ctx", "chan"),
            P("groups", "ctx"),
            P("groups"),
            P(),
            P(("chan", "grp")),
            P(("chan", "grp")),
            P(None, None, ("chan", "grp")),
            P(None, ("chan", "grp"), None),
            P(("chan", "grp")),
        ),
        out_specs=P("groups", "ctx", ("chan", "grp")),
        check_vma=False,
    )
```

time: 50.3 us -> 45.2 us (0.90)
  the two profiles are of different devices: /device:TPU:0 before, /device:TPU:1 now
where the time goes in v3:
time: 45.2 us; the launch traced here: 44.9 us
  Pallas kernels  13.6 us (30%)
  starting transfers between devices  12.6 us (28%)
  waiting for transfers between devices  10.3 us (23%)
  local copies, waits for them, and re-layouts  5.87 us (13%)
  other arithmetic  2.22 us (5%)
    pallas_call x10, Pallas kernels, call(): pl.pallas_call(body, name=name, out_shape=out_shape, in_specs=in_specs or...  13.6 us
    ppermute x13, starting transfers between devices, swap(): return lax.ppermute(array, axes, [(i, i ^ k) for i in range(size)])  12.6 us
    ppermute x13, waiting for transfers between devices, swap(): return lax.ppermute(array, axes, [(i, i ^ k) for i in range(size)])  10.3 us
    optimization_barrier x1, local copies, waits for them, and re-layouts, local(): lax.optimization_barrier((in_proj, decay_oth, freq_oth))  2.87 us
    another operation x1, local copies, waits for them, and re-layouts, local(): raw_oth = with_layout_constraint(raw_oth, stored)  2.86 us
    mul x1, other arithmetic, tables(): magnitude * jnp.sin(turned)  1.88 us
  transfers between devices with their start and end apart: 13, of which 7 were waited for; matrix products, arithmetic and copies ran while one was open for 18% of the time, Pallas kernels for 23%

profile of v3, /device:TPU:1, one launch (start us, length us, event | category | flops | bytes accessed | tf_op | source)
XLA Modules:
  0.0 44.9 jit_solution(530495677609980113)
XLA Ops:
  0.1 0.5 %collective-permute-start.1 = (f32[512]{0:T(512)}, f32[512]{0:T(512)S(1)}, u32[]{:S(2)}, u32[]{:S(2)}) collective-permute-start(f32[512]{0:T(512)} %param.14), channel_id=1, source_target_pairs={{0,1},{1,0},{2,3},{3,2},{4,5},{5,4},{6,7},{7,6},{8,9},{9,8},{10,11... | collective-permute-start | bytes 6152 | tf_op jit(solution)/shard_map/ppermute | solution.py:303
  0.5 0.9 %collective-permute-done = f32[512]{0:T(512)S(1)} collective-permute-done((f32[512]{0:T(512)}, f32[512]{0:T(512)S(1)}, u32[]{:S(2)}, u32[]{:S(2)}) %collective-permute-start) | collective-permute-done | bytes 2080 | tf_op jit(solution)/shard_map/ppermute | solution.py:303
  1.4 0.2 collective-permute-done.1
  1.5 0.3 collective-permute-start.3
  1.9 0.2 collective-permute-start.8
  2.2 2.6 %collective-permute-start.2 = (bf16[128,1024]{1,0:T(8,128)(2,1)S(1)}, bf16[128,1024]{1,0:T(8,128)(2,1)S(1)}, u32[]{:S(2)}, u32[]{:S(2)}) collective-permute-start(bf16[128,1024]{1,0:T(8,128)(2,1)S(1)} %get-tuple-element.45), channel_id=1, source_target_pairs={{0,2},{2,0},{1,3},{3,1},{4,6},{6,4},{5,7},{7,5},{8,10},{10,8},{9,1... | collective-permute-start | bytes 786440 | tf_op jit(solution)/shard_map/ppermute | solution.py:303
  4.8 0.1 collective-permute-start.4
  4.9 1.9 %fusion.7 = (f32[64,512]{1,0:T(8,128)S(1)}, f32[64,512]{1,0:T(8,128)S(1)}, f32[64,512]{1,0:T(8,128)S(1)}, f32[64,512]{1,0:T(8,128)S(1)}, f32[64,512]{1,0:T(8,128)S(1)}, /*index=5*/f32[64,512]{1,0:T(8,128)S(1)}) fusion(f32[512]{0:T(512)S(1)} %collective-permute-done.1, f32[512]{0:T(512)S(1)} %collective-permute-done, f32[64]{0:T(128)} %param.12, ...), kind=kLoop, calls=%fused_computation.19 | loop fusion | flops 458752 | bytes 794880 | tf_op jit(solution)/shard_map/mul | solution.py:339
  6.8 2.9 %copy.16 = bf16[2048,2,512]{2,0,1:T(8,128)(2,1)S(1)} copy(bf16[2048,2,512]{2,1,0:T(2,128)(2,1)} %param.15) | data formatting | bytes 8388608 | tf_op jit(solution)/shard_map/optimization_barrier | solution.py:314
  9.7 1.2 %decays.1 = (f32[3,2,256,512]{3,2,1,0:T(8,128)S(1)}, f32[2,2,256,512]{3,2,1,0:T(8,128)S(1)}, f32[4,2,512]{2,1,0:T(2,128)S(1)}, f32[2,2,16,512]{3,2,1,0:T(8,128)S(1)}, s32[3,2,512]{2,1,0:T(2,128)S(1)}) custom-call(s32[2,256]{1,0:T(2,128)S(1)} %copy-done.4, f32[64,512]{1,0:T(8,128)S(1)} %get-tuple-element.84.refs_0_, f32[64,512]{1,0:T(8,128)S(1)} %get-tuple-element.85.refs_1_, ...), custom_call_target="tpu_custom_call" | custom-call | flops 301989888 | bytes 5242880 | tf_op jit(solution)/shard_map/decays/pallas_call | solution.py:263
  10.9 0.9 %own_drive_0.1.refs_3_ = f32[2,256,512]{2,1,0:T(8,128)S(1)} custom-call(bf16[2,128,1024]{2,1,0:T(8,128)(2,1)S(1)} %constant_dynamic-slice_fusion.1.events, bf16[2,2048,512]{2,1,0:T(8,128)(2,1)S(1)} %bitcast.17), custom_call_target="tpu_custom_call" | custom-call | flops 536870912 | bytes 3145728 | tf_op jit(solution)/shard_map/own_drive_0/pallas_call | solution.py:263
  11.8 2.9 %copy.15 = bf16[2048,2,512]{2,0,1:T(8,128)(2,1)S(1)} copy(bf16[2048,2,512]{2,1,0:T(2,128)(2,1)} %collective-permute-done.3) | data formatting | bytes 8388608 | tf_op jit(solution)/shard_map/layout_constraint | solution.py:317
  14.6 0.9 %own_drive_1.1.refs_4_ = f32[2,256,512]{2,1,0:T(8,128)S(1)} custom-call(bf16[2,128,1024]{2,1,0:T(8,128)(2,1)S(1)} %constant_dynamic-slice_fusion.1.events, bf16[2,2048,512]{2,1,0:T(8,128)(2,1)S(1)} %bitcast.20), custom_call_target="tpu_custom_call" | custom-call | flops 536870912 | bytes 3145728 | tf_op jit(solution)/shard_map/own_drive_1/pallas_call | solution.py:263
  15.5 1.2 %drive_scan_0.1 = (f32[2,2,128,512]{3,2,1,0:T(8,128)S(1)}, f32[4,1,512]{2,1,0:T(1,128)S(1)}) custom-call(bf16[128,1024]{1,0:T(8,128)(2,1)S(1)} %collective-permute-done.2.refs_0_, bf16[2,2048,512]{2,1,0:T(8,128)(2,1)S(1)} %bitcast.18, bf16[2,2048,512]{2,1,0:T(8,128)(2,1)S(1)} %bitcast.21, f32[2,256,512]{2,1,0:T(8,128)S(1)} %own_drive_0.1.refs_3_, ...), custom_call_target="tpu_custom_call" | custom-call | flops 536870912 | bytes 7340032 | tf_op jit(solution)/shard_map/drive_scan_0/pallas_call | solution.py:263
  16.7 0.3 collective-permute-done.4.refs_0_
  17.0 1.2 %drive_scan_1.1 = (f32[2,2,128,512]{3,2,1,0:T(8,128)S(1)}, f32[4,1,512]{2,1,0:T(1,128)S(1)}) custom-call(bf16[128,1024]{1,0:T(8,128)(2,1)S(1)} %collective-permute-done.4.refs_0_, bf16[2,2048,512]{2,1,0:T(8,128)(2,1)S(1)} %bitcast.19, bf16[2,2048,512]{2,1,0:T(8,128)(2,1)S(1)} %bitcast.22, f32[2,256,512]{2,1,0:T(8,128)S(1)} %own_drive_0.1.refs_3_, ...), custom_call_target="tpu_custom_call" | custom-call | flops 536870912 | bytes 7340032 | tf_op jit(solution)/shard_map/drive_scan_1/pallas_call | solution.py:263
  18.3 0.7 %collective-permute-start.5 = (f32[8,2,512]{2,1,0:T(2,128)S(1)}, f32[8,2,512]{2,1,0:T(2,128)S(1)}, u32[]{:S(2)}, u32[]{:S(2)}) collective-permute-start(f32[8,2,512]{2,1,0:T(2,128)S(1)} %maximum_maximum_fusion), channel_id=1, source_target_pairs={{0,1},{1,0},{4,5},{5,4},{8,9},{9,8},{12,13},{13,12},{2,3},{3,2},{6... | collective-permute-start | bytes 98312 | tf_op jit(solution)/shard_map/ppermute | solution.py:303
  19.0 0.8 %collective-permute-done.5 = f32[8,2,512]{2,1,0:T(2,128)S(1)} collective-permute-done((f32[8,2,512]{2,1,0:T(2,128)S(1)}, f32[8,2,512]{2,1,0:T(2,128)S(1)}, u32[]{:S(2)}, u32[]{:S(2)}) %collective-permute-start.5) | collective-permute-done | bytes 32800 | tf_op jit(solution)/shard_map/ppermute | solution.py:303
  20.1 1.6 %collective-permute-start.6 = (f32[8,2,512]{2,1,0:T(2,128)S(1)}, f32[8,2,512]{2,1,0:T(2,128)S(1)}, u32[]{:S(2)}, u32[]{:S(2)}) collective-permute-start(f32[8,2,512]{2,1,0:T(2,128)S(1)} %pad_maximum_fusion), channel_id=1, source_target_pairs={{0,4},{1,5},{4,0},{5,1},{8,12},{9,13},{12,8},{13,9},{2,6},{3,7},{6... | collective-permute-start | bytes 98312 | tf_op jit(solution)/shard_map/ppermute | solution.py:303
  21.7 1.3 %collective-permute-done.6 = f32[8,2,512]{2,1,0:T(2,128)S(1)} collective-permute-done((f32[8,2,512]{2,1,0:T(2,128)S(1)}, f32[8,2,512]{2,1,0:T(2,128)S(1)}, u32[]{:S(2)}, u32[]{:S(2)}) %collective-permute-start.6) | collective-permute-done | bytes 32800 | tf_op jit(solution)/shard_map/ppermute | solution.py:303
  23.1 2.5 %collective-permute-start.7 = (f32[8,2,512]{2,1,0:T(2,128)S(1)}, f32[8,2,512]{2,1,0:T(2,128)S(1)}, u32[]{:S(2)}, u32[]{:S(2)}) collective-permute-start(f32[8,2,512]{2,1,0:T(2,128)S(1)} %pad_maximum_fusion.1), channel_id=1, source_target_pairs={{0,8},{1,9},{4,12},{5,13},{8,0},{9,1},{12,4},{13,5},{2,10},{3,11},... | collective-permute-start | bytes 98312 | tf_op jit(solution)/shard_map/ppermute | solution.py:303
  25.7 2.2 %hold.1.refs_4_.w_oth = bf16[2,512,2048]{2,1,0:T(8,128)(2,1)S(1)} custom-call(bf16[2,512,2048]{2,1,0:T(8,128)(2,1)} %collective-permute-done.8.source), custom_call_target="tpu_custom_call" | custom-call | bytes 8388608 | tf_op jit(solution)/shard_map/hold/pallas_call | solution.py:263
  27.9 1.7 %carry_far.1 = (bf16[2,2,256,512]{3,2,1,0:T(8,128)(2,1)S(1)}, bf16[256,512]{1,0:T(8,128)(2,1)S(1)}, bf16[256,512]{1,0:T(8,128)(2,1)S(1)}) custom-call(f32[4,2,512]{2,1,0:T(2,128)S(1)} %maximum_select_fusion.6.carry, f32[2,2,128,512]{3,2,1,0:T(8,128)S(1)} %get-tuple-element.36.refs_0_, f32[2,2,128,512]{3,2,1,0:T(8,128)S(1)} %get-tuple-element.37.refs_1_, ...), custom_call_target="tpu_custom_call" | custom-call | flops 1073741824 | bytes 5242880 | tf_op jit(solution)/shard_map/carry_far/pallas_call | solution.py:263
  29.7 1.3 %collective-permute-start.9 = (bf16[256,512]{1,0:T(8,128)(2,1)S(1)}, bf16[256,512]{1,0:T(8,128)(2,1)S(1)}, u32[]{:S(2)}, u32[]{:S(2)}) collective-permute-start(bf16[256,512]{1,0:T(8,128)(2,1)S(1)} %get-tuple-element.41), channel_id=1, source_target_pairs={{0,2},{1,3},{2,0},{3,1},{4,6},{5,7},{6,4},{7,5},{8,10},{9,11},{10,... | collective-permute-start | bytes 786440 | tf_op jit(solution)/shard_map/ppermute | solution.py:303
  31.0 2.2 %collective-permute-start.12 = (bf16[256,512]{1,0:T(8,128)(2,1)S(1)}, bf16[256,512]{1,0:T(8,128)(2,1)S(1)}, u32[]{:S(2)}, u32[]{:S(2)}) collective-permute-start(bf16[256,512]{1,0:T(8,128)(2,1)S(1)} %get-tuple-element.44), channel_id=1, source_target_pairs={{0,3},{1,2},{2,1},{3,0},{4,7},{5,6},{6,5},{7,4},{8,11},{9,10},{10,... | collective-permute-start | bytes 786440 | tf_op jit(solution)/shard_map/ppermute | solution.py:303
  33.2 1.2 %near.1 = (f32[256,512]{1,0:T(8,128)S(1)}, bf16[128,512]{1,0:T(8,128)(2,1)S(1)}, bf16[128,512]{1,0:T(8,128)(2,1)S(1)}) custom-call(bf16[2,2,256,512]{3,2,1,0:T(8,128)(2,1)S(1)} %get-tuple-element.39.states, bf16[2,512,2048]{2,1,0:T(8,128)(2,1)S(1)} %copy-done.1, bf16[2,512,2048]{2,1,0:T(8,128)(2,1)S(1)} %hold.1.refs_4_.w_oth), custom_call_target="tpu_custom_call" | custom-call | flops 1073741824 | bytes 5242880 | tf_op jit(solution)/shard_map/near/pallas_call | solution.py:263
  34.4 0.1 collective-permute-start.10
  34.5 0.5 %collective-permute-start.11 = (bf16[128,512]{1,0:T(8,128)(2,1)S(1)}, bf16[128,512]{1,0:T(8,128)(2,1)S(1)}, u32[]{:S(2)}, u32[]{:S(2)}) collective-permute-start(bf16[128,512]{1,0:T(8,128)(2,1)S(1)} %get-tuple-element.43), channel_id=1, source_target_pairs={{0,1},{1,0},{2,3},{3,2},{4,5},{5,4},{6,7},{7,6},{8,9},{9,8},{10,11... | collective-permute-start | bytes 393224 | tf_op jit(solution)/shard_map/ppermute | solution.py:303
  35.0 0.8 %collective-permute-done.9.refs_1_ = bf16[256,512]{1,0:T(8,128)(2,1)S(1)} collective-permute-done((bf16[256,512]{1,0:T(8,128)(2,1)S(1)}, bf16[256,512]{1,0:T(8,128)(2,1)S(1)}, u32[]{:S(2)}, u32[]{:S(2)}) %collective-permute-start.9) | collective-permute-done | bytes 262176 | tf_op jit(solution)/shard_map/ppermute | solution.py:303
  35.8 1.5 %same.1.done = bf16[2,256,512]{2,1,0:T(8,128)(2,1)} custom-call(s32[2]{0:T(128)S(1)} %copy-done.3, bf16[2,256,512]{2,1,0:T(8,128)(2,1)S(1)} %constant_dynamic-slice_fusion.events, f32[1,512]{1,0:T(1,128)S(1)} %bitcast.23, f32[256,512]{1,0:T(8,128)S(1)} %get-tuple-element.40.refs_0_, bf16[256,512]{1,0:T(8,128)(2,1)S(1)} %collective-permute-done.9.refs_1_), custom_call_target="tpu_custom_call" | custom-call | bytes 1048576 | tf_op jit(solution)/shard_map/same/pallas_call | solution.py:263
  37.3 6.1 %collective-permute-done.12.refs_2_ = bf16[256,512]{1,0:T(8,128)(2,1)S(1)} collective-permute-done((bf16[256,512]{1,0:T(8,128)(2,1)S(1)}, bf16[256,512]{1,0:T(8,128)(2,1)S(1)}, u32[]{:S(2)}, u32[]{:S(2)}) %collective-permute-start.12) | collective-permute-done | bytes 262176 | tf_op jit(solution)/shard_map/ppermute | solution.py:303
  43.4 1.5 %final.1 = bf16[2,256,512]{2,1,0:T(8,128)(2,1)} custom-call(s32[2]{0:T(128)S(1)} %copy-done.3, bf16[2,256,512]{2,1,0:T(8,128)(2,1)S(1)} %constant_dynamic-slice_fusion.events, f32[1,512]{1,0:T(1,128)S(1)} %bitcast.24, bf16[2,256,512]{2,1,0:T(8,128)(2,1)} %same.1.done, ...), custom_call_target="tpu_custom_call", output_to_operand_aliasing={{}: (3, {})} | custom-call | bytes 1048576 | tf_op jit(solution)/shard_map/final/pallas_call | solution.py:263
  (36 shorter events, 0.6 us)
Async XLA Ops:
  0.0 2.1 %copy-start = (bf16[2,256,1024]{2,1,0:T(8,128)(2,1)S(1)}, bf16[2,256,1024]{2,1,0:T(8,128)(2,1)}, u32[]{:S(2)}) copy-start(bf16[2,256,1024]{2,1,0:T(8,128)(2,1)} %param.9) | copy-start | bytes 3145732
  0.0 1.4 %collective-permute-start = (f32[512]{0:T(512)}, f32[512]{0:T(512)S(1)}, u32[]{:S(2)}, u32[]{:S(2)}) collective-permute-start(f32[512]{0:T(512)} %param.13), channel_id=1, source_target_pairs={{0,1},{1,0},{2,3},{3,2},{4,5},{5,4},{6,7},{7,6},{8,9},{9,8},{10,11... | collective-permute-start | bytes 6152 | tf_op jit(solution)/shard_map/ppermute | solution.py:303
  0.1 1.5 %collective-permute-start.1 = (f32[512]{0:T(512)}, f32[512]{0:T(512)S(1)}, u32[]{:S(2)}, u32[]{:S(2)}) collective-permute-start(f32[512]{0:T(512)} %param.14), channel_id=1, source_target_pairs={{0,1},{1,0},{2,3},{3,2},{4,5},{5,4},{6,7},{7,6},{8,9},{9,8},{10,11... | collective-permute-start | bytes 6152 | tf_op jit(solution)/shard_map/ppermute | solution.py:303
  1.5 10.2 %collective-permute-start.3 = (bf16[2048,2,512]{2,1,0:T(2,128)(2,1)}, bf16[2048,2,512]{2,1,0:T(2,128)(2,1)}, u32[]{:S(2)}, u32[]{:S(2)}) collective-permute-start(bf16[2048,2,512]{2,1,0:T(2,128)(2,1)} %param.15), channel_id=1, source_target_pairs={{0,1},{1,0},{2,3},{3,2},{4,5},{5,4},{6,7},{7,6},{8,9},{9,8},{10,11... | collective-permute-start | bytes 12582920 | tf_op jit(solution)/shard_map/ppermute | solution.py:303
  1.9 23.8 %collective-permute-start.8 = (bf16[2,512,2048]{2,1,0:T(8,128)(2,1)}, bf16[2,512,2048]{2,1,0:T(8,128)(2,1)}, u32[]{:S(2)}, u32[]{:S(2)}) collective-permute-start(bf16[2,512,2048]{2,1,0:T(8,128)(2,1)} %w_own.1), channel_id=1, source_target_pairs={{0,1},{1,0},{2,3},{3,2},{4,5},{5,4},{6,7},{7,6},{8,9},{9,8},{10,11... | collective-permute-start | bytes 12582920 | tf_op jit(solution)/shard_map/ppermute | solution.py:303
  2.2 13.3 %collective-permute-start.2 = (bf16[128,1024]{1,0:T(8,128)(2,1)S(1)}, bf16[128,1024]{1,0:T(8,128)(2,1)S(1)}, u32[]{:S(2)}, u32[]{:S(2)}) collective-permute-start(bf16[128,1024]{1,0:T(8,128)(2,1)S(1)} %get-tuple-element.45), channel_id=1, source_target_pairs={{0,2},{2,0},{1,3},{3,1},{4,6},{6,4},{5,7},{7,5},{8,10},{10,8},{9,1... | collective-permute-start | bytes 786440 | tf_op jit(solution)/shard_map/ppermute | solution.py:303
  4.8 12.2 %collective-permute-start.4 = (bf16[128,1024]{1,0:T(8,128)(2,1)S(1)}, bf16[128,1024]{1,0:T(8,128)(2,1)S(1)}, u32[]{:S(2)}, u32[]{:S(2)}) collective-permute-start(bf16[128,1024]{1,0:T(8,128)(2,1)S(1)} %get-tuple-element.46), channel_id=1, source_target_pairs={{0,2},{2,0},{1,3},{3,1},{4,6},{6,4},{5,7},{7,5},{8,10},{10,8},{9,1... | collective-permute-start | bytes 786440 | tf_op jit(solution)/shard_map/ppermute | solution.py:303
  6.8 2.9 %copy-start.4 = (s32[2,256]{1,0:T(2,128)S(1)}, s32[2,256]{1,0:T(2,128)}, u32[]{:S(2)}) copy-start(s32[2,256]{1,0:T(2,128)} %bins.1) | copy-start | bytes 6148
  16.7 3.2 %copy-start.5 = (f32[4,2,512]{2,1,0:T(2,128)S(1)}, f32[4,2,512]{2,1,0:T(2,128)}, u32[]{:S(2)}) copy-start(f32[4,2,512]{2,1,0:T(2,128)} %constant.6.clone.1) | copy-start | bytes 49156
  18.3 1.6 %collective-permute-start.5 = (f32[8,2,512]{2,1,0:T(2,128)S(1)}, f32[8,2,512]{2,1,0:T(2,128)S(1)}, u32[]{:S(2)}, u32[]{:S(2)}) collective-permute-start(f32[8,2,512]{2,1,0:T(2,128)S(1)} %maximum_maximum_fusion), channel_id=1, source_target_pairs={{0,1},{1,0},{4,5},{5,4},{8,9},{9,8},{12,13},{13,12},{2,3},{3,2},{6... | collective-permute-start | bytes 98312 | tf_op jit(solution)/shard_map/ppermute | solution.py:303
  20.1 2.9 %collective-permute-start.6 = (f32[8,2,512]{2,1,0:T(2,128)S(1)}, f32[8,2,512]{2,1,0:T(2,128)S(1)}, u32[]{:S(2)}, u32[]{:S(2)}) collective-permute-start(f32[8,2,512]{2,1,0:T(2,128)S(1)} %pad_maximum_fusion), channel_id=1, source_target_pairs={{0,4},{1,5},{4,0},{5,1},{8,12},{9,13},{12,8},{13,9},{2,6},{3,7},{6... | collective-permute-start | bytes 98312 | tf_op jit(solution)/shard_map/ppermute | solution.py:303
  23.1 4.8 %copy-start.1 = (bf16[2,512,2048]{2,1,0:T(8,128)(2,1)S(1)}, bf16[2,512,2048]{2,1,0:T(8,128)(2,1)}, u32[]{:S(2)}) copy-start(bf16[2,512,2048]{2,1,0:T(8,128)(2,1)} %w_own.1) | copy-start | bytes 12582916
  23.1 4.7 %collective-permute-start.7 = (f32[8,2,512]{2,1,0:T(2,128)S(1)}, f32[8,2,512]{2,1,0:T(2,128)S(1)}, u32[]{:S(2)}, u32[]{:S(2)}) collective-permute-start(f32[8,2,512]{2,1,0:T(2,128)S(1)} %pad_maximum_fusion.1), channel_id=1, source_target_pairs={{0,8},{1,9},{4,12},{5,13},{8,0},{9,1},{12,4},{13,5},{2,10},{3,11},... | collective-permute-start | bytes 98312 | tf_op jit(solution)/shard_map/ppermute | solution.py:303
  29.7 6.1 %collective-permute-start.9 = (bf16[256,512]{1,0:T(8,128)(2,1)S(1)}, bf16[256,512]{1,0:T(8,128)(2,1)S(1)}, u32[]{:S(2)}, u32[]{:S(2)}) collective-permute-start(bf16[256,512]{1,0:T(8,128)(2,1)S(1)} %get-tuple-element.41), channel_id=1, source_target_pairs={{0,2},{1,3},{2,0},{3,1},{4,6},{5,7},{6,4},{7,5},{8,10},{9,11},{10,... | collective-permute-start | bytes 786440 | tf_op jit(solution)/shard_map/ppermute | solution.py:303
  31.0 12.4 %collective-permute-start.12 = (bf16[256,512]{1,0:T(8,128)(2,1)S(1)}, bf16[256,512]{1,0:T(8,128)(2,1)S(1)}, u32[]{:S(2)}, u32[]{:S(2)}) collective-permute-start(bf16[256,512]{1,0:T(8,128)(2,1)S(1)} %get-tuple-element.44), channel_id=1, source_target_pairs={{0,3},{1,2},{2,1},{3,0},{4,7},{5,6},{6,5},{7,4},{8,11},{9,10},{10,... | collective-permute-start | bytes 786440 | tf_op jit(solution)/shard_map/ppermute | solution.py:303
  33.2 2.6 %copy-start.2 = (f32[512]{0:T(512)S(1)}, f32[512]{0:T(512)}, u32[]{:S(2)}) copy-start(f32[512]{0:T(512)} %param.17) | copy-start | bytes 6148
  33.2 2.6 %copy-start.3 = (s32[2]{0:T(128)S(1)}, s32[2]{0:T(128)}, u32[]{:S(2)}) copy-start(s32[2]{0:T(128)} %lengths.3) | copy-start | bytes 28
  34.4 2.9 %collective-permute-start.10 = (bf16[128,512]{1,0:T(8,128)(2,1)S(1)}, bf16[128,512]{1,0:T(8,128)(2,1)S(1)}, u32[]{:S(2)}, u32[]{:S(2)}) collective-permute-start(bf16[128,512]{1,0:T(8,128)(2,1)S(1)} %get-tuple-element.42), channel_id=1, source_target_pairs={{0,1},{1,0},{2,3},{3,2},{4,5},{5,4},{6,7},{7,6},{8,9},{9,8},{10,11... | collective-permute-start | bytes 393224 | tf_op jit(solution)/shard_map/ppermute | solution.py:303
  34.5 2.8 %collective-permute-start.11 = (bf16[128,512]{1,0:T(8,128)(2,1)S(1)}, bf16[128,512]{1,0:T(8,128)(2,1)S(1)}, u32[]{:S(2)}, u32[]{:S(2)}) collective-permute-start(bf16[128,512]{1,0:T(8,128)(2,1)S(1)} %get-tuple-element.43), channel_id=1, source_target_pairs={{0,1},{1,0},{2,3},{3,2},{4,5},{5,4},{6,7},{7,6},{8,9},{9,8},{10,11... | collective-permute-start | bytes 393224 | tf_op jit(solution)/shard_map/ppermute | solution.py:303

commit v4 on v3

v4 whole, which is shorter than its diff:
```python
import functools

import jax
import jax.numpy as jnp
from jax import lax
from jax.experimental import pallas as pl
from jax.experimental.layout import Layout, with_layout_constraint
from jax.experimental.pallas import tpu as pltpu
from jax.sharding import PartitionSpec as P

F32 = jnp.float32
BF16 = jnp.bfloat16
SEGS = 8
VMEM = 16 * 1024 * 1024
HERE = pl.BlockSpec(memory_space=pltpu.VMEM)


def dot(a, b):
    return jnp.dot(a, b, preferred_element_type=F32)


def cmul(ar, ai, br, bi):
    return ar * br - ai * bi, ar * bi + ai * br


def order_matrix(tokens):
    steps = tokens // SEGS
    r = lax.broadcasted_iota(jnp.int32, (tokens, tokens), 0)
    t = lax.broadcasted_iota(jnp.int32, (tokens, tokens), 1)
    return (t == (r % SEGS) * steps + r // SEGS).astype(F32).astype(BF16)


def run_starts(ar, ai, er, ei, cr, ci):
    rows_r, rows_i = [], []
    for i in range(SEGS):
        rows_r.append(cr)
        rows_i.append(ci)
        xr, xi = cmul(ar[i : i + 1], ai[i : i + 1], cr, ci)
        cr, ci = xr + er[i : i + 1], xi + ei[i : i + 1]
    return jnp.concatenate(rows_r, 0), jnp.concatenate(rows_i, 0), cr, ci


def run_products(ar, ai, cr, ci):
    rows_r, rows_i = [], []
    for i in range(SEGS):
        rows_r.append(cr)
        rows_i.append(ci)
        cr, ci = cmul(ar[i : i + 1], ai[i : i + 1], cr, ci)
    return jnp.concatenate(rows_r, 0), jnp.concatenate(rows_i, 0), cr, ci


def step_rows(tokens, chunk, s):
    start = chunk * tokens + s * SEGS
    return slice(start, start + SEGS)


def decay_kernel(tokens, bins, *refs):
    tables, (dec, prod, runs, starts, later) = refs[:6], refs[6:]
    grp = lax.axis_index("grp")
    count = tables[0].shape[0]
    ctx = lax.axis_index("ctx")
    for k in range(later.shape[0]):
        later[k] = jnp.full(later.shape[1:], (ctx >> k) & 1, jnp.int32)
    order = order_matrix(tokens)
    steps = tokens // SEGS
    chunks = bins.shape[1] // tokens
    picks = []
    for u in range(chunks):
        at = slice(u * tokens, (u + 1) * tokens)
        row = jnp.where(grp == 0, bins[0:1, at], bins[1:2, at])
        hit = (lax.broadcasted_iota(jnp.int32, (count, tokens), 0) == row).astype(F32).astype(BF16)
        picks.append(
            lax.dot_general(
                order, hit, (((1,), (1,)), ((), ())), preferred_element_type=F32
            ).astype(BF16)
        )
    pick = jnp.concatenate(picks, 0)
    pick = jnp.concatenate([pick] * 3, 1)
    for h in range(2):
        place = grp if h == 0 else 1 - grp
        for k in range(3):
            full = tables[3 * h + k][...]
            high = full.astype(BF16)
            rest = full - high.astype(F32)
            mid = rest.astype(BF16)
            low = (rest - mid.astype(F32)).astype(BF16)
            dec[k, h] = dot(pick, jnp.concatenate([high, mid, low], 0))
        cr = jnp.ones((1, dec.shape[3]), F32)
        ci = jnp.zeros((1, dec.shape[3]), F32)
        for u in range(chunks):
            at = step_rows(tokens, u, 0)
            pr, pi = dec[0, h, at, :], dec[1, h, at, :]
            for s in range(1, steps):
                at = step_rows(tokens, u, s)
                pr, pi = cmul(dec[0, h, at, :], dec[1, h, at, :], pr, pi)
            at = slice(u * SEGS, (u + 1) * SEGS)
            runs[0, h, at, :] = pr
            runs[1, h, at, :] = pi
            starts[0, h, at, :], starts[1, h, at, :], cr, ci = run_products(pr, pi, cr, ci)
        prod[place] = cr
        prod[2 + place] = ci


def product_kernel(tokens, dec, starts, cum):
    for h in range(2):
        for u in range(dec.shape[2] // tokens):
            at = slice(u * SEGS, (u + 1) * SEGS)
            cr, ci = starts[0, h, at, :], starts[1, h, at, :]
            for s in range(tokens // SEGS):
                at = step_rows(tokens, u, s)
                cr, ci = cmul(dec[0, h, at, :], dec[1, h, at, :], cr, ci)
                cum[0, h, at, :] = cr
                cum[1, h, at, :] = ci


def own_kernel(tokens, events, w, out):
    chan = lax.axis_index("chan")
    seg_rows, width = events.shape
    order = order_matrix(tokens)
    rows = jnp.concatenate(
        [dot(order, events[u : u + tokens, :]).astype(BF16) for u in range(0, seg_rows, tokens)], 0
    )
    start = pl.ds(pl.multiple_of(chan * width, width), width)
    for c in range(2):
        out[c] = dot(rows, w[c, start, :])


def scan_kernel(tokens, peers, chunk, *refs):
    events = refs[:peers]
    weights = refs[peers : peers + 2]
    parts = refs[peers + 2 : peers + 4]
    dec, runs, *earlier, state, ends, drive = refs[peers + 4 :]
    chan, grp = lax.axis_index("chan"), lax.axis_index("grp")
    width = events[0].shape[1]
    steps = tokens // SEGS
    base = chunk * tokens
    order = order_matrix(tokens)
    rows = [dot(order, ev[...]).astype(BF16) for ev in events]
    for h in range(2):
        place = grp if h == 0 else 1 - grp
        for c in range(2):
            total = parts[h][c, base : base + tokens, :]
            for n in range(peers):
                start = pl.multiple_of((chan ^ (n + 1)) * width, width)
                total = total + dot(rows[n], weights[h][c, pl.ds(start, width), :])
            drive[c] = dec[2, h, base : base + tokens, :] * total

        def at(s):
            sl = slice(base + s * SEGS, base + (s + 1) * SEGS)
            to = slice(s * SEGS, (s + 1) * SEGS)
            return dec[0, h, sl, :], dec[1, h, sl, :], drive[0, to, :], drive[1, to, :]

        _, _, sr, si = at(0)
        for s in range(1, steps):
            dr, di, vr, vi = at(s)
            xr, xi = cmul(dr, di, sr, si)
            sr, si = xr + vr, xi + vi
        ar = runs[0, h, chunk * SEGS : (chunk + 1) * SEGS, :]
        ai = runs[1, h, chunk * SEGS : (chunk + 1) * SEGS, :]
        if earlier:
            cr, ci = earlier[0][place], earlier[0][2 + place]
        else:
            cr, ci = jnp.zeros_like(sr[:1]), jnp.zeros_like(si[:1])
        sr, si, er, ei = run_starts(ar, ai, sr, si, cr, ci)
        ends[place] = er
        ends[2 + place] = ei
        for s in range(steps):
            dr, di, vr, vi = at(s)
            xr, xi = cmul(dr, di, sr, si)
            sr, si = xr + vr, xi + vi
            to = slice(s * SEGS, (s + 1) * SEGS)
            state[0, h, to, :] = sr
            state[1, h, to, :] = si


def carry_in(tokens, carry, states, cum, out):
    grp = lax.axis_index("grp")
    order = order_matrix(tokens)
    for h in range(2):
        place = grp if h == 0 else 1 - grp
        cr, ci = carry[place], carry[2 + place]
        for u, state in enumerate(states):
            sl = slice(u * tokens, (u + 1) * tokens)
            xr, xi = cmul(cum[0, h, sl, :], cum[1, h, sl, :], cr, ci)
            for c, value in ((0, state[0, h] + xr), (1, state[1, h] + xi)):
                moved = lax.dot_general(
                    order, value.astype(BF16), (((0,), (0,)), ((), ())), preferred_element_type=F32
                )
                out[c, h, sl, :] = moved.astype(BF16)


def mix(d, states, w_own, w_oth, *outs):
    at = (lax.axis_index("chan") * lax.axis_size("grp") + lax.axis_index("grp")) ^ d
    count, width = outs[0].shape
    cols = pl.ds(pl.multiple_of(at * width, width), width)
    total = None
    for h, w in enumerate((w_own, w_oth)):
        for c in range(2):
            term = dot(states[c, h], w[c, :, cols])
            total = term if total is None else total + term
    for i, out in enumerate(outs):
        out[...] = total[i * count : (i + 1) * count].astype(out.dtype)


def first_kernel(tokens, d, carry, *refs):
    *states, cum, w_own, w_oth, rounded, out = refs
    carry_in(tokens, carry, states, cum, rounded)
    mix(d, rounded, w_own, w_oth, out)


def far_kernel(far, states, w_own, w_oth, *outs):
    for d, out in zip(far, outs):
        mix(d, states, w_own, w_oth, out)


def near_kernel(states, w_own, w_oth, same, *cross):
    mix(1, states, w_own, w_oth, *cross)
    mix(0, states, w_own, w_oth, same)


def hold_kernel(source, target, sem):
    copy = pltpu.make_async_copy(source, target, sem)
    copy.start()
    copy.wait()


def finish(user, lengths, sums, events, gain, out, held, sems):
    seg_rows = events.shape[1]
    chunks, tokens, _ = held.shape
    first = lax.axis_index("ctx") * seg_rows
    copies = []
    for i in range(chunks):
        rows = slice(i * tokens, (i + 1) * tokens)
        total = gain[...] * events[user, rows, :].astype(F32)
        for parts in sums:
            part = parts[i][...] if len(parts) == chunks else parts[0][rows, :]
            total = total + part.astype(F32)
        result = jax.nn.gelu(total)
        position = first + i * tokens + lax.broadcasted_iota(jnp.int32, result.shape, 0)
        held[i] = jnp.where(position < lengths[user], result, 0.0).astype(BF16)
        copies.append(pltpu.make_async_copy(held.at[i], out.at[user, rows, :], sems.at[i]))
        copies[-1].start()
    for copy in copies:
        copy.wait()


def same_kernel(lengths, events, gain, *refs):
    sums, room = refs[:-3], refs[-3:]
    finish(lax.axis_index("grp"), lengths, [(r,) for r in sums], events, gain, *room)


def final_kernel(chunks, lengths, events, gain, done, *refs):
    cross, sums, room = refs[:chunks], refs[chunks:-3], refs[-3:]
    sums = [cross] + [(r,) for r in sums]
    finish(1 - lax.axis_index("grp"), lengths, sums, events, gain, *room)


def call(body, name, args, out_shape, scratch=(), flops=0, bytes_=0, in_specs=None, out_specs=None, aliases=None):
    single = not isinstance(out_shape, tuple)
    return pl.pallas_call(
        body,
        name=name,
        out_shape=out_shape,
        in_specs=in_specs or [HERE] * len(args),
        out_specs=out_specs or (HERE if single else (HERE,) * len(out_shape)),
        scratch_shapes=list(scratch),
        input_output_aliases=aliases or {},
        compiler_params=pltpu.CompilerParams(vmem_limit_bytes=VMEM),
        cost_estimate=pl.CostEstimate(flops=flops, bytes_accessed=bytes_, transcendentals=0),
    )(*args)


def shape(dims, kind):
    return jax.ShapeDtypeStruct(dims, kind)


def join(first, second):
    ar, ai, br, bi = first[0][:2], first[0][2:], second[0][:2], second[0][2:]
    er, ei, fr, fi = first[1][:2], first[1][2:], second[1][:2], second[1][2:]
    pr, pi = cmul(br, bi, ar, ai)
    xr, xi = cmul(br, bi, er, ei)
    return jnp.concatenate([pr, pi]), jnp.concatenate([xr + fr, xi + fi])


def local(
    events, gap_bins, lengths, gap_table, decay_rate, frequency, in_proj, out_proj, skip_gain
):
    users, seg_rows, width = events.shape
    model_width = in_proj.shape[0]
    q = decay_rate.shape[0]
    grps, chans, ctxs = (lax.axis_size(a) for a in ("grp", "chan", "ctx"))
    assert grps == 2 and users == 2
    chunks = 2
    tokens, rows = seg_rows // chunks, seg_rows
    devices = chans * grps
    part_width = model_width // devices
    grp = lax.axis_index("grp")

    def swap(array, axes, size, k):
        return lax.ppermute(array, axes, [(i, i ^ k) for i in range(size)])

    own_rows = lax.dynamic_slice_in_dim(events, grp, 1, 0)[0]
    own_events = lax.dynamic_slice_in_dim(events, grp * part_width, part_width, 2)
    own_rows, own_events = lax.optimization_barrier((own_rows, own_events))
    peer_rows = [
        [swap(own_rows[u : u + tokens], "chan", chans, k) for k in range(1, chans)]
        for u in range(0, rows, tokens)
    ]

    groups = lax.axis_size("groups")
    by = 3 if groups == 2 else 1
    rates_oth = swap(jnp.stack([decay_rate, frequency]), ("groups", "grp"), groups * grps, by)
    stored = Layout((0, 1, 2))
    raw_oth = swap(with_layout_constraint(in_proj, stored), "grp", grps, 1)
    raw_oth = with_layout_constraint(raw_oth, stored)
    o_oth = swap(out_proj, "grp", grps, 1)
    w_own = jnp.transpose(in_proj, (1, 0, 2))
    w_oth = jnp.transpose(raw_oth, (1, 0, 2))

    parts = [
        call(
            functools.partial(own_kernel, tokens),
            "own_drive_%d" % h,
            (own_rows, w),
            shape((2, rows, q), F32),
            flops=2 * rows * width * 2 * q,
            bytes_=2 * width * q * 2 + 2 * rows * q * 4,
        )
        for h, w in enumerate((w_own, w_oth))
    ]
    rates_oth, peer_rows[0], _ = lax.optimization_barrier((rates_oth, peer_rows[0], parts[1]))

    def tables(decay, turn):
        scaled = gap_table[:, None] * decay
        turned = gap_table[:, None] * turn
        magnitude = jnp.exp(-scaled)
        return (
            magnitude * jnp.cos(turned),
            magnitude * jnp.sin(turned),
            jnp.sqrt(-jnp.expm1(-2.0 * scaled)),
        )

    rounds = ctxs.bit_length() - 1
    dec, prod, runs, starts, later = call(
        functools.partial(decay_kernel, tokens),
        "decays",
        (gap_bins, *tables(decay_rate, frequency), *tables(rates_oth[0], rates_oth[1])),
        (
            shape((3, 2, rows, q), F32),
            shape((4, 1, q), F32),
            shape((2, 2, chunks * SEGS, q), F32),
            shape((2, 2, chunks * SEGS, q), F32),
            shape((rounds, 1, q), jnp.int32),
        ),
        flops=2 * rows * q * 2 * 9 * gap_table.shape[0],
        bytes_=5 * 2 * rows * q * 4,
    )

    peers = chans - 1
    states, ends = [], None
    for u in range(chunks):
        state, ends = call(
            functools.partial(scan_kernel, tokens, peers, u),
            "drive_scan_%d" % u,
            (*peer_rows[u], w_own, w_oth, *parts, dec, runs) + ((ends,) if u else ()),
            (shape((2, 2, tokens, q), F32), shape((4, 1, q), F32)),
            scratch=[pltpu.VMEM((2, tokens, q), F32)],
            flops=2 * tokens * width * 4 * q * peers,
            bytes_=4 * width * q * 2 * peers + 4 * tokens * q * 12,
        )
        states.append(state)
    starts, _ = lax.optimization_barrier((starts, ends))
    cum = call(
        functools.partial(product_kernel, tokens),
        "products",
        (dec, starts),
        shape((2, 2, rows, q), F32),
        bytes_=4 * 2 * rows * q * 4,
    )
    o_oth = call(
        hold_kernel,
        "hold",
        (o_oth,),
        shape(o_oth.shape, BF16),
        scratch=[pltpu.SemaphoreType.DMA(())],
        in_specs=[pl.BlockSpec(memory_space=pl.ANY)],
        bytes_=4 * o_oth.size,
    )

    group = (prod, ends)
    before = (jnp.concatenate([jnp.ones_like(prod[:2]), jnp.zeros_like(prod[2:])]), jnp.zeros_like(ends))

    def send(k):
        got = swap(jnp.concatenate(group), "ctx", ctxs, k)
        return got[:4], got[4:]

    def choose(second, a, b):
        return tuple(jnp.where(second, x, y) for x, y in zip(a, b))

    for k in range(rounds):
        bit = later[k] > 0
        near = send(1 << k)
        if k == 0:
            near, o_oth = lax.optimization_barrier((near, o_oth))
        before = choose(bit, join(near, before), before)
        group = choose(bit, join(near, group), join(group, near))
    carry = before[1]

    far = list(range(2, devices))
    rounded, piece = call(
        functools.partial(first_kernel, tokens, far[0]),
        "carry_far",
        (carry, *states, cum, out_proj, o_oth),
        (shape((2, 2, rows, q), BF16), shape((rows, part_width), BF16)),
        flops=2 * rows * part_width * 4 * q,
        bytes_=4 * q * part_width * 2 + 6 * rows * q * 4,
    )
    pieces = call(
        functools.partial(far_kernel, far[1:]),
        "far",
        (rounded, out_proj, o_oth),
        (shape((rows, part_width), BF16),) * len(far[1:]),
        flops=2 * rows * part_width * 4 * q * len(far[1:]),
        bytes_=4 * q * part_width * 2 + 6 * rows * q * 4,
    )
    received = {d: swap(p, ("chan", "grp"), devices, d) for d, p in zip(far, (piece, *pieces))}
    received[0], *cross = call(
        near_kernel,
        "near",
        (rounded, out_proj, o_oth),
        (shape((rows, part_width), F32),) + (shape((tokens, part_width), BF16),) * chunks,
        flops=2 * rows * part_width * 8 * q,
        bytes_=8 * q * part_width * 2 + 4 * rows * q * 2,
    )
    cross = [swap(c, ("chan", "grp"), devices, 1) for c in cross]

    common = (lengths, own_events, skip_gain[None])
    kinds = [pl.BlockSpec(memory_space=pltpu.SMEM), HERE, HERE]
    evens = [received[d] for d in range(0, devices, 2)]
    odds = [received[d] for d in range(3, devices, 2)]
    whole = shape((users, seg_rows, part_width), BF16)
    room = [
        pltpu.VMEM((chunks, tokens, part_width), BF16),
        pltpu.SemaphoreType.DMA((chunks,)),
    ]
    anywhere = pl.BlockSpec(memory_space=pl.ANY)
    done = call(
        same_kernel,
        "same",
        (*common, *evens),
        whole,
        scratch=room,
        in_specs=kinds + [HERE] * len(evens),
        out_specs=anywhere,
        bytes_=rows * part_width * 8,
    )
    return call(
        functools.partial(final_kernel, chunks),
        "final",
        (*common, done, *cross, *odds),
        whole,
        scratch=room,
        in_specs=kinds + [anywhere] + [HERE] * (chunks + len(odds)),
        out_specs=anywhere,
        aliases={3: 0},
        bytes_=rows * part_width * 8,
    )


def solution(mesh):
    return jax.shard_map(
        local,
        mesh=mesh,
        in_specs=(
            P("groups", "ctx", "chan"),
            P("groups", "ctx"),
            P("groups"),
            P(),
            P(("chan", "grp")),
            P(("chan", "grp")),
            P(None, None, ("chan", "grp")),
            P(None, ("chan", "grp"), None),
            P(("chan", "grp")),
        ),
        out_specs=P("groups", "ctx", ("chan", "grp")),
        check_vma=False,
    )
```

time: 45.2 us -> 42.9 us (0.949)
  waiting for transfers between devices: 10.3 us -> 7.88 us
  local copies, waits for them, and re-layouts: 5.87 us -> 6.6 us
    unnamed x12 -> x19, local copies, waits for them, and re-layouts: 0.03 us -> 3.62 us
    optimization_barrier x1 -> x0, local copies, waits for them, and re-layouts: 2.87 us -> none  [local(): lax.optimization_barrier((in_proj, decay_oth, freq_oth))]
    ppermute x13 -> x11, waiting for transfers between devices: 10.3 us -> 7.88 us  [swap(): return lax.ppermute(array, axes, [(i, i ^ k) for i in range(size)])]
    another operation x0 -> x1, other arithmetic: none -> 0.71 us  [local(): jnp.stack([decay_rate, frequency])]
    mul x1, other arithmetic: 1.88 us -> 1.17 us  [tables(): magnitude * jnp.sin(turned)]
    ppermute x13 -> x11, starting transfers between devices: 12.6 us -> 12.2 us  [swap(): return lax.ppermute(array, axes, [(i, i ^ k) for i in range(size)])]
    pallas_call x10 -> x12, Pallas kernels: 13.6 us -> 13.6 us  [call(): pl.pallas_call(body, name=name, out_shape=out_shape, in_specs=in_specs or...]
  transfers between devices with their start and end apart: 13 -> 11, of which waited for: 7 -> 3; matrix products, arithmetic and copies ran while one was open for 18% -> 18% of each run, Pallas kernels for 23% -> 26%
where the time goes in v4:
time: 42.9 us; the launch traced here: 42.7 us
  Pallas kernels  13.6 us (32%)
  starting transfers between devices  12.2 us (28%)
  waiting for transfers between devices  7.88 us (18%)
  local copies, waits for them, and re-layouts  6.6 us (15%)
  other arithmetic  2.07 us (5%)
    pallas_call x12, Pallas kernels, call(): pl.pallas_call(body, name=name, out_shape=out_shape, in_specs=in_specs or...  13.6 us
    ppermute x11, starting transfers between devices, swap(): return lax.ppermute(array, axes, [(i, i ^ k) for i in range(size)])  12.2 us
    ppermute x11, waiting for transfers between devices, swap(): return lax.ppermute(array, axes, [(i, i ^ k) for i in range(size)])  7.88 us
    unnamed x19, local copies, waits for them, and re-layouts  3.62 us
    another operation x1, local copies, waits for them, and re-layouts, local(): raw_oth = with_layout_constraint(raw_oth, stored)  2.86 us
    mul x1, other arithmetic, tables(): magnitude * jnp.sin(turned)  1.17 us
  transfers between devices with their start and end apart: 11, of which 3 were waited for; matrix products, arithmetic and copies ran while one was open for 18% of the time, Pallas kernels for 26%

profile of v4, /device:TPU:1, one launch (start us, length us, event | category | flops | bytes accessed | tf_op | source)
XLA Modules:
  0.0 42.7 jit_solution(2682022355018354008)
XLA Ops:
  0.0 0.1 collective-permute-start.2
  0.1 0.5 %collective-permute-start.5 = (bf16[2,512,2048]{2,1,0:T(8,128)(2,1)}, bf16[2,512,2048]{2,1,0:T(8,128)(2,1)}, u32[]{:S(2)}, u32[]{:S(2)}) collective-permute-start(bf16[2,512,2048]{2,1,0:T(8,128)(2,1)} %w_own.3), channel_id=1, source_target_pairs={{0,1},{1,0},{2,3},{3,2},{4,5},{5,4},{6,7},{7,6},{8,9},{9,8},{10,11... | collective-permute-start | bytes 12582920 | tf_op jit(solution)/shard_map/ppermute | solution.py:300
  0.5 0.7 %copy-done = bf16[2,256,1024]{2,1,0:T(8,128)(2,1)S(1)} copy-done((bf16[2,256,1024]{2,1,0:T(8,128)(2,1)S(1)}, bf16[2,256,1024]{2,1,0:T(8,128)(2,1)}, u32[]{:S(2)}) %copy-start) | copy-done | bytes 1048600
  1.4 2.1 %collective-permute-start.1 = (bf16[128,1024]{1,0:T(8,128)(2,1)S(1)}, bf16[128,1024]{1,0:T(8,128)(2,1)S(1)}, u32[]{:S(2)}, u32[]{:S(2)}) collective-permute-start(bf16[128,1024]{1,0:T(8,128)(2,1)S(1)} %get-tuple-element.52), channel_id=1, source_target_pairs={{0,2},{2,0},{1,3},{3,1},{4,6},{6,4},{5,7},{7,5},{8,10},{10,8},{9,1... | collective-permute-start | bytes 786440 | tf_op jit(solution)/shard_map/ppermute | solution.py:300
  3.5 0.7 %pad_maximum_fusion.2 = f32[2,512]{1,0:T(2,128)S(1)} fusion(f32[1,512]{1,0:T(1,128)} %bitcast.21, f32[1,512]{1,0:T(1,128)} %bitcast.22), kind=kLoop, calls=%fused_computation.33 | loop fusion | flops 1024 | bytes 8192 | tf_op jit(solution)/shard_map/stack | solution.py:312
  4.2 2.1 %collective-permute-start = (f32[2,512]{1,0:T(2,128)S(1)}, f32[2,512]{1,0:T(2,128)S(1)}, u32[]{:S(2)}, u32[]{:S(2)}) collective-permute-start(f32[2,512]{1,0:T(2,128)S(1)} %pad_maximum_fusion.2), channel_id=1, source_target_pairs={{0,17},{1,16},{16,1},{17,0},{2,19},{3,18},{18,3},{19,2},{4,21},{5,... | collective-permute-start | bytes 12296 | tf_op jit(solution)/shard_map/ppermute | solution.py:300
  6.3 0.3 collective-permute-start.3
  6.6 2.9 %copy.15 = bf16[2048,2,512]{2,0,1:T(8,128)(2,1)S(1)} copy(bf16[2048,2,512]{2,1,0:T(2,128)(2,1)} %param.15) | data formatting | bytes 8388608 | tf_op args[6]
  9.4 0.9 %own_drive_0.1.refs_3_ = f32[2,256,512]{2,1,0:T(8,128)S(1)} custom-call(bf16[256,1024]{1,0:T(8,128)(2,1)S(1)} %dynamic-slice_bitcast_fusion.events, bf16[2,2048,512]{2,1,0:T(8,128)(2,1)S(1)} %bitcast.13), custom_call_target="tpu_custom_call" | custom-call | flops 536870912 | bytes 3145728 | tf_op jit(solution)/shard_map/own_drive_0/pallas_call | solution.py:260
  10.3 2.9 %copy.16 = bf16[2048,2,512]{2,0,1:T(8,128)(2,1)S(1)} copy(bf16[2048,2,512]{2,1,0:T(2,128)(2,1)} %collective-permute-done.2) | data formatting | bytes 8388608 | tf_op jit(solution)/shard_map/layout_constraint | solution.py:315
  13.2 0.0 copy-start.5
  13.2 0.9 %own_drive_1.1.refs_4_ = f32[2,256,512]{2,1,0:T(8,128)S(1)} custom-call(bf16[256,1024]{1,0:T(8,128)(2,1)S(1)} %dynamic-slice_bitcast_fusion.events, bf16[2,2048,512]{2,1,0:T(8,128)(2,1)S(1)} %bitcast.16), custom_call_target="tpu_custom_call" | custom-call | flops 536870912 | bytes 3145728 | tf_op jit(solution)/shard_map/own_drive_1/pallas_call | solution.py:260
  14.2 1.2 %fusion.7 = (f32[64,512]{1,0:T(8,128)S(1)}, f32[64,512]{1,0:T(8,128)S(1)}, f32[64,512]{1,0:T(8,128)S(1)}, f32[64,512]{1,0:T(8,128)S(1)}, f32[64,512]{1,0:T(8,128)S(1)}, /*index=5*/f32[64,512]{1,0:T(8,128)S(1)}) fusion(f32[512]{0:T(512)S(1)} %bitcast.24, f32[512]{0:T(512)S(1)} %bitcast.23, f32[64]{0:T(128)S(1)} %copy-done.8, f32[512]{0:T(512)S(1)} %copy-done.6, ...), kind=kLoop, calls=%fused_computation.18 | loop fusion | flops 458752 | bytes 794880 | tf_op jit(solution)/shard_map/mul | solution.py:339
  15.3 1.0 %decays.1 = (f32[3,2,256,512]{3,2,1,0:T(8,128)S(1)}, f32[4,1,512]{2,1,0:T(1,128)S(1)}, f32[2,2,16,512]{3,2,1,0:T(8,128)S(1)}, f32[2,2,16,512]{3,2,1,0:T(8,128)S(1)}, s32[2,1,512]{2,1,0:T(1,128)S(1)}) custom-call(s32[2,256]{1,0:T(2,128)S(1)} %copy-done.4, f32[64,512]{1,0:T(8,128)S(1)} %get-tuple-element.79.refs_0_, f32[64,512]{1,0:T(8,128)S(1)} %get-tuple-element.80.refs_1_, ...), custom_call_target="tpu_custom_call" | custom-call | flops 301989888 | bytes 5242880 | tf_op jit(solution)/shard_map/decays/pallas_call | solution.py:260
  16.3 1.2 %drive_scan_0.1 = (f32[2,2,128,512]{3,2,1,0:T(8,128)S(1)}, f32[4,1,512]{2,1,0:T(1,128)S(1)}) custom-call(bf16[128,1024]{1,0:T(8,128)(2,1)S(1)} %collective-permute-done.1.refs_0_, bf16[2,2048,512]{2,1,0:T(8,128)(2,1)S(1)} %bitcast.14, bf16[2,2048,512]{2,1,0:T(8,128)(2,1)S(1)} %bitcast.17, f32[2,256,512]{2,1,0:T(8,128)S(1)} %own_drive_0.1.refs_3_, ...), custom_call_target="tpu_custom_call" | custom-call | flops 536870912 | bytes 7340032 | tf_op jit(solution)/shard_map/drive_scan_0/pallas_call | solution.py:260
  17.5 1.2 %drive_scan_1.1 = (f32[2,2,128,512]{3,2,1,0:T(8,128)S(1)}, f32[4,1,512]{2,1,0:T(1,128)S(1)}) custom-call(bf16[128,1024]{1,0:T(8,128)(2,1)S(1)} %collective-permute-done.3.refs_0_, bf16[2,2048,512]{2,1,0:T(8,128)(2,1)S(1)} %bitcast.15, bf16[2,2048,512]{2,1,0:T(8,128)(2,1)S(1)} %bitcast.18, f32[2,256,512]{2,1,0:T(8,128)S(1)} %own_drive_0.1.refs_3_, ...), custom_call_target="tpu_custom_call" | custom-call | flops 536870912 | bytes 7340032 | tf_op jit(solution)/shard_map/drive_scan_1/pallas_call | solution.py:260
  18.7 1.4 %collective-permute-start.4 = (f32[8,1,512]{2,1,0:T(1,128)S(1)}, f32[8,1,512]{2,1,0:T(1,128)S(1)}, u32[]{:S(2)}, u32[]{:S(2)}) collective-permute-start(f32[8,1,512]{2,1,0:T(1,128)S(1)} %pad_maximum_fusion), channel_id=1, source_target_pairs={{0,4},{4,0},{8,12},{12,8},{1,5},{5,1},{9,13},{13,9},{2,6},{6,2},{1... | collective-permute-start | bytes 49160 | tf_op jit(solution)/shard_map/ppermute | solution.py:300
  20.1 2.2 %hold.1.refs_4_.w_oth = bf16[2,512,2048]{2,1,0:T(8,128)(2,1)S(1)} custom-call(bf16[2,512,2048]{2,1,0:T(8,128)(2,1)} %collective-permute-done.5.source), custom_call_target="tpu_custom_call" | custom-call | bytes 8388608 | tf_op jit(solution)/shard_map/hold/pallas_call | solution.py:260
  22.5 2.4 %collective-permute-start.6 = (f32[8,1,512]{2,1,0:T(1,128)S(1)}, f32[8,1,512]{2,1,0:T(1,128)S(1)}, u32[]{:S(2)}, u32[]{:S(2)}) collective-permute-start(f32[8,1,512]{2,1,0:T(1,128)S(1)} %pad_maximum_fusion.1), channel_id=1, source_target_pairs={{0,8},{4,12},{8,0},{12,4},{1,9},{5,13},{9,1},{13,5},{2,10},{6,14},... | collective-permute-start | bytes 49160 | tf_op jit(solution)/shard_map/ppermute | solution.py:300
  24.9 0.2 products.1.refs_2_
  25.1 1.1 %collective-permute-done.6 = f32[8,1,512]{2,1,0:T(1,128)S(1)} collective-permute-done((f32[8,1,512]{2,1,0:T(1,128)S(1)}, f32[8,1,512]{2,1,0:T(1,128)S(1)}, u32[]{:S(2)}, u32[]{:S(2)}) %collective-permute-start.6) | collective-permute-done | bytes 16416 | tf_op jit(solution)/shard_map/ppermute | solution.py:300
  26.3 1.1 %carry_far.1 = (bf16[2,2,256,512]{3,2,1,0:T(8,128)(2,1)S(1)}, bf16[256,512]{1,0:T(8,128)(2,1)S(1)}) custom-call(f32[4,1,512]{2,1,0:T(1,128)S(1)} %broadcast_select_fusion.3.carry, f32[2,2,128,512]{3,2,1,0:T(8,128)S(1)} %get-tuple-element.39.refs_0_, f32[2,2,128,512]{3,2,1,0:T(8,128)S(1)} %get-tuple-element.40.refs_1_, ...), custom_call_target="tpu_custom_call" | custom-call | flops 536870912 | bytes 5242880 | tf_op jit(solution)/shard_map/carry_far/pallas_call | solution.py:260
  27.4 1.3 %collective-permute-start.7 = (bf16[256,512]{1,0:T(8,128)(2,1)S(1)}, bf16[256,512]{1,0:T(8,128)(2,1)S(1)}, u32[]{:S(2)}, u32[]{:S(2)}) collective-permute-start(bf16[256,512]{1,0:T(8,128)(2,1)S(1)} %get-tuple-element.46), channel_id=1, source_target_pairs={{0,2},{1,3},{2,0},{3,1},{4,6},{5,7},{6,4},{7,5},{8,10},{9,11},{10,... | collective-permute-start | bytes 786440 | tf_op jit(solution)/shard_map/ppermute | solution.py:300
  28.7 0.7 %far.1 = bf16[256,512]{1,0:T(8,128)(2,1)S(1)} custom-call(bf16[2,2,256,512]{3,2,1,0:T(8,128)(2,1)S(1)} %get-tuple-element.44.states, bf16[2,512,2048]{2,1,0:T(8,128)(2,1)S(1)} %copy-done.1, bf16[2,512,2048]{2,1,0:T(8,128)(2,1)S(1)} %hold.1.refs_4_.w_oth), custom_call_target="tpu_custom_call" | custom-call | flops 536870912 | bytes 5242880 | tf_op jit(solution)/shard_map/far/pallas_call | solution.py:260
  29.4 1.6 %collective-permute-start.10 = (bf16[256,512]{1,0:T(8,128)(2,1)S(1)}, bf16[256,512]{1,0:T(8,128)(2,1)S(1)}, u32[]{:S(2)}, u32[]{:S(2)}) collective-permute-start(bf16[256,512]{1,0:T(8,128)(2,1)S(1)} %far.1), channel_id=1, source_target_pairs={{0,3},{1,2},{2,1},{3,0},{4,7},{5,6},{6,5},{7,4},{8,11},{9,10},{10,... | collective-permute-start | bytes 786440 | tf_op jit(solution)/shard_map/ppermute | solution.py:300
  31.1 1.2 %near.1 = (f32[256,512]{1,0:T(8,128)S(1)}, bf16[128,512]{1,0:T(8,128)(2,1)S(1)}, bf16[128,512]{1,0:T(8,128)(2,1)S(1)}) custom-call(bf16[2,2,256,512]{3,2,1,0:T(8,128)(2,1)S(1)} %get-tuple-element.44.states, bf16[2,512,2048]{2,1,0:T(8,128)(2,1)S(1)} %copy-done.1, bf16[2,512,2048]{2,1,0:T(8,128)(2,1)S(1)} %hold.1.refs_4_.w_oth), custom_call_target="tpu_custom_call" | custom-call | flops 1073741824 | bytes 5242880 | tf_op jit(solution)/shard_map/near/pallas_call | solution.py:260
  32.3 0.1 collective-permute-start.8
  32.4 0.5 %collective-permute-start.9 = (bf16[128,512]{1,0:T(8,128)(2,1)S(1)}, bf16[128,512]{1,0:T(8,128)(2,1)S(1)}, u32[]{:S(2)}, u32[]{:S(2)}) collective-permute-start(bf16[128,512]{1,0:T(8,128)(2,1)S(1)} %get-tuple-element.48), channel_id=1, source_target_pairs={{0,1},{1,0},{2,3},{3,2},{4,5},{5,4},{6,7},{7,6},{8,9},{9,8},{10,11... | collective-permute-start | bytes 393224 | tf_op jit(solution)/shard_map/ppermute | solution.py:300
  32.9 1.3 %collective-permute-done.7.refs_1_ = bf16[256,512]{1,0:T(8,128)(2,1)S(1)} collective-permute-done((bf16[256,512]{1,0:T(8,128)(2,1)S(1)}, bf16[256,512]{1,0:T(8,128)(2,1)S(1)}, u32[]{:S(2)}, u32[]{:S(2)}) %collective-permute-start.7) | collective-permute-done | bytes 262176 | tf_op jit(solution)/shard_map/ppermute | solution.py:300
  34.2 1.5 %same.1.done = bf16[2,256,512]{2,1,0:T(8,128)(2,1)} custom-call(s32[2]{0:T(128)S(1)} %copy-done.3, bf16[2,256,512]{2,1,0:T(8,128)(2,1)S(1)} %constant_dynamic-slice_fusion.events, f32[1,512]{1,0:T(1,128)S(1)} %bitcast.19, f32[256,512]{1,0:T(8,128)S(1)} %get-tuple-element.45.refs_0_, bf16[256,512]{1,0:T(8,128)(2,1)S(1)} %collective-permute-done.7.refs_1_), custom_call_target="tpu_custom_call" | custom-call | bytes 1048576 | tf_op jit(solution)/shard_map/same/pallas_call | solution.py:260
  35.7 5.4 %collective-permute-done.10.refs_2_ = bf16[256,512]{1,0:T(8,128)(2,1)S(1)} collective-permute-done((bf16[256,512]{1,0:T(8,128)(2,1)S(1)}, bf16[256,512]{1,0:T(8,128)(2,1)S(1)}, u32[]{:S(2)}, u32[]{:S(2)}) %collective-permute-start.10) | collective-permute-done | bytes 262176 | tf_op jit(solution)/shard_map/ppermute | solution.py:300
  41.1 1.5 %final.1 = bf16[2,256,512]{2,1,0:T(8,128)(2,1)} custom-call(s32[2]{0:T(128)S(1)} %copy-done.3, bf16[2,256,512]{2,1,0:T(8,128)(2,1)S(1)} %constant_dynamic-slice_fusion.events, f32[1,512]{1,0:T(1,128)S(1)} %bitcast.20, bf16[2,256,512]{2,1,0:T(8,128)(2,1)} %same.1.done, ...), custom_call_target="tpu_custom_call", output_to_operand_aliasing={{}: (3, {})} | custom-call | bytes 1048576 | tf_op jit(solution)/shard_map/final/pallas_call | solution.py:260
  (38 shorter events, 0.4 us)
Async XLA Ops:
  0.0 1.2 %copy-start = (bf16[2,256,1024]{2,1,0:T(8,128)(2,1)S(1)}, bf16[2,256,1024]{2,1,0:T(8,128)(2,1)}, u32[]{:S(2)}) copy-start(bf16[2,256,1024]{2,1,0:T(8,128)(2,1)} %param.9) | copy-start | bytes 3145732
  0.0 10.3 %collective-permute-start.2 = (bf16[2048,2,512]{2,1,0:T(2,128)(2,1)}, bf16[2048,2,512]{2,1,0:T(2,128)(2,1)}, u32[]{:S(2)}, u32[]{:S(2)}) collective-permute-start(bf16[2048,2,512]{2,1,0:T(2,128)(2,1)} %param.15), channel_id=1, source_target_pairs={{0,1},{1,0},{2,3},{3,2},{4,5},{5,4},{6,7},{7,6},{8,9},{9,8},{10,11... | collective-permute-start | bytes 12582920 | tf_op jit(solution)/shard_map/ppermute | solution.py:300
  0.1 20.1 %collective-permute-start.5 = (bf16[2,512,2048]{2,1,0:T(8,128)(2,1)}, bf16[2,512,2048]{2,1,0:T(8,128)(2,1)}, u32[]{:S(2)}, u32[]{:S(2)}) collective-permute-start(bf16[2,512,2048]{2,1,0:T(8,128)(2,1)} %w_own.3), channel_id=1, source_target_pairs={{0,1},{1,0},{2,3},{3,2},{4,5},{5,4},{6,7},{7,6},{8,9},{9,8},{10,11... | collective-permute-start | bytes 12582920 | tf_op jit(solution)/shard_map/ppermute | solution.py:300
  1.4 12.7 %collective-permute-start.1 = (bf16[128,1024]{1,0:T(8,128)(2,1)S(1)}, bf16[128,1024]{1,0:T(8,128)(2,1)S(1)}, u32[]{:S(2)}, u32[]{:S(2)}) collective-permute-start(bf16[128,1024]{1,0:T(8,128)(2,1)S(1)} %get-tuple-element.52), channel_id=1, source_target_pairs={{0,2},{2,0},{1,3},{3,1},{4,6},{6,4},{5,7},{7,5},{8,10},{10,8},{9,1... | collective-permute-start | bytes 786440 | tf_op jit(solution)/shard_map/ppermute | solution.py:300
  4.2 9.9 %collective-permute-start = (f32[2,512]{1,0:T(2,128)S(1)}, f32[2,512]{1,0:T(2,128)S(1)}, u32[]{:S(2)}, u32[]{:S(2)}) collective-permute-start(f32[2,512]{1,0:T(2,128)S(1)} %pad_maximum_fusion.2), channel_id=1, source_target_pairs={{0,17},{1,16},{16,1},{17,0},{2,19},{3,18},{18,3},{19,2},{4,21},{5,... | collective-permute-start | bytes 12296 | tf_op jit(solution)/shard_map/ppermute | solution.py:300
  6.3 11.2 %collective-permute-start.3 = (bf16[128,1024]{1,0:T(8,128)(2,1)S(1)}, bf16[128,1024]{1,0:T(8,128)(2,1)S(1)}, u32[]{:S(2)}, u32[]{:S(2)}) collective-permute-start(bf16[128,1024]{1,0:T(8,128)(2,1)S(1)} %get-tuple-element.51), channel_id=1, source_target_pairs={{0,2},{2,0},{1,3},{3,1},{4,6},{6,4},{5,7},{7,5},{8,10},{10,8},{9,1... | collective-permute-start | bytes 786440 | tf_op jit(solution)/shard_map/ppermute | solution.py:300
  13.2 1.0 %copy-start.5 = (f32[512]{0:T(512)S(1)}, f32[512]{0:T(512)}, u32[]{:S(2)}) copy-start(f32[512]{0:T(512)} %param.14) | copy-start | bytes 6148
  13.2 1.0 %copy-start.6 = (f32[512]{0:T(512)S(1)}, f32[512]{0:T(512)}, u32[]{:S(2)}) copy-start(f32[512]{0:T(512)} %param.13) | copy-start | bytes 6148
  13.2 0.9 %copy-start.8 = (f32[64]{0:T(128)S(1)}, f32[64]{0:T(128)}, u32[]{:S(2)}) copy-start(f32[64]{0:T(128)} %param.12) | copy-start | bytes 772
  13.2 2.1 %copy-start.4 = (s32[2,256]{1,0:T(2,128)S(1)}, s32[2,256]{1,0:T(2,128)}, u32[]{:S(2)}) copy-start(s32[2,256]{1,0:T(2,128)} %bins.1) | copy-start | bytes 6148
  18.7 3.6 %collective-permute-start.4 = (f32[8,1,512]{2,1,0:T(1,128)S(1)}, f32[8,1,512]{2,1,0:T(1,128)S(1)}, u32[]{:S(2)}, u32[]{:S(2)}) collective-permute-start(f32[8,1,512]{2,1,0:T(1,128)S(1)} %pad_maximum_fusion), channel_id=1, source_target_pairs={{0,4},{4,0},{8,12},{12,8},{1,5},{5,1},{9,13},{13,9},{2,6},{6,2},{1... | collective-permute-start | bytes 49160 | tf_op jit(solution)/shard_map/ppermute | solution.py:300
  20.1 2.3 %copy-start.7 = (f32[4,1,512]{2,1,0:T(1,128)S(1)}, f32[4,1,512]{2,1,0:T(1,128)}, u32[]{:S(2)}) copy-start(f32[4,1,512]{2,1,0:T(1,128)} %constant.27.clone.1) | copy-start | bytes 24580
  22.3 4.0 %copy-start.1 = (bf16[2,512,2048]{2,1,0:T(8,128)(2,1)S(1)}, bf16[2,512,2048]{2,1,0:T(8,128)(2,1)}, u32[]{:S(2)}) copy-start(bf16[2,512,2048]{2,1,0:T(8,128)(2,1)} %w_own.3) | copy-start | bytes 12582916
  22.5 3.7 %collective-permute-start.6 = (f32[8,1,512]{2,1,0:T(1,128)S(1)}, f32[8,1,512]{2,1,0:T(1,128)S(1)}, u32[]{:S(2)}, u32[]{:S(2)}) collective-permute-start(f32[8,1,512]{2,1,0:T(1,128)S(1)} %pad_maximum_fusion.1), channel_id=1, source_target_pairs={{0,8},{4,12},{8,0},{12,4},{1,9},{5,13},{9,1},{13,5},{2,10},{6,14},... | collective-permute-start | bytes 49160 | tf_op jit(solution)/shard_map/ppermute | solution.py:300
  27.4 6.7 %collective-permute-start.7 = (bf16[256,512]{1,0:T(8,128)(2,1)S(1)}, bf16[256,512]{1,0:T(8,128)(2,1)S(1)}, u32[]{:S(2)}, u32[]{:S(2)}) collective-permute-start(bf16[256,512]{1,0:T(8,128)(2,1)S(1)} %get-tuple-element.46), channel_id=1, source_target_pairs={{0,2},{1,3},{2,0},{3,1},{4,6},{5,7},{6,4},{7,5},{8,10},{9,11},{10,... | collective-permute-start | bytes 786440 | tf_op jit(solution)/shard_map/ppermute | solution.py:300
  29.4 4.8 %copy-start.2 = (f32[512]{0:T(512)S(1)}, f32[512]{0:T(512)}, u32[]{:S(2)}) copy-start(f32[512]{0:T(512)} %param.17) | copy-start | bytes 6148
  29.4 4.7 %copy-start.3 = (s32[2]{0:T(128)S(1)}, s32[2]{0:T(128)}, u32[]{:S(2)}) copy-start(s32[2]{0:T(128)} %lengths.3) | copy-start | bytes 28
  29.4 11.7 %collective-permute-start.10 = (bf16[256,512]{1,0:T(8,128)(2,1)S(1)}, bf16[256,512]{1,0:T(8,128)(2,1)S(1)}, u32[]{:S(2)}, u32[]{:S(2)}) collective-permute-start(bf16[256,512]{1,0:T(8,128)(2,1)S(1)} %far.1), channel_id=1, source_target_pairs={{0,3},{1,2},{2,1},{3,0},{4,7},{5,6},{6,5},{7,4},{8,11},{9,10},{10,... | collective-permute-start | bytes 786440 | tf_op jit(solution)/shard_map/ppermute | solution.py:300
  32.3 3.4 %collective-permute-start.8 = (bf16[128,512]{1,0:T(8,128)(2,1)S(1)}, bf16[128,512]{1,0:T(8,128)(2,1)S(1)}, u32[]{:S(2)}, u32[]{:S(2)}) collective-permute-start(bf16[128,512]{1,0:T(8,128)(2,1)S(1)} %get-tuple-element.47), channel_id=1, source_target_pairs={{0,1},{1,0},{2,3},{3,2},{4,5},{5,4},{6,7},{7,6},{8,9},{9,8},{10,11... | collective-permute-start | bytes 393224 | tf_op jit(solution)/shard_map/ppermute | solution.py:300
  32.4 3.3 %collective-permute-start.9 = (bf16[128,512]{1,0:T(8,128)(2,1)S(1)}, bf16[128,512]{1,0:T(8,128)(2,1)S(1)}, u32[]{:S(2)}, u32[]{:S(2)}) collective-permute-start(bf16[128,512]{1,0:T(8,128)(2,1)S(1)} %get-tuple-element.48), channel_id=1, source_target_pairs={{0,1},{1,0},{2,3},{3,2},{4,5},{5,4},{6,7},{7,6},{8,9},{9,8},{10,11... | collective-permute-start | bytes 393224 | tf_op jit(solution)/shard_map/ppermute | solution.py:300

commit v5 on v4

--- a/solution.py
+++ b/solution.py
@@ -224,35 +224,69 @@
     copy.wait()
 
 
-def finish(user, lengths, sums, events, gain, out, held, sems):
-    seg_rows = events.shape[1]
-    chunks, tokens, _ = held.shape
-    first = lax.axis_index("ctx") * seg_rows
+def chunk_of(part, i, tokens):
+    return part[...] if part.shape[0] == tokens else part[i * tokens : (i + 1) * tokens, :]
+
+
+def before_gelu(user, i, tokens, sums, events, gain):
+    total = gain[...] * events[user, i * tokens : (i + 1) * tokens, :].astype(F32)
+    for parts in sums:
+        total = total + chunk_of(parts[min(i, len(parts) - 1)], i, tokens).astype(F32)
+    return total
+
+
+def valid(user, i, tokens, lengths, events, width):
+    start = lax.axis_index("ctx") * events.shape[1] + i * tokens
+    position = start + lax.broadcasted_iota(jnp.int32, (tokens, width), 0)
+    return position < lengths[user]
+
+
+def put(user, i, value, out, held, sems):
+    held[i] = value.astype(BF16)
+    tokens = value.shape[0]
+    copy = pltpu.make_async_copy(
+        held.at[i], out.at[user, i * tokens : (i + 1) * tokens, :], sems.at[i]
+    )
+    copy.start()
+    return copy
+
+
+def same_kernel(counts, lengths, events, gain, *refs):
+    refs, room = refs[:-3], refs[-3:]
+    chunks, tokens, width = room[1].shape
+    sums = [refs[sum(counts[:n]) :][:c] for n, c in enumerate(counts)]
+    user = lax.axis_index("grp")
+    copies = []
+    for i in range(chunks):
+        result = jax.nn.gelu(before_gelu(user, i, tokens, sums, events, gain))
+        keep = valid(user, i, tokens, lengths, events, width)
+        copies.append(put(user, i, jnp.where(keep, result, 0.0), *room))
+    for copy in copies:
+        copy.wait()
+
+
+def almost_kernel(counts, lengths, events, gain, *refs):
+    refs, (total, keep) = refs[:-2], refs[-2:]
+    tokens = refs[0].shape[0]
+    sums = [refs[sum(counts[:n]) :][:c] for n, c in enumerate(counts)]
+    user = 1 - lax.axis_index("grp")
+    for i in range(total.shape[0] // tokens):
+        rows = slice(i * tokens, (i + 1) * tokens)
+        total[rows, :] = before_gelu(user, i, tokens, sums, events, gain)
+        keep[rows, :] = valid(user, i, tokens, lengths, events, keep.shape[1]).astype(F32)
+
+
+def final_kernel(total, keep, last, done, *room):
+    chunks, tokens, width = room[1].shape
+    user = 1 - lax.axis_index("grp")
     copies = []
     for i in range(chunks):
         rows = slice(i * tokens, (i + 1) * tokens)
-        total = gain[...] * events[user, rows, :].astype(F32)
-        for parts in sums:
-            part = parts[i][...] if len(parts) == chunks else parts[0][rows, :]
-            total = total + part.astype(F32)
-        result = jax.nn.gelu(total)
-        position = first + i * tokens + lax.broadcasted_iota(jnp.int32, result.shape, 0)
-        held[i] = jnp.where(position < lengths[user], result, 0.0).astype(BF16)
-        copies.append(pltpu.make_async_copy(held.at[i], out.at[user, rows, :], sems.at[i]))
-        copies[-1].start()
+        result = jax.nn.gelu(total[rows, :] + last[rows, :].astype(F32))
+        kept = jnp.concatenate([keep[rows, :]] * (width // keep.shape[1]), 1)
+        copies.append(put(user, i, jnp.where(kept > 0, result, 0.0), *room))
     for copy in copies:
         copy.wait()
-
-
-def same_kernel(lengths, events, gain, *refs):
-    sums, room = refs[:-3], refs[-3:]
-    finish(lax.axis_index("grp"), lengths, [(r,) for r in sums], events, gain, *room)
-
-
-def final_kernel(chunks, lengths, events, gain, done, *refs):
-    cross, sums, room = refs[:chunks], refs[chunks:-3], refs[-3:]
-    sums = [cross] + [(r,) for r in sums]
-    finish(1 - lax.axis_index("grp"), lengths, sums, events, gain, *room)
 
 
 def call(body, name, args, out_shape, scratch=(), flops=0, bytes_=0, in_specs=None, out_specs=None, aliases=None):
@@ -436,31 +470,41 @@
 
     common = (lengths, own_events, skip_gain[None])
     kinds = [pl.BlockSpec(memory_space=pltpu.SMEM), HERE, HERE]
-    evens = [received[d] for d in range(0, devices, 2)]
-    odds = [received[d] for d in range(3, devices, 2)]
+    evens = [[received[d]] for d in range(0, devices, 2)]
+    odds = [cross] + [[received[d]] for d in range(5, devices, 2)]
     whole = shape((users, seg_rows, part_width), BF16)
     room = [
         pltpu.VMEM((chunks, tokens, part_width), BF16),
         pltpu.SemaphoreType.DMA((chunks,)),
     ]
     anywhere = pl.BlockSpec(memory_space=pl.ANY)
+    flat = [p for parts in evens for p in parts]
     done = call(
-        same_kernel,
+        functools.partial(same_kernel, [len(parts) for parts in evens]),
         "same",
-        (*common, *evens),
+        (*common, *flat),
         whole,
         scratch=room,
-        in_specs=kinds + [HERE] * len(evens),
+        in_specs=kinds + [HERE] * len(flat),
         out_specs=anywhere,
         bytes_=rows * part_width * 8,
     )
+    flat = [p for parts in odds for p in parts]
+    total, keep = call(
+        functools.partial(almost_kernel, [len(parts) for parts in odds]),
+        "almost",
+        (*common, *flat),
+        (shape((rows, part_width), F32), shape((rows, 128), F32)),
+        in_specs=kinds + [HERE] * len(flat),
+        bytes_=rows * part_width * 8,
+    )
     return call(
-        functools.partial(final_kernel, chunks),
+        final_kernel,
         "final",
-        (*common, done, *cross, *odds),
+        (total, keep, received[3], done),
         whole,
         scratch=room,
-        in_specs=kinds + [anywhere] + [HERE] * (chunks + len(odds)),
+        in_specs=[HERE] * 3 + [anywhere],
         out_specs=anywhere,
         aliases={3: 0},
         bytes_=rows * part_width * 8,

time: 42.9 us -> 42.3 us (0.986)
  waiting for transfers between devices: 7.88 us -> 7.24 us
    ppermute x11, waiting for transfers between devices: 7.88 us -> 7.24 us  [swap(): return lax.ppermute(array, axes, [(i, i ^ k) for i in range(size)])]
    pallas_call x12 -> x13, Pallas kernels: 13.6 us -> 13.6 us  [call(): pl.pallas_call(body, name=name, out_shape=out_shape, in_specs=in_specs or...]
  transfers between devices with their start and end apart: 11 -> 11, of which waited for: 3 -> 4; matrix products, arithmetic and copies ran while one was open for 18% -> 18% of each run, Pallas kernels for 26% -> 28%
where the time goes in v5:
time: 42.3 us; the launch traced here: 42 us
  Pallas kernels  13.6 us (32%)
  starting transfers between devices  12.2 us (29%)
  waiting for transfers between devices  7.24 us (17%)
  local copies, waits for them, and re-layouts  6.6 us (16%)
  other arithmetic  2.07 us (5%)
    pallas_call x13, Pallas kernels, call(): pl.pallas_call(body, name=name, out_shape=out_shape, in_specs=in_specs or...  13.6 us
    ppermute x11, starting transfers between devices, swap(): return lax.ppermute(array, axes, [(i, i ^ k) for i in range(size)])  12.2 us
    ppermute x11, waiting for transfers between devices, swap(): return lax.ppermute(array, axes, [(i, i ^ k) for i in range(size)])  7.24 us
    unnamed x19, local copies, waits for them, and re-layouts  3.62 us
    another operation x1, local copies, waits for them, and re-layouts, local(): raw_oth = with_layout_constraint(raw_oth, stored)  2.86 us
    mul x1, other arithmetic, tables(): magnitude * jnp.sin(turned)  1.17 us
  transfers between devices with their start and end apart: 11, of which 4 were waited for; matrix products, arithmetic and copies ran while one was open for 18% of the time, Pallas kernels for 28%

profile of v5, /device:TPU:1, one launch (start us, length us, event | category | flops | bytes accessed | tf_op | source)
XLA Modules:
  0.0 42.0 jit_solution(11679753795724611092)
XLA Ops:
  0.1 0.5 %collective-permute-start.5 = (bf16[2,512,2048]{2,1,0:T(8,128)(2,1)}, bf16[2,512,2048]{2,1,0:T(8,128)(2,1)}, u32[]{:S(2)}, u32[]{:S(2)}) collective-permute-start(bf16[2,512,2048]{2,1,0:T(8,128)(2,1)} %w_own.3), channel_id=1, source_target_pairs={{0,1},{1,0},{2,3},{3,2},{4,5},{5,4},{6,7},{7,6},{8,9},{9,8},{10,11... | collective-permute-start | bytes 12582920 | tf_op jit(solution)/shard_map/ppermute | solution.py:334
  0.5 0.7 %copy-done = bf16[2,256,1024]{2,1,0:T(8,128)(2,1)S(1)} copy-done((bf16[2,256,1024]{2,1,0:T(8,128)(2,1)S(1)}, bf16[2,256,1024]{2,1,0:T(8,128)(2,1)}, u32[]{:S(2)}) %copy-start) | copy-done | bytes 1048600
  1.4 2.1 %collective-permute-start.1 = (bf16[128,1024]{1,0:T(8,128)(2,1)S(1)}, bf16[128,1024]{1,0:T(8,128)(2,1)S(1)}, u32[]{:S(2)}, u32[]{:S(2)}) collective-permute-start(bf16[128,1024]{1,0:T(8,128)(2,1)S(1)} %get-tuple-element.56), channel_id=1, source_target_pairs={{0,2},{2,0},{1,3},{3,1},{4,6},{6,4},{5,7},{7,5},{8,10},{10,8},{9,1... | collective-permute-start | bytes 786440 | tf_op jit(solution)/shard_map/ppermute | solution.py:334
  3.5 0.7 %pad_maximum_fusion.2 = f32[2,512]{1,0:T(2,128)S(1)} fusion(f32[1,512]{1,0:T(1,128)} %bitcast.21, f32[1,512]{1,0:T(1,128)} %bitcast.22), kind=kLoop, calls=%fused_computation.33 | loop fusion | flops 1024 | bytes 8192 | tf_op jit(solution)/shard_map/stack | solution.py:346
  4.2 2.1 %collective-permute-start = (f32[2,512]{1,0:T(2,128)S(1)}, f32[2,512]{1,0:T(2,128)S(1)}, u32[]{:S(2)}, u32[]{:S(2)}) collective-permute-start(f32[2,512]{1,0:T(2,128)S(1)} %pad_maximum_fusion.2), channel_id=1, source_target_pairs={{0,17},{1,16},{16,1},{17,0},{2,19},{3,18},{18,3},{19,2},{4,21},{5,... | collective-permute-start | bytes 12296 | tf_op jit(solution)/shard_map/ppermute | solution.py:334
  6.3 0.3 collective-permute-start.3
  6.6 2.9 %copy.15 = bf16[2048,2,512]{2,0,1:T(8,128)(2,1)S(1)} copy(bf16[2048,2,512]{2,1,0:T(2,128)(2,1)} %param.15) | data formatting | bytes 8388608 | tf_op args[6]
  9.4 0.9 %own_drive_0.1.refs_3_ = f32[2,256,512]{2,1,0:T(8,128)S(1)} custom-call(bf16[256,1024]{1,0:T(8,128)(2,1)S(1)} %dynamic-slice_bitcast_fusion.events, bf16[2,2048,512]{2,1,0:T(8,128)(2,1)S(1)} %bitcast.13), custom_call_target="tpu_custom_call" | custom-call | flops 536870912 | bytes 3145728 | tf_op jit(solution)/shard_map/own_drive_0/pallas_call | solution.py:294
  10.3 2.9 %copy.16 = bf16[2048,2,512]{2,0,1:T(8,128)(2,1)S(1)} copy(bf16[2048,2,512]{2,1,0:T(2,128)(2,1)} %collective-permute-done.2) | data formatting | bytes 8388608 | tf_op jit(solution)/shard_map/layout_constraint | solution.py:349
  13.2 0.9 %own_drive_1.1.refs_4_ = f32[2,256,512]{2,1,0:T(8,128)S(1)} custom-call(bf16[256,1024]{1,0:T(8,128)(2,1)S(1)} %dynamic-slice_bitcast_fusion.events, bf16[2,2048,512]{2,1,0:T(8,128)(2,1)S(1)} %bitcast.16), custom_call_target="tpu_custom_call" | custom-call | flops 536870912 | bytes 3145728 | tf_op jit(solution)/shard_map/own_drive_1/pallas_call | solution.py:294
  14.2 1.2 %fusion.7 = (f32[64,512]{1,0:T(8,128)S(1)}, f32[64,512]{1,0:T(8,128)S(1)}, f32[64,512]{1,0:T(8,128)S(1)}, f32[64,512]{1,0:T(8,128)S(1)}, f32[64,512]{1,0:T(8,128)S(1)}, /*index=5*/f32[64,512]{1,0:T(8,128)S(1)}) fusion(f32[512]{0:T(512)S(1)} %bitcast.24, f32[512]{0:T(512)S(1)} %bitcast.23, f32[64]{0:T(128)S(1)} %copy-done.8, f32[512]{0:T(512)S(1)} %copy-done.6, ...), kind=kLoop, calls=%fused_computation.18 | loop fusion | flops 458752 | bytes 794880 | tf_op jit(solution)/shard_map/mul | solution.py:373
  15.3 1.0 %decays.1 = (f32[3,2,256,512]{3,2,1,0:T(8,128)S(1)}, f32[4,1,512]{2,1,0:T(1,128)S(1)}, f32[2,2,16,512]{3,2,1,0:T(8,128)S(1)}, f32[2,2,16,512]{3,2,1,0:T(8,128)S(1)}, s32[2,1,512]{2,1,0:T(1,128)S(1)}) custom-call(s32[2,256]{1,0:T(2,128)S(1)} %copy-done.4, f32[64,512]{1,0:T(8,128)S(1)} %get-tuple-element.83.refs_0_, f32[64,512]{1,0:T(8,128)S(1)} %get-tuple-element.84.refs_1_, ...), custom_call_target="tpu_custom_call" | custom-call | flops 301989888 | bytes 5242880 | tf_op jit(solution)/shard_map/decays/pallas_call | solution.py:294
  16.3 1.2 %drive_scan_0.1 = (f32[2,2,128,512]{3,2,1,0:T(8,128)S(1)}, f32[4,1,512]{2,1,0:T(1,128)S(1)}) custom-call(bf16[128,1024]{1,0:T(8,128)(2,1)S(1)} %collective-permute-done.1.refs_0_, bf16[2,2048,512]{2,1,0:T(8,128)(2,1)S(1)} %bitcast.14, bf16[2,2048,512]{2,1,0:T(8,128)(2,1)S(1)} %bitcast.17, f32[2,256,512]{2,1,0:T(8,128)S(1)} %own_drive_0.1.refs_3_, ...), custom_call_target="tpu_custom_call" | custom-call | flops 536870912 | bytes 7340032 | tf_op jit(solution)/shard_map/drive_scan_0/pallas_call | solution.py:294
  17.5 1.2 %drive_scan_1.1 = (f32[2,2,128,512]{3,2,1,0:T(8,128)S(1)}, f32[4,1,512]{2,1,0:T(1,128)S(1)}) custom-call(bf16[128,1024]{1,0:T(8,128)(2,1)S(1)} %collective-permute-done.3.refs_0_, bf16[2,2048,512]{2,1,0:T(8,128)(2,1)S(1)} %bitcast.15, bf16[2,2048,512]{2,1,0:T(8,128)(2,1)S(1)} %bitcast.18, f32[2,256,512]{2,1,0:T(8,128)S(1)} %own_drive_0.1.refs_3_, ...), custom_call_target="tpu_custom_call" | custom-call | flops 536870912 | bytes 7340032 | tf_op jit(solution)/shard_map/drive_scan_1/pallas_call | solution.py:294
  18.7 1.4 %collective-permute-start.4 = (f32[8,1,512]{2,1,0:T(1,128)S(1)}, f32[8,1,512]{2,1,0:T(1,128)S(1)}, u32[]{:S(2)}, u32[]{:S(2)}) collective-permute-start(f32[8,1,512]{2,1,0:T(1,128)S(1)} %pad_maximum_fusion), channel_id=1, source_target_pairs={{0,4},{4,0},{8,12},{12,8},{1,5},{5,1},{9,13},{13,9},{2,6},{6,2},{1... | collective-permute-start | bytes 49160 | tf_op jit(solution)/shard_map/ppermute | solution.py:334
  20.1 2.2 %hold.1.refs_4_.w_oth = bf16[2,512,2048]{2,1,0:T(8,128)(2,1)S(1)} custom-call(bf16[2,512,2048]{2,1,0:T(8,128)(2,1)} %collective-permute-done.5.source), custom_call_target="tpu_custom_call" | custom-call | bytes 8388608 | tf_op jit(solution)/shard_map/hold/pallas_call | solution.py:294
  22.5 2.4 %collective-permute-start.6 = (f32[8,1,512]{2,1,0:T(1,128)S(1)}, f32[8,1,512]{2,1,0:T(1,128)S(1)}, u32[]{:S(2)}, u32[]{:S(2)}) collective-permute-start(f32[8,1,512]{2,1,0:T(1,128)S(1)} %pad_maximum_fusion.1), channel_id=1, source_target_pairs={{0,8},{4,12},{8,0},{12,4},{1,9},{5,13},{9,1},{13,5},{2,10},{6,14},... | collective-permute-start | bytes 49160 | tf_op jit(solution)/shard_map/ppermute | solution.py:334
  24.9 0.2 products.1.refs_2_
  25.1 1.1 %collective-permute-done.6 = f32[8,1,512]{2,1,0:T(1,128)S(1)} collective-permute-done((f32[8,1,512]{2,1,0:T(1,128)S(1)}, f32[8,1,512]{2,1,0:T(1,128)S(1)}, u32[]{:S(2)}, u32[]{:S(2)}) %collective-permute-start.6) | collective-permute-done | bytes 16416 | tf_op jit(solution)/shard_map/ppermute | solution.py:334
  26.3 1.1 %carry_far.1 = (bf16[2,2,256,512]{3,2,1,0:T(8,128)(2,1)S(1)}, bf16[256,512]{1,0:T(8,128)(2,1)S(1)}) custom-call(f32[4,1,512]{2,1,0:T(1,128)S(1)} %broadcast_select_fusion.3.carry, f32[2,2,128,512]{3,2,1,0:T(8,128)S(1)} %get-tuple-element.41.refs_0_, f32[2,2,128,512]{3,2,1,0:T(8,128)S(1)} %get-tuple-element.42.refs_1_, ...), custom_call_target="tpu_custom_call" | custom-call | flops 536870912 | bytes 5242880 | tf_op jit(solution)/shard_map/carry_far/pallas_call | solution.py:294
  27.4 1.3 %collective-permute-start.10 = (bf16[256,512]{1,0:T(8,128)(2,1)S(1)}, bf16[256,512]{1,0:T(8,128)(2,1)S(1)}, u32[]{:S(2)}, u32[]{:S(2)}) collective-permute-start(bf16[256,512]{1,0:T(8,128)(2,1)S(1)} %get-tuple-element.52), channel_id=1, source_target_pairs={{0,2},{1,3},{2,0},{3,1},{4,6},{5,7},{6,4},{7,5},{8,10},{9,11},{10,... | collective-permute-start | bytes 786440 | tf_op jit(solution)/shard_map/ppermute | solution.py:334
  28.7 0.7 %far.1 = bf16[256,512]{1,0:T(8,128)(2,1)S(1)} custom-call(bf16[2,2,256,512]{3,2,1,0:T(8,128)(2,1)S(1)} %get-tuple-element.46.states, bf16[2,512,2048]{2,1,0:T(8,128)(2,1)S(1)} %copy-done.1, bf16[2,512,2048]{2,1,0:T(8,128)(2,1)S(1)} %hold.1.refs_4_.w_oth), custom_call_target="tpu_custom_call" | custom-call | flops 536870912 | bytes 5242880 | tf_op jit(solution)/shard_map/far/pallas_call | solution.py:294
  29.4 1.6 %collective-permute-start.9 = (bf16[256,512]{1,0:T(8,128)(2,1)S(1)}, bf16[256,512]{1,0:T(8,128)(2,1)S(1)}, u32[]{:S(2)}, u32[]{:S(2)}) collective-permute-start(bf16[256,512]{1,0:T(8,128)(2,1)S(1)} %far.1), channel_id=1, source_target_pairs={{0,3},{1,2},{2,1},{3,0},{4,7},{5,6},{6,5},{7,4},{8,11},{9,10},{10,... | collective-permute-start | bytes 786440 | tf_op jit(solution)/shard_map/ppermute | solution.py:334
  31.1 1.2 %near.1 = (f32[256,512]{1,0:T(8,128)S(1)}, bf16[128,512]{1,0:T(8,128)(2,1)S(1)}, bf16[128,512]{1,0:T(8,128)(2,1)S(1)}) custom-call(bf16[2,2,256,512]{3,2,1,0:T(8,128)(2,1)S(1)} %get-tuple-element.46.states, bf16[2,512,2048]{2,1,0:T(8,128)(2,1)S(1)} %copy-done.1, bf16[2,512,2048]{2,1,0:T(8,128)(2,1)S(1)} %hold.1.refs_4_.w_oth), custom_call_target="tpu_custom_call" | custom-call | flops 1073741824 | bytes 5242880 | tf_op jit(solution)/shard_map/near/pallas_call | solution.py:294
  32.3 0.1 collective-permute-start.7
  32.4 0.5 %collective-permute-start.8 = (bf16[128,512]{1,0:T(8,128)(2,1)S(1)}, bf16[128,512]{1,0:T(8,128)(2,1)S(1)}, u32[]{:S(2)}, u32[]{:S(2)}) collective-permute-start(bf16[128,512]{1,0:T(8,128)(2,1)S(1)} %get-tuple-element.48), channel_id=1, source_target_pairs={{0,1},{1,0},{2,3},{3,2},{4,5},{5,4},{6,7},{7,6},{8,9},{9,8},{10,11... | collective-permute-start | bytes 393224 | tf_op jit(solution)/shard_map/ppermute | solution.py:334
  32.9 0.8 %collective-permute-done.7.refs_0_ = bf16[128,512]{1,0:T(8,128)(2,1)S(1)} collective-permute-done((bf16[128,512]{1,0:T(8,128)(2,1)S(1)}, bf16[128,512]{1,0:T(8,128)(2,1)S(1)}, u32[]{:S(2)}, u32[]{:S(2)}) %collective-permute-start.7) | collective-permute-done | bytes 131104 | tf_op jit(solution)/shard_map/ppermute | solution.py:334
  33.7 0.2 collective-permute-done.8.refs_1_
  33.9 0.6 %almost.1 = (f32[256,512]{1,0:T(8,128)S(1)}, f32[256,128]{1,0:T(8,128)S(1)}) custom-call(s32[2]{0:T(128)S(1)} %copy-done.3, bf16[2,256,512]{2,1,0:T(8,128)(2,1)S(1)} %constant_dynamic-slice_fusion.events, f32[1,512]{1,0:T(1,128)S(1)} %bitcast.19, bf16[128,512]{1,0:T(8,128)(2,1)S(1)} %collective-permute-done.7.refs_0_, ...), custom_call_target="tpu_custom_call" | custom-call | bytes 1048576 | tf_op jit(solution)/shard_map/almost/pallas_call | solution.py:294
  34.6 1.5 %same.1.done = bf16[2,256,512]{2,1,0:T(8,128)(2,1)} custom-call(s32[2]{0:T(128)S(1)} %copy-done.3, bf16[2,256,512]{2,1,0:T(8,128)(2,1)S(1)} %constant_dynamic-slice_fusion.events, f32[1,512]{1,0:T(1,128)S(1)} %bitcast.20, f32[256,512]{1,0:T(8,128)S(1)} %get-tuple-element.51.refs_0_, bf16[256,512]{1,0:T(8,128)(2,1)S(1)} %collective-permute-done.10.refs_1_), custom_call_target="tpu_custom_call" | custom-call | bytes 1048576 | tf_op jit(solution)/shard_map/same/pallas_call | solution.py:294
  36.1 5.1 %collective-permute-done.9.last = bf16[256,512]{1,0:T(8,128)(2,1)S(1)} collective-permute-done((bf16[256,512]{1,0:T(8,128)(2,1)S(1)}, bf16[256,512]{1,0:T(8,128)(2,1)S(1)}, u32[]{:S(2)}, u32[]{:S(2)}) %collective-permute-start.9) | collective-permute-done | bytes 262176 | tf_op jit(solution)/shard_map/ppermute | solution.py:334
  41.1 0.9 %final.1 = bf16[2,256,512]{2,1,0:T(8,128)(2,1)} custom-call(f32[256,512]{1,0:T(8,128)S(1)} %get-tuple-element.49.total, f32[256,128]{1,0:T(8,128)S(1)} %get-tuple-element.50.keep, bf16[256,512]{1,0:T(8,128)(2,1)S(1)} %collective-permute-done.9.last, bf16[2,256,512]{2,1,0:T(8,128)(2,1)} %same.1.done), custom_call_target="tpu_custom_call", output_to_operand_aliasing={{}: (3, {})} | custom-call | bytes 1048576 | tf_op jit(solution)/shard_map/final/pallas_call | solution.py:294
  (39 shorter events, 0.4 us)
Async XLA Ops:
  0.0 1.2 %copy-start = (bf16[2,256,1024]{2,1,0:T(8,128)(2,1)S(1)}, bf16[2,256,1024]{2,1,0:T(8,128)(2,1)}, u32[]{:S(2)}) copy-start(bf16[2,256,1024]{2,1,0:T(8,128)(2,1)} %param.9) | copy-start | bytes 3145732
  0.0 10.3 %collective-permute-start.2 = (bf16[2048,2,512]{2,1,0:T(2,128)(2,1)}, bf16[2048,2,512]{2,1,0:T(2,128)(2,1)}, u32[]{:S(2)}, u32[]{:S(2)}) collective-permute-start(bf16[2048,2,512]{2,1,0:T(2,128)(2,1)} %param.15), channel_id=1, source_target_pairs={{0,1},{1,0},{2,3},{3,2},{4,5},{5,4},{6,7},{7,6},{8,9},{9,8},{10,11... | collective-permute-start | bytes 12582920 | tf_op jit(solution)/shard_map/ppermute | solution.py:334
  0.1 20.1 %collective-permute-start.5 = (bf16[2,512,2048]{2,1,0:T(8,128)(2,1)}, bf16[2,512,2048]{2,1,0:T(8,128)(2,1)}, u32[]{:S(2)}, u32[]{:S(2)}) collective-permute-start(bf16[2,512,2048]{2,1,0:T(8,128)(2,1)} %w_own.3), channel_id=1, source_target_pairs={{0,1},{1,0},{2,3},{3,2},{4,5},{5,4},{6,7},{7,6},{8,9},{9,8},{10,11... | collective-permute-start | bytes 12582920 | tf_op jit(solution)/shard_map/ppermute | solution.py:334
  1.4 12.7 %collective-permute-start.1 = (bf16[128,1024]{1,0:T(8,128)(2,1)S(1)}, bf16[128,1024]{1,0:T(8,128)(2,1)S(1)}, u32[]{:S(2)}, u32[]{:S(2)}) collective-permute-start(bf16[128,1024]{1,0:T(8,128)(2,1)S(1)} %get-tuple-element.56), channel_id=1, source_target_pairs={{0,2},{2,0},{1,3},{3,1},{4,6},{6,4},{5,7},{7,5},{8,10},{10,8},{9,1... | collective-permute-start | bytes 786440 | tf_op jit(solution)/shard_map/ppermute | solution.py:334
  4.2 9.9 %collective-permute-start = (f32[2,512]{1,0:T(2,128)S(1)}, f32[2,512]{1,0:T(2,128)S(1)}, u32[]{:S(2)}, u32[]{:S(2)}) collective-permute-start(f32[2,512]{1,0:T(2,128)S(1)} %pad_maximum_fusion.2), channel_id=1, source_target_pairs={{0,17},{1,16},{16,1},{17,0},{2,19},{3,18},{18,3},{19,2},{4,21},{5,... | collective-permute-start | bytes 12296 | tf_op jit(solution)/shard_map/ppermute | solution.py:334
  6.3 11.2 %collective-permute-start.3 = (bf16[128,1024]{1,0:T(8,128)(2,1)S(1)}, bf16[128,1024]{1,0:T(8,128)(2,1)S(1)}, u32[]{:S(2)}, u32[]{:S(2)}) collective-permute-start(bf16[128,1024]{1,0:T(8,128)(2,1)S(1)} %get-tuple-element.55), channel_id=1, source_target_pairs={{0,2},{2,0},{1,3},{3,1},{4,6},{6,4},{5,7},{7,5},{8,10},{10,8},{9,1... | collective-permute-start | bytes 786440 | tf_op jit(solution)/shard_map/ppermute | solution.py:334
  13.2 1.0 %copy-start.5 = (f32[512]{0:T(512)S(1)}, f32[512]{0:T(512)}, u32[]{:S(2)}) copy-start(f32[512]{0:T(512)} %param.14) | copy-start | bytes 6148
  13.2 1.0 %copy-start.6 = (f32[512]{0:T(512)S(1)}, f32[512]{0:T(512)}, u32[]{:S(2)}) copy-start(f32[512]{0:T(512)} %param.13) | copy-start | bytes 6148
  13.2 0.9 %copy-start.8 = (f32[64]{0:T(128)S(1)}, f32[64]{0:T(128)}, u32[]{:S(2)}) copy-start(f32[64]{0:T(128)} %param.12) | copy-start | bytes 772
  13.2 2.1 %copy-start.4 = (s32[2,256]{1,0:T(2,128)S(1)}, s32[2,256]{1,0:T(2,128)}, u32[]{:S(2)}) copy-start(s32[2,256]{1,0:T(2,128)} %bins.1) | copy-start | bytes 6148
  18.7 3.6 %collective-permute-start.4 = (f32[8,1,512]{2,1,0:T(1,128)S(1)}, f32[8,1,512]{2,1,0:T(1,128)S(1)}, u32[]{:S(2)}, u32[]{:S(2)}) collective-permute-start(f32[8,1,512]{2,1,0:T(1,128)S(1)} %pad_maximum_fusion), channel_id=1, source_target_pairs={{0,4},{4,0},{8,12},{12,8},{1,5},{5,1},{9,13},{13,9},{2,6},{6,2},{1... | collective-permute-start | bytes 49160 | tf_op jit(solution)/shard_map/ppermute | solution.py:334
  20.1 2.3 %copy-start.7 = (f32[4,1,512]{2,1,0:T(1,128)S(1)}, f32[4,1,512]{2,1,0:T(1,128)}, u32[]{:S(2)}) copy-start(f32[4,1,512]{2,1,0:T(1,128)} %constant.27.clone.1) | copy-start | bytes 24580
  22.3 4.0 %copy-start.1 = (bf16[2,512,2048]{2,1,0:T(8,128)(2,1)S(1)}, bf16[2,512,2048]{2,1,0:T(8,128)(2,1)}, u32[]{:S(2)}) copy-start(bf16[2,512,2048]{2,1,0:T(8,128)(2,1)} %w_own.3) | copy-start | bytes 12582916
  22.5 3.7 %collective-permute-start.6 = (f32[8,1,512]{2,1,0:T(1,128)S(1)}, f32[8,1,512]{2,1,0:T(1,128)S(1)}, u32[]{:S(2)}, u32[]{:S(2)}) collective-permute-start(f32[8,1,512]{2,1,0:T(1,128)S(1)} %pad_maximum_fusion.1), channel_id=1, source_target_pairs={{0,8},{4,12},{8,0},{12,4},{1,9},{5,13},{9,1},{13,5},{2,10},{6,14},... | collective-permute-start | bytes 49160 | tf_op jit(solution)/shard_map/ppermute | solution.py:334
  27.4 7.1 %collective-permute-start.10 = (bf16[256,512]{1,0:T(8,128)(2,1)S(1)}, bf16[256,512]{1,0:T(8,128)(2,1)S(1)}, u32[]{:S(2)}, u32[]{:S(2)}) collective-permute-start(bf16[256,512]{1,0:T(8,128)(2,1)S(1)} %get-tuple-element.52), channel_id=1, source_target_pairs={{0,2},{1,3},{2,0},{3,1},{4,6},{5,7},{6,4},{7,5},{8,10},{9,11},{10,... | collective-permute-start | bytes 786440 | tf_op jit(solution)/shard_map/ppermute | solution.py:334
  29.4 4.5 %copy-start.2 = (f32[512]{0:T(512)S(1)}, f32[512]{0:T(512)}, u32[]{:S(2)}) copy-start(f32[512]{0:T(512)} %param.17) | copy-start | bytes 6148
  29.4 4.5 %copy-start.3 = (s32[2]{0:T(128)S(1)}, s32[2]{0:T(128)}, u32[]{:S(2)}) copy-start(s32[2]{0:T(128)} %lengths.3) | copy-start | bytes 28
  29.4 11.7 %collective-permute-start.9 = (bf16[256,512]{1,0:T(8,128)(2,1)S(1)}, bf16[256,512]{1,0:T(8,128)(2,1)S(1)}, u32[]{:S(2)}, u32[]{:S(2)}) collective-permute-start(bf16[256,512]{1,0:T(8,128)(2,1)S(1)} %far.1), channel_id=1, source_target_pairs={{0,3},{1,2},{2,1},{3,0},{4,7},{5,6},{6,5},{7,4},{8,11},{9,10},{10,... | collective-permute-start | bytes 786440 | tf_op jit(solution)/shard_map/ppermute | solution.py:334
  32.3 1.4 %collective-permute-start.7 = (bf16[128,512]{1,0:T(8,128)(2,1)S(1)}, bf16[128,512]{1,0:T(8,128)(2,1)S(1)}, u32[]{:S(2)}, u32[]{:S(2)}) collective-permute-start(bf16[128,512]{1,0:T(8,128)(2,1)S(1)} %get-tuple-element.47), channel_id=1, source_target_pairs={{0,1},{1,0},{2,3},{3,2},{4,5},{5,4},{6,7},{7,6},{8,9},{9,8},{10,11... | collective-permute-start | bytes 393224 | tf_op jit(solution)/shard_map/ppermute | solution.py:334
  32.4 1.5 %collective-permute-start.8 = (bf16[128,512]{1,0:T(8,128)(2,1)S(1)}, bf16[128,512]{1,0:T(8,128)(2,1)S(1)}, u32[]{:S(2)}, u32[]{:S(2)}) collective-permute-start(bf16[128,512]{1,0:T(8,128)(2,1)S(1)} %get-tuple-element.48), channel_id=1, source_target_pairs={{0,1},{1,0},{2,3},{3,2},{4,5},{5,4},{6,7},{7,6},{8,9},{9,8},{10,11... | collective-permute-start | bytes 393224 | tf_op jit(solution)/shard_map/ppermute | solution.py:334

commit v6 on v5

--- a/solution.py
+++ b/solution.py
@@ -341,9 +341,6 @@
         for u in range(0, rows, tokens)
     ]
 
-    groups = lax.axis_size("groups")
-    by = 3 if groups == 2 else 1
-    rates_oth = swap(jnp.stack([decay_rate, frequency]), ("groups", "grp"), groups * grps, by)
     stored = Layout((0, 1, 2))
     raw_oth = swap(with_layout_constraint(in_proj, stored), "grp", grps, 1)
     raw_oth = with_layout_constraint(raw_oth, stored)
@@ -362,6 +359,8 @@
         )
         for h, w in enumerate((w_own, w_oth))
     ]
+    rates, _ = lax.optimization_barrier((jnp.stack([decay_rate, frequency]), parts[0]))
+    rates_oth = swap(rates, ("ctx", "grp"), ctxs * grps, 3 if ctxs > 1 else 1)
     rates_oth, peer_rows[0], _ = lax.optimization_barrier((rates_oth, peer_rows[0], parts[1]))
 
     def tables(decay, turn):

time: 42.3 us -> 41 us (0.969)
  other arithmetic: 2.07 us -> 1.37 us
    another operation x1, other arithmetic: 0.71 us -> 0.01 us  [local(): jnp.stack([decay_rate, frequency])]
  transfers between devices with their start and end apart: 11 -> 11, of which waited for: 4 -> 5; matrix products, arithmetic and copies ran while one was open for 18% -> 17% of each run, Pallas kernels for 28% -> 28%
where the time goes in v6:
time: 41 us; the launch traced here: 40.7 us
  Pallas kernels  13.6 us (33%)
  starting transfers between devices  12 us (29%)
  waiting for transfers between devices  6.83 us (17%)
  local copies, waits for them, and re-layouts  6.61 us (16%)
  other arithmetic  1.37 us (3%)
    pallas_call x13, Pallas kernels, call(): pl.pallas_call(body, name=name, out_shape=out_shape, in_specs=in_specs or...  13.6 us
    ppermute x11, starting transfers between devices, swap(): return lax.ppermute(array, axes, [(i, i ^ k) for i in range(size)])  12 us
    ppermute x11, waiting for transfers between devices, swap(): return lax.ppermute(array, axes, [(i, i ^ k) for i in range(size)])  6.83 us
    unnamed x19, local copies, waits for them, and re-layouts  3.63 us
    another operation x1, local copies, waits for them, and re-layouts, local(): raw_oth = with_layout_constraint(raw_oth, stored)  2.86 us
    mul x1, other arithmetic, tables(): magnitude * jnp.sin(turned)  1.17 us
  transfers between devices with their start and end apart: 11, of which 5 were waited for; matrix products, arithmetic and copies ran while one was open for 17% of the time, Pallas kernels for 28%

profile of v6, /device:TPU:1, one launch (start us, length us, event | category | flops | bytes accessed | tf_op | source)
XLA Modules:
  0.0 40.7 jit_solution(11993244259934691538)
XLA Ops:
  0.1 0.5 %collective-permute-start.5 = (bf16[2,512,2048]{2,1,0:T(8,128)(2,1)}, bf16[2,512,2048]{2,1,0:T(8,128)(2,1)}, u32[]{:S(2)}, u32[]{:S(2)}) collective-permute-start(bf16[2,512,2048]{2,1,0:T(8,128)(2,1)} %w_own.3), channel_id=1, source_target_pairs={{0,1},{1,0},{2,3},{3,2},{4,5},{5,4},{6,7},{7,6},{8,9},{9,8},{10,11... | collective-permute-start | bytes 12582920 | tf_op jit(solution)/shard_map/ppermute | solution.py:334
  0.5 0.7 %copy-done = bf16[2,256,1024]{2,1,0:T(8,128)(2,1)S(1)} copy-done((bf16[2,256,1024]{2,1,0:T(8,128)(2,1)S(1)}, bf16[2,256,1024]{2,1,0:T(8,128)(2,1)}, u32[]{:S(2)}) %copy-start) | copy-done | bytes 1048600
  1.4 2.1 %collective-permute-start.1 = (bf16[128,1024]{1,0:T(8,128)(2,1)S(1)}, bf16[128,1024]{1,0:T(8,128)(2,1)S(1)}, u32[]{:S(2)}, u32[]{:S(2)}) collective-permute-start(bf16[128,1024]{1,0:T(8,128)(2,1)S(1)} %get-tuple-element.58), channel_id=1, source_target_pairs={{0,2},{2,0},{1,3},{3,1},{4,6},{6,4},{5,7},{7,5},{8,10},{10,8},{9,1... | collective-permute-start | bytes 786440 | tf_op jit(solution)/shard_map/ppermute | solution.py:334
  3.5 0.1 collective-permute-start.3
  3.5 2.9 %copy.16 = bf16[2048,2,512]{2,0,1:T(8,128)(2,1)S(1)} copy(bf16[2048,2,512]{2,1,0:T(2,128)(2,1)} %param.15) | data formatting | bytes 8388608 | tf_op args[6]
  6.4 0.9 %own_drive_0.1.refs_3_ = f32[2,256,512]{2,1,0:T(8,128)S(1)} custom-call(bf16[256,1024]{1,0:T(8,128)(2,1)S(1)} %dynamic-slice_bitcast_fusion.events, bf16[2,2048,512]{2,1,0:T(8,128)(2,1)S(1)} %bitcast.13), custom_call_target="tpu_custom_call" | custom-call | flops 536870912 | bytes 3145728 | tf_op jit(solution)/shard_map/own_drive_0/pallas_call | solution.py:294
  7.3 2.7 %collective-permute-start = (f32[2,512]{1,0:T(2,128)S(1)}, f32[2,512]{1,0:T(2,128)S(1)}, u32[]{:S(2)}, u32[]{:S(2)}) collective-permute-start(f32[2,512]{1,0:T(2,128)S(1)} %pad_maximum_fusion.2), channel_id=1, source_target_pairs={{0,5},{1,4},{4,1},{5,0},{8,13},{9,12},{12,9},{13,8},{2,7},{3,6},{6... | collective-permute-start | bytes 12296 | tf_op jit(solution)/shard_map/ppermute | solution.py:334
  10.0 2.9 %copy.15 = bf16[2048,2,512]{2,0,1:T(8,128)(2,1)S(1)} copy(bf16[2048,2,512]{2,1,0:T(2,128)(2,1)} %collective-permute-done.2) | data formatting | bytes 8388608 | tf_op jit(solution)/shard_map/layout_constraint | solution.py:346
  12.9 0.9 %own_drive_1.1.refs_4_ = f32[2,256,512]{2,1,0:T(8,128)S(1)} custom-call(bf16[256,1024]{1,0:T(8,128)(2,1)S(1)} %dynamic-slice_bitcast_fusion.events, bf16[2,2048,512]{2,1,0:T(8,128)(2,1)S(1)} %bitcast.16), custom_call_target="tpu_custom_call" | custom-call | flops 536870912 | bytes 3145728 | tf_op jit(solution)/shard_map/own_drive_1/pallas_call | solution.py:294
  13.8 1.2 %fusion.7 = (f32[64,512]{1,0:T(8,128)S(1)}, f32[64,512]{1,0:T(8,128)S(1)}, f32[64,512]{1,0:T(8,128)S(1)}, f32[64,512]{1,0:T(8,128)S(1)}, f32[64,512]{1,0:T(8,128)S(1)}, /*index=5*/f32[64,512]{1,0:T(8,128)S(1)}) fusion(f32[512]{0:T(512)S(1)} %bitcast.24, f32[512]{0:T(512)S(1)} %bitcast.23, f32[64]{0:T(128)S(1)} %copy-done.8, f32[512]{0:T(512)S(1)} %copy-done.6, ...), kind=kLoop, calls=%fused_computation.18 | loop fusion | flops 458752 | bytes 794880 | tf_op jit(solution)/shard_map/mul | solution.py:372
  15.0 1.0 %decays.1 = (f32[3,2,256,512]{3,2,1,0:T(8,128)S(1)}, f32[4,1,512]{2,1,0:T(1,128)S(1)}, f32[2,2,16,512]{3,2,1,0:T(8,128)S(1)}, f32[2,2,16,512]{3,2,1,0:T(8,128)S(1)}, s32[2,1,512]{2,1,0:T(1,128)S(1)}) custom-call(s32[2,256]{1,0:T(2,128)S(1)} %copy-done.4, f32[64,512]{1,0:T(8,128)S(1)} %get-tuple-element.85.refs_0_, f32[64,512]{1,0:T(8,128)S(1)} %get-tuple-element.86.refs_1_, ...), custom_call_target="tpu_custom_call" | custom-call | flops 301989888 | bytes 5242880 | tf_op jit(solution)/shard_map/decays/pallas_call | solution.py:294
  16.0 1.2 %drive_scan_0.1 = (f32[2,2,128,512]{3,2,1,0:T(8,128)S(1)}, f32[4,1,512]{2,1,0:T(1,128)S(1)}) custom-call(bf16[128,1024]{1,0:T(8,128)(2,1)S(1)} %collective-permute-done.1.refs_0_, bf16[2,2048,512]{2,1,0:T(8,128)(2,1)S(1)} %bitcast.14, bf16[2,2048,512]{2,1,0:T(8,128)(2,1)S(1)} %bitcast.17, f32[2,256,512]{2,1,0:T(8,128)S(1)} %own_drive_0.1.refs_3_, ...), custom_call_target="tpu_custom_call" | custom-call | flops 536870912 | bytes 7340032 | tf_op jit(solution)/shard_map/drive_scan_0/pallas_call | solution.py:294
  17.2 1.2 %drive_scan_1.1 = (f32[2,2,128,512]{3,2,1,0:T(8,128)S(1)}, f32[4,1,512]{2,1,0:T(1,128)S(1)}) custom-call(bf16[128,1024]{1,0:T(8,128)(2,1)S(1)} %collective-permute-done.3.refs_0_, bf16[2,2048,512]{2,1,0:T(8,128)(2,1)S(1)} %bitcast.15, bf16[2,2048,512]{2,1,0:T(8,128)(2,1)S(1)} %bitcast.18, f32[2,256,512]{2,1,0:T(8,128)S(1)} %own_drive_0.1.refs_3_, ...), custom_call_target="tpu_custom_call" | custom-call | flops 536870912 | bytes 7340032 | tf_op jit(solution)/shard_map/drive_scan_1/pallas_call | solution.py:294
  18.4 0.1 collective-permute-start.4
  18.5 2.2 %hold.1.refs_4_.w_oth = bf16[2,512,2048]{2,1,0:T(8,128)(2,1)S(1)} custom-call(bf16[2,512,2048]{2,1,0:T(8,128)(2,1)} %collective-permute-done.5.source), custom_call_target="tpu_custom_call" | custom-call | bytes 8388608 | tf_op jit(solution)/shard_map/hold/pallas_call | solution.py:294
  20.7 0.3 collective-permute-done.4
  21.2 2.6 %collective-permute-start.6 = (f32[8,1,512]{2,1,0:T(1,128)S(1)}, f32[8,1,512]{2,1,0:T(1,128)S(1)}, u32[]{:S(2)}, u32[]{:S(2)}) collective-permute-start(f32[8,1,512]{2,1,0:T(1,128)S(1)} %pad_maximum_fusion.1), channel_id=1, source_target_pairs={{0,8},{4,12},{8,0},{12,4},{1,9},{5,13},{9,1},{13,5},{2,10},{6,14},... | collective-permute-start | bytes 49160 | tf_op jit(solution)/shard_map/ppermute | solution.py:334
  23.8 0.2 products.1.refs_2_
  24.1 0.9 %collective-permute-done.6 = f32[8,1,512]{2,1,0:T(1,128)S(1)} collective-permute-done((f32[8,1,512]{2,1,0:T(1,128)S(1)}, f32[8,1,512]{2,1,0:T(1,128)S(1)}, u32[]{:S(2)}, u32[]{:S(2)}) %collective-permute-start.6) | collective-permute-done | bytes 16416 | tf_op jit(solution)/shard_map/ppermute | solution.py:334
  25.0 1.1 %carry_far.1 = (bf16[2,2,256,512]{3,2,1,0:T(8,128)(2,1)S(1)}, bf16[256,512]{1,0:T(8,128)(2,1)S(1)}) custom-call(f32[4,1,512]{2,1,0:T(1,128)S(1)} %broadcast_select_fusion.3.carry, f32[2,2,128,512]{3,2,1,0:T(8,128)S(1)} %get-tuple-element.43.refs_0_, f32[2,2,128,512]{3,2,1,0:T(8,128)S(1)} %get-tuple-element.44.refs_1_, ...), custom_call_target="tpu_custom_call" | custom-call | flops 536870912 | bytes 5242880 | tf_op jit(solution)/shard_map/carry_far/pallas_call | solution.py:294
  26.1 1.3 %collective-permute-start.10 = (bf16[256,512]{1,0:T(8,128)(2,1)S(1)}, bf16[256,512]{1,0:T(8,128)(2,1)S(1)}, u32[]{:S(2)}, u32[]{:S(2)}) collective-permute-start(bf16[256,512]{1,0:T(8,128)(2,1)S(1)} %get-tuple-element.54), channel_id=1, source_target_pairs={{0,2},{1,3},{2,0},{3,1},{4,6},{5,7},{6,4},{7,5},{8,10},{9,11},{10,... | collective-permute-start | bytes 786440 | tf_op jit(solution)/shard_map/ppermute | solution.py:334
  27.5 0.7 %far.1 = bf16[256,512]{1,0:T(8,128)(2,1)S(1)} custom-call(bf16[2,2,256,512]{3,2,1,0:T(8,128)(2,1)S(1)} %get-tuple-element.48.states, bf16[2,512,2048]{2,1,0:T(8,128)(2,1)S(1)} %copy-done.1, bf16[2,512,2048]{2,1,0:T(8,128)(2,1)S(1)} %hold.1.refs_4_.w_oth), custom_call_target="tpu_custom_call" | custom-call | flops 536870912 | bytes 5242880 | tf_op jit(solution)/shard_map/far/pallas_call | solution.py:294
  28.2 2.1 %collective-permute-start.9 = (bf16[256,512]{1,0:T(8,128)(2,1)S(1)}, bf16[256,512]{1,0:T(8,128)(2,1)S(1)}, u32[]{:S(2)}, u32[]{:S(2)}) collective-permute-start(bf16[256,512]{1,0:T(8,128)(2,1)S(1)} %far.1), channel_id=1, source_target_pairs={{0,3},{1,2},{2,1},{3,0},{4,7},{5,6},{6,5},{7,4},{8,11},{9,10},{10,... | collective-permute-start | bytes 786440 | tf_op jit(solution)/shard_map/ppermute | solution.py:334
  30.3 1.2 %near.1 = (f32[256,512]{1,0:T(8,128)S(1)}, bf16[128,512]{1,0:T(8,128)(2,1)S(1)}, bf16[128,512]{1,0:T(8,128)(2,1)S(1)}) custom-call(bf16[2,2,256,512]{3,2,1,0:T(8,128)(2,1)S(1)} %get-tuple-element.48.states, bf16[2,512,2048]{2,1,0:T(8,128)(2,1)S(1)} %copy-done.1, bf16[2,512,2048]{2,1,0:T(8,128)(2,1)S(1)} %hold.1.refs_4_.w_oth), custom_call_target="tpu_custom_call" | custom-call | flops 1073741824 | bytes 5242880 | tf_op jit(solution)/shard_map/near/pallas_call | solution.py:294
  31.5 0.1 collective-permute-start.7
  31.6 0.5 %collective-permute-start.8 = (bf16[128,512]{1,0:T(8,128)(2,1)S(1)}, bf16[128,512]{1,0:T(8,128)(2,1)S(1)}, u32[]{:S(2)}, u32[]{:S(2)}) collective-permute-start(bf16[128,512]{1,0:T(8,128)(2,1)S(1)} %get-tuple-element.50), channel_id=1, source_target_pairs={{0,1},{1,0},{2,3},{3,2},{4,5},{5,4},{6,7},{7,6},{8,9},{9,8},{10,11... | collective-permute-start | bytes 393224 | tf_op jit(solution)/shard_map/ppermute | solution.py:334
  32.1 0.8 %collective-permute-done.7.refs_0_ = bf16[128,512]{1,0:T(8,128)(2,1)S(1)} collective-permute-done((bf16[128,512]{1,0:T(8,128)(2,1)S(1)}, bf16[128,512]{1,0:T(8,128)(2,1)S(1)}, u32[]{:S(2)}, u32[]{:S(2)}) %collective-permute-start.7) | collective-permute-done | bytes 131104 | tf_op jit(solution)/shard_map/ppermute | solution.py:334
  32.9 0.2 collective-permute-done.8.refs_1_
  33.1 0.6 %almost.1 = (f32[256,512]{1,0:T(8,128)S(1)}, f32[256,128]{1,0:T(8,128)S(1)}) custom-call(s32[2]{0:T(128)S(1)} %copy-done.3, bf16[2,256,512]{2,1,0:T(8,128)(2,1)S(1)} %constant_dynamic-slice_fusion.events, f32[1,512]{1,0:T(1,128)S(1)} %bitcast.19, bf16[128,512]{1,0:T(8,128)(2,1)S(1)} %collective-permute-done.7.refs_0_, ...), custom_call_target="tpu_custom_call" | custom-call | bytes 1048576 | tf_op jit(solution)/shard_map/almost/pallas_call | solution.py:294
  33.8 1.5 %same.1.done = bf16[2,256,512]{2,1,0:T(8,128)(2,1)} custom-call(s32[2]{0:T(128)S(1)} %copy-done.3, bf16[2,256,512]{2,1,0:T(8,128)(2,1)S(1)} %constant_dynamic-slice_fusion.events, f32[1,512]{1,0:T(1,128)S(1)} %bitcast.20, f32[256,512]{1,0:T(8,128)S(1)} %get-tuple-element.53.refs_0_, bf16[256,512]{1,0:T(8,128)(2,1)S(1)} %collective-permute-done.10.refs_1_), custom_call_target="tpu_custom_call" | custom-call | bytes 1048576 | tf_op jit(solution)/shard_map/same/pallas_call | solution.py:294
  35.3 4.5 %collective-permute-done.9.last = bf16[256,512]{1,0:T(8,128)(2,1)S(1)} collective-permute-done((bf16[256,512]{1,0:T(8,128)(2,1)S(1)}, bf16[256,512]{1,0:T(8,128)(2,1)S(1)}, u32[]{:S(2)}, u32[]{:S(2)}) %collective-permute-start.9) | collective-permute-done | bytes 262176 | tf_op jit(solution)/shard_map/ppermute | solution.py:334
  39.8 0.9 %final.1 = bf16[2,256,512]{2,1,0:T(8,128)(2,1)} custom-call(f32[256,512]{1,0:T(8,128)S(1)} %get-tuple-element.51.total, f32[256,128]{1,0:T(8,128)S(1)} %get-tuple-element.52.keep, bf16[256,512]{1,0:T(8,128)(2,1)S(1)} %collective-permute-done.9.last, bf16[2,256,512]{2,1,0:T(8,128)(2,1)} %same.1.done), custom_call_target="tpu_custom_call", output_to_operand_aliasing={{}: (3, {})} | custom-call | bytes 1048576 | tf_op jit(solution)/shard_map/final/pallas_call | solution.py:294
  (39 shorter events, 0.4 us)
Async XLA Ops:
  0.0 1.2 %copy-start = (bf16[2,256,1024]{2,1,0:T(8,128)(2,1)S(1)}, bf16[2,256,1024]{2,1,0:T(8,128)(2,1)}, u32[]{:S(2)}) copy-start(bf16[2,256,1024]{2,1,0:T(8,128)(2,1)} %param.9) | copy-start | bytes 3145732
  0.0 10.0 %collective-permute-start.2 = (bf16[2048,2,512]{2,1,0:T(2,128)(2,1)}, bf16[2048,2,512]{2,1,0:T(2,128)(2,1)}, u32[]{:S(2)}, u32[]{:S(2)}) collective-permute-start(bf16[2048,2,512]{2,1,0:T(2,128)(2,1)} %param.15), channel_id=1, source_target_pairs={{0,1},{1,0},{2,3},{3,2},{4,5},{5,4},{6,7},{7,6},{8,9},{9,8},{10,11... | collective-permute-start | bytes 12582920 | tf_op jit(solution)/shard_map/ppermute | solution.py:334
  0.1 18.4 %collective-permute-start.5 = (bf16[2,512,2048]{2,1,0:T(8,128)(2,1)}, bf16[2,512,2048]{2,1,0:T(8,128)(2,1)}, u32[]{:S(2)}, u32[]{:S(2)}) collective-permute-start(bf16[2,512,2048]{2,1,0:T(8,128)(2,1)} %w_own.3), channel_id=1, source_target_pairs={{0,1},{1,0},{2,3},{3,2},{4,5},{5,4},{6,7},{7,6},{8,9},{9,8},{10,11... | collective-permute-start | bytes 12582920 | tf_op jit(solution)/shard_map/ppermute | solution.py:334
  1.4 12.4 %collective-permute-start.1 = (bf16[128,1024]{1,0:T(8,128)(2,1)S(1)}, bf16[128,1024]{1,0:T(8,128)(2,1)S(1)}, u32[]{:S(2)}, u32[]{:S(2)}) collective-permute-start(bf16[128,1024]{1,0:T(8,128)(2,1)S(1)} %get-tuple-element.58), channel_id=1, source_target_pairs={{0,2},{2,0},{1,3},{3,1},{4,6},{6,4},{5,7},{7,5},{8,10},{10,8},{9,1... | collective-permute-start | bytes 786440 | tf_op jit(solution)/shard_map/ppermute | solution.py:334
  3.5 13.7 %collective-permute-start.3 = (bf16[128,1024]{1,0:T(8,128)(2,1)S(1)}, bf16[128,1024]{1,0:T(8,128)(2,1)S(1)}, u32[]{:S(2)}, u32[]{:S(2)}) collective-permute-start(bf16[128,1024]{1,0:T(8,128)(2,1)S(1)} %get-tuple-element.57), channel_id=1, source_target_pairs={{0,2},{2,0},{1,3},{3,1},{4,6},{6,4},{5,7},{7,5},{8,10},{10,8},{9,1... | collective-permute-start | bytes 786440 | tf_op jit(solution)/shard_map/ppermute | solution.py:334
  6.4 0.9 %copy-start.5 = (f32[512]{0:T(512)S(1)}, f32[512]{0:T(512)}, u32[]{:S(2)}) copy-start(f32[512]{0:T(512)} %param.14) | copy-start | bytes 6148
  6.4 0.9 %copy-start.6 = (f32[512]{0:T(512)S(1)}, f32[512]{0:T(512)}, u32[]{:S(2)}) copy-start(f32[512]{0:T(512)} %param.13) | copy-start | bytes 6148
  7.3 6.4 %collective-permute-start = (f32[2,512]{1,0:T(2,128)S(1)}, f32[2,512]{1,0:T(2,128)S(1)}, u32[]{:S(2)}, u32[]{:S(2)}) collective-permute-start(f32[2,512]{1,0:T(2,128)S(1)} %pad_maximum_fusion.2), channel_id=1, source_target_pairs={{0,5},{1,4},{4,1},{5,0},{8,13},{9,12},{12,9},{13,8},{2,7},{3,6},{6... | collective-permute-start | bytes 12296 | tf_op jit(solution)/shard_map/ppermute | solution.py:334
  12.9 0.9 %copy-start.8 = (f32[64]{0:T(128)S(1)}, f32[64]{0:T(128)}, u32[]{:S(2)}) copy-start(f32[64]{0:T(128)} %param.12) | copy-start | bytes 772
  12.9 2.1 %copy-start.4 = (s32[2,256]{1,0:T(2,128)S(1)}, s32[2,256]{1,0:T(2,128)}, u32[]{:S(2)}) copy-start(s32[2,256]{1,0:T(2,128)} %bins.1) | copy-start | bytes 6148
  18.4 2.7 %collective-permute-start.4 = (f32[8,1,512]{2,1,0:T(1,128)S(1)}, f32[8,1,512]{2,1,0:T(1,128)S(1)}, u32[]{:S(2)}, u32[]{:S(2)}) collective-permute-start(f32[8,1,512]{2,1,0:T(1,128)S(1)} %pad_maximum_fusion), channel_id=1, source_target_pairs={{0,4},{4,0},{8,12},{12,8},{1,5},{5,1},{9,13},{13,9},{2,6},{6,2},{1... | collective-permute-start | bytes 49160 | tf_op jit(solution)/shard_map/ppermute | solution.py:334
  18.5 2.7 %copy-start.7 = (f32[4,1,512]{2,1,0:T(1,128)S(1)}, f32[4,1,512]{2,1,0:T(1,128)}, u32[]{:S(2)}) copy-start(f32[4,1,512]{2,1,0:T(1,128)} %constant.27.clone.1) | copy-start | bytes 24580
  20.7 4.3 %copy-start.1 = (bf16[2,512,2048]{2,1,0:T(8,128)(2,1)S(1)}, bf16[2,512,2048]{2,1,0:T(8,128)(2,1)}, u32[]{:S(2)}) copy-start(bf16[2,512,2048]{2,1,0:T(8,128)(2,1)} %w_own.3) | copy-start | bytes 12582916
  21.2 3.7 %collective-permute-start.6 = (f32[8,1,512]{2,1,0:T(1,128)S(1)}, f32[8,1,512]{2,1,0:T(1,128)S(1)}, u32[]{:S(2)}, u32[]{:S(2)}) collective-permute-start(f32[8,1,512]{2,1,0:T(1,128)S(1)} %pad_maximum_fusion.1), channel_id=1, source_target_pairs={{0,8},{4,12},{8,0},{12,4},{1,9},{5,13},{9,1},{13,5},{2,10},{6,14},... | collective-permute-start | bytes 49160 | tf_op jit(solution)/shard_map/ppermute | solution.py:334
  26.1 7.7 %collective-permute-start.10 = (bf16[256,512]{1,0:T(8,128)(2,1)S(1)}, bf16[256,512]{1,0:T(8,128)(2,1)S(1)}, u32[]{:S(2)}, u32[]{:S(2)}) collective-permute-start(bf16[256,512]{1,0:T(8,128)(2,1)S(1)} %get-tuple-element.54), channel_id=1, source_target_pairs={{0,2},{1,3},{2,0},{3,1},{4,6},{5,7},{6,4},{7,5},{8,10},{9,11},{10,... | collective-permute-start | bytes 786440 | tf_op jit(solution)/shard_map/ppermute | solution.py:334
  28.2 5.0 %copy-start.2 = (f32[512]{0:T(512)S(1)}, f32[512]{0:T(512)}, u32[]{:S(2)}) copy-start(f32[512]{0:T(512)} %param.17) | copy-start | bytes 6148
  28.2 4.9 %copy-start.3 = (s32[2]{0:T(128)S(1)}, s32[2]{0:T(128)}, u32[]{:S(2)}) copy-start(s32[2]{0:T(128)} %lengths.3) | copy-start | bytes 28
  28.2 11.6 %collective-permute-start.9 = (bf16[256,512]{1,0:T(8,128)(2,1)S(1)}, bf16[256,512]{1,0:T(8,128)(2,1)S(1)}, u32[]{:S(2)}, u32[]{:S(2)}) collective-permute-start(bf16[256,512]{1,0:T(8,128)(2,1)S(1)} %far.1), channel_id=1, source_target_pairs={{0,3},{1,2},{2,1},{3,0},{4,7},{5,6},{6,5},{7,4},{8,11},{9,10},{10,... | collective-permute-start | bytes 786440 | tf_op jit(solution)/shard_map/ppermute | solution.py:334
  31.5 1.4 %collective-permute-start.7 = (bf16[128,512]{1,0:T(8,128)(2,1)S(1)}, bf16[128,512]{1,0:T(8,128)(2,1)S(1)}, u32[]{:S(2)}, u32[]{:S(2)}) collective-permute-start(bf16[128,512]{1,0:T(8,128)(2,1)S(1)} %get-tuple-element.49), channel_id=1, source_target_pairs={{0,1},{1,0},{2,3},{3,2},{4,5},{5,4},{6,7},{7,6},{8,9},{9,8},{10,11... | collective-permute-start | bytes 393224 | tf_op jit(solution)/shard_map/ppermute | solution.py:334
  31.6 1.5 %collective-permute-start.8 = (bf16[128,512]{1,0:T(8,128)(2,1)S(1)}, bf16[128,512]{1,0:T(8,128)(2,1)S(1)}, u32[]{:S(2)}, u32[]{:S(2)}) collective-permute-start(bf16[128,512]{1,0:T(8,128)(2,1)S(1)} %get-tuple-element.50), channel_id=1, source_target_pairs={{0,1},{1,0},{2,3},{3,2},{4,5},{5,4},{6,7},{7,6},{8,9},{9,8},{10,11... | collective-permute-start | bytes 393224 | tf_op jit(solution)/shard_map/ppermute | solution.py:334

commit v7 on v6

--- a/solution.py
+++ b/solution.py
@@ -101,16 +101,25 @@
         prod[2 + place] = ci
 
 
-def product_kernel(tokens, dec, starts, cum):
+def state_kernel(tokens, dec, starts, *refs):
+    chunks = dec.shape[2] // tokens
+    drives, begins, (cum, state) = refs[:chunks], refs[chunks : 2 * chunks], refs[2 * chunks :]
     for h in range(2):
-        for u in range(dec.shape[2] // tokens):
+        for u in range(chunks):
             at = slice(u * SEGS, (u + 1) * SEGS)
             cr, ci = starts[0, h, at, :], starts[1, h, at, :]
+            sr, si = begins[u][0, h], begins[u][1, h]
             for s in range(tokens // SEGS):
                 at = step_rows(tokens, u, s)
-                cr, ci = cmul(dec[0, h, at, :], dec[1, h, at, :], cr, ci)
+                to = step_rows(tokens, 0, s)
+                dr, di = dec[0, h, at, :], dec[1, h, at, :]
+                cr, ci = cmul(dr, di, cr, ci)
+                xr, xi = cmul(dr, di, sr, si)
+                sr, si = xr + drives[u][0, h, to, :], xi + drives[u][1, h, to, :]
                 cum[0, h, at, :] = cr
                 cum[1, h, at, :] = ci
+                state[0, h, at, :] = sr
+                state[1, h, at, :] = si
 
 
 def own_kernel(tokens, events, w, out):
@@ -129,7 +138,7 @@
     events = refs[:peers]
     weights = refs[peers : peers + 2]
     parts = refs[peers + 2 : peers + 4]
-    dec, runs, *earlier, state, ends, drive = refs[peers + 4 :]
+    dec, runs, *earlier, drive, begin, ends = refs[peers + 4 :]
     chan, grp = lax.axis_index("chan"), lax.axis_index("grp")
     width = events[0].shape[1]
     steps = tokens // SEGS
@@ -143,12 +152,12 @@
             for n in range(peers):
                 start = pl.multiple_of((chan ^ (n + 1)) * width, width)
                 total = total + dot(rows[n], weights[h][c, pl.ds(start, width), :])
-            drive[c] = dec[2, h, base : base + tokens, :] * total
+            drive[c, h] = dec[2, h, base : base + tokens, :] * total
 
         def at(s):
             sl = slice(base + s * SEGS, base + (s + 1) * SEGS)
             to = slice(s * SEGS, (s + 1) * SEGS)
-            return dec[0, h, sl, :], dec[1, h, sl, :], drive[0, to, :], drive[1, to, :]
+            return dec[0, h, sl, :], dec[1, h, sl, :], drive[0, h, to, :], drive[1, h, to, :]
 
         _, _, sr, si = at(0)
         for s in range(1, steps):
@@ -161,28 +170,21 @@
             cr, ci = earlier[0][place], earlier[0][2 + place]
         else:
             cr, ci = jnp.zeros_like(sr[:1]), jnp.zeros_like(si[:1])
-        sr, si, er, ei = run_starts(ar, ai, sr, si, cr, ci)
+        begin[0, h], begin[1, h], er, ei = run_starts(ar, ai, sr, si, cr, ci)
         ends[place] = er
         ends[2 + place] = ei
-        for s in range(steps):
-            dr, di, vr, vi = at(s)
-            xr, xi = cmul(dr, di, sr, si)
-            sr, si = xr + vr, xi + vi
-            to = slice(s * SEGS, (s + 1) * SEGS)
-            state[0, h, to, :] = sr
-            state[1, h, to, :] = si
-
-
-def carry_in(tokens, carry, states, cum, out):
+
+
+def carry_in(tokens, carry, state, cum, out):
     grp = lax.axis_index("grp")
     order = order_matrix(tokens)
     for h in range(2):
         place = grp if h == 0 else 1 - grp
         cr, ci = carry[place], carry[2 + place]
-        for u, state in enumerate(states):
-            sl = slice(u * tokens, (u + 1) * tokens)
+        for u in range(0, state.shape[2], tokens):
+            sl = slice(u, u + tokens)
             xr, xi = cmul(cum[0, h, sl, :], cum[1, h, sl, :], cr, ci)
-            for c, value in ((0, state[0, h] + xr), (1, state[1, h] + xi)):
+            for c, value in ((0, state[0, h, sl, :] + xr), (1, state[1, h, sl, :] + xi)):
                 moved = lax.dot_general(
                     order, value.astype(BF16), (((0,), (0,)), ((), ())), preferred_element_type=F32
                 )
@@ -202,9 +204,8 @@
         out[...] = total[i * count : (i + 1) * count].astype(out.dtype)
 
 
-def first_kernel(tokens, d, carry, *refs):
-    *states, cum, w_own, w_oth, rounded, out = refs
-    carry_in(tokens, carry, states, cum, rounded)
+def first_kernel(tokens, d, carry, state, cum, w_own, w_oth, rounded, out):
+    carry_in(tokens, carry, state, cum, rounded)
     mix(d, rounded, w_own, w_oth, out)
 
 
@@ -390,24 +391,28 @@
     )
 
     peers = chans - 1
-    states, ends = [], None
+    drives, begins, ends = [], [], None
     for u in range(chunks):
-        state, ends = call(
+        drive, begin, ends = call(
             functools.partial(scan_kernel, tokens, peers, u),
             "drive_scan_%d" % u,
             (*peer_rows[u], w_own, w_oth, *parts, dec, runs) + ((ends,) if u else ()),
-            (shape((2, 2, tokens, q), F32), shape((4, 1, q), F32)),
-            scratch=[pltpu.VMEM((2, tokens, q), F32)],
+            (
+                shape((2, 2, tokens, q), F32),
+                shape((2, 2, SEGS, q), F32),
+                shape((4, 1, q), F32),
+            ),
             flops=2 * tokens * width * 4 * q * peers,
             bytes_=4 * width * q * 2 * peers + 4 * tokens * q * 12,
         )
-        states.append(state)
+        drives.append(drive)
+        begins.append(begin)
     starts, _ = lax.optimization_barrier((starts, ends))
-    cum = call(
-        functools.partial(product_kernel, tokens),
-        "products",
-        (dec, starts),
-        shape((2, 2, rows, q), F32),
+    cum, state = call(
+        functools.partial(state_kernel, tokens),
+        "states",
+        (dec, starts, *drives, *begins),
+        (shape((2, 2, rows, q), F32),) * 2,
         bytes_=4 * 2 * rows * q * 4,
     )
     o_oth = call(
@@ -443,7 +448,7 @@
     rounded, piece = call(
         functools.partial(first_kernel, tokens, far[0]),
         "carry_far",
-        (carry, *states, cum, out_proj, o_oth),
+        (carry, state, cum, out_proj, o_oth),
         (shape((2, 2, rows, q), BF16), shape((rows, part_width), BF16)),
         flops=2 * rows * part_width * 4 * q,
         bytes_=4 * q * part_width * 2 + 6 * rows * q * 4,

time: 41 us -> 40.9 us (level)
  transfers between devices with their start and end apart: 11 -> 11, of which waited for: 5 -> 5; matrix products, arithmetic and copies ran while one was open for 17% -> 17% of each run, Pallas kernels for 28% -> 29%
where the time goes in v7:
time: 40.9 us; the launch traced here: 40.7 us
  Pallas kernels  13.7 us (33%)
  starting transfers between devices  12.1 us (30%)
  local copies, waits for them, and re-layouts  6.61 us (16%)
  waiting for transfers between devices  6.58 us (16%)
  other arithmetic  1.37 us (3%)
    pallas_call x13, Pallas kernels, call(): pl.pallas_call(body, name=name, out_shape=out_shape, in_specs=in_specs or...  13.7 us
    ppermute x11, starting transfers between devices, swap(): return lax.ppermute(array, axes, [(i, i ^ k) for i in range(size)])  12.1 us
    ppermute x11, waiting for transfers between devices, swap(): return lax.ppermute(array, axes, [(i, i ^ k) for i in range(size)])  6.58 us
    unnamed x19, local copies, waits for them, and re-layouts  3.63 us
    another operation x1, local copies, waits for them, and re-layouts, local(): raw_oth = with_layout_constraint(raw_oth, stored)  2.86 us
    mul x1, other arithmetic, tables(): magnitude * jnp.sin(turned)  1.17 us
  transfers between devices with their start and end apart: 11, of which 5 were waited for; matrix products, arithmetic and copies ran while one was open for 17% of the time, Pallas kernels for 29%

profile of v7, /device:TPU:1, one launch (start us, length us, event | category | flops | bytes accessed | tf_op | source)
XLA Modules:
  0.0 40.7 jit_solution(16666620269091849706)
XLA Ops:
  0.1 0.5 %collective-permute-start.5 = (bf16[2,512,2048]{2,1,0:T(8,128)(2,1)}, bf16[2,512,2048]{2,1,0:T(8,128)(2,1)}, u32[]{:S(2)}, u32[]{:S(2)}) collective-permute-start(bf16[2,512,2048]{2,1,0:T(8,128)(2,1)} %w_own.5), channel_id=1, source_target_pairs={{0,1},{1,0},{2,3},{3,2},{4,5},{5,4},{6,7},{7,6},{8,9},{9,8},{10,11... | collective-permute-start | bytes 12582920 | tf_op jit(solution)/shard_map/ppermute | solution.py:335
  0.5 0.7 %copy-done = bf16[2,256,1024]{2,1,0:T(8,128)(2,1)S(1)} copy-done((bf16[2,256,1024]{2,1,0:T(8,128)(2,1)S(1)}, bf16[2,256,1024]{2,1,0:T(8,128)(2,1)}, u32[]{:S(2)}) %copy-start) | copy-done | bytes 1048600
  1.4 2.1 %collective-permute-start.1 = (bf16[128,1024]{1,0:T(8,128)(2,1)S(1)}, bf16[128,1024]{1,0:T(8,128)(2,1)S(1)}, u32[]{:S(2)}, u32[]{:S(2)}) collective-permute-start(bf16[128,1024]{1,0:T(8,128)(2,1)S(1)} %get-tuple-element.66), channel_id=1, source_target_pairs={{0,2},{2,0},{1,3},{3,1},{4,6},{6,4},{5,7},{7,5},{8,10},{10,8},{9,1... | collective-permute-start | bytes 786440 | tf_op jit(solution)/shard_map/ppermute | solution.py:335
  3.5 0.1 collective-permute-start.3
  3.5 2.9 %copy.16 = bf16[2048,2,512]{2,0,1:T(8,128)(2,1)S(1)} copy(bf16[2048,2,512]{2,1,0:T(2,128)(2,1)} %param.15) | data formatting | bytes 8388608 | tf_op args[6]
  6.4 0.9 %own_drive_0.1.refs_3_ = f32[2,256,512]{2,1,0:T(8,128)S(1)} custom-call(bf16[256,1024]{1,0:T(8,128)(2,1)S(1)} %dynamic-slice_bitcast_fusion.events, bf16[2,2048,512]{2,1,0:T(8,128)(2,1)S(1)} %bitcast.13), custom_call_target="tpu_custom_call" | custom-call | flops 536870912 | bytes 3145728 | tf_op jit(solution)/shard_map/own_drive_0/pallas_call | solution.py:295
  7.3 2.7 %collective-permute-start = (f32[2,512]{1,0:T(2,128)S(1)}, f32[2,512]{1,0:T(2,128)S(1)}, u32[]{:S(2)}, u32[]{:S(2)}) collective-permute-start(f32[2,512]{1,0:T(2,128)S(1)} %pad_maximum_fusion.2), channel_id=1, source_target_pairs={{0,5},{1,4},{4,1},{5,0},{8,13},{9,12},{12,9},{13,8},{2,7},{3,6},{6... | collective-permute-start | bytes 12296 | tf_op jit(solution)/shard_map/ppermute | solution.py:335
  10.0 2.9 %copy.15 = bf16[2048,2,512]{2,0,1:T(8,128)(2,1)S(1)} copy(bf16[2048,2,512]{2,1,0:T(2,128)(2,1)} %collective-permute-done.2) | data formatting | bytes 8388608 | tf_op jit(solution)/shard_map/layout_constraint | solution.py:347
  12.9 0.9 %own_drive_1.1.refs_4_ = f32[2,256,512]{2,1,0:T(8,128)S(1)} custom-call(bf16[256,1024]{1,0:T(8,128)(2,1)S(1)} %dynamic-slice_bitcast_fusion.events, bf16[2,2048,512]{2,1,0:T(8,128)(2,1)S(1)} %bitcast.16), custom_call_target="tpu_custom_call" | custom-call | flops 536870912 | bytes 3145728 | tf_op jit(solution)/shard_map/own_drive_1/pallas_call | solution.py:295
  13.8 1.2 %fusion.7 = (f32[64,512]{1,0:T(8,128)S(1)}, f32[64,512]{1,0:T(8,128)S(1)}, f32[64,512]{1,0:T(8,128)S(1)}, f32[64,512]{1,0:T(8,128)S(1)}, f32[64,512]{1,0:T(8,128)S(1)}, /*index=5*/f32[64,512]{1,0:T(8,128)S(1)}) fusion(f32[512]{0:T(512)S(1)} %bitcast.24, f32[512]{0:T(512)S(1)} %bitcast.23, f32[64]{0:T(128)S(1)} %copy-done.8, f32[512]{0:T(512)S(1)} %copy-done.6, ...), kind=kLoop, calls=%fused_computation.18 | loop fusion | flops 458752 | bytes 794880 | tf_op jit(solution)/shard_map/mul | solution.py:373
  15.0 1.0 %decays.1 = (f32[3,2,256,512]{3,2,1,0:T(8,128)S(1)}, f32[4,1,512]{2,1,0:T(1,128)S(1)}, f32[2,2,16,512]{3,2,1,0:T(8,128)S(1)}, f32[2,2,16,512]{3,2,1,0:T(8,128)S(1)}, s32[2,1,512]{2,1,0:T(1,128)S(1)}) custom-call(s32[2,256]{1,0:T(2,128)S(1)} %copy-done.4, f32[64,512]{1,0:T(8,128)S(1)} %get-tuple-element.93.refs_0_, f32[64,512]{1,0:T(8,128)S(1)} %get-tuple-element.94.refs_1_, ...), custom_call_target="tpu_custom_call" | custom-call | flops 301989888 | bytes 5242880 | tf_op jit(solution)/shard_map/decays/pallas_call | solution.py:295
  16.0 1.1 %drive_scan_0.1 = (f32[2,2,128,512]{3,2,1,0:T(8,128)S(1)}, f32[2,2,8,512]{3,2,1,0:T(8,128)S(1)}, f32[4,1,512]{2,1,0:T(1,128)S(1)}) custom-call(bf16[128,1024]{1,0:T(8,128)(2,1)S(1)} %collective-permute-done.1.refs_0_, bf16[2,2048,512]{2,1,0:T(8,128)(2,1)S(1)} %bitcast.14, bf16[2,2048,512]{2,1,0:T(8,128)(2,1)S(1)} %bitcast.17, ...), custom_call_target="tpu_custom_call" | custom-call | flops 536870912 | bytes 7340032 | tf_op jit(solution)/shard_map/drive_scan_0/pallas_call | solution.py:295
  17.0 1.1 %drive_scan_1.1 = (f32[2,2,128,512]{3,2,1,0:T(8,128)S(1)}, f32[2,2,8,512]{3,2,1,0:T(8,128)S(1)}, f32[4,1,512]{2,1,0:T(1,128)S(1)}) custom-call(bf16[128,1024]{1,0:T(8,128)(2,1)S(1)} %collective-permute-done.3.refs_0_, bf16[2,2048,512]{2,1,0:T(8,128)(2,1)S(1)} %bitcast.15, bf16[2,2048,512]{2,1,0:T(8,128)(2,1)S(1)} %bitcast.18, ...), custom_call_target="tpu_custom_call" | custom-call | flops 536870912 | bytes 7340032 | tf_op jit(solution)/shard_map/drive_scan_1/pallas_call | solution.py:295
  18.1 0.1 collective-permute-start.4
  18.3 2.2 %hold.1.w_oth = bf16[2,512,2048]{2,1,0:T(8,128)(2,1)S(1)} custom-call(bf16[2,512,2048]{2,1,0:T(8,128)(2,1)} %collective-permute-done.5.source), custom_call_target="tpu_custom_call" | custom-call | bytes 8388608 | tf_op jit(solution)/shard_map/hold/pallas_call | solution.py:295
  20.5 0.4 collective-permute-done.4
  21.0 2.7 %collective-permute-start.6 = (f32[8,1,512]{2,1,0:T(1,128)S(1)}, f32[8,1,512]{2,1,0:T(1,128)S(1)}, u32[]{:S(2)}, u32[]{:S(2)}) collective-permute-start(f32[8,1,512]{2,1,0:T(1,128)S(1)} %pad_maximum_fusion.1), channel_id=1, source_target_pairs={{0,8},{4,12},{8,0},{12,4},{1,9},{5,13},{9,1},{13,5},{2,10},{6,14},... | collective-permute-start | bytes 49160 | tf_op jit(solution)/shard_map/ppermute | solution.py:335
  23.7 0.6 %states.1 = (f32[2,2,256,512]{3,2,1,0:T(8,128)S(1)}, f32[2,2,256,512]{3,2,1,0:T(8,128)S(1)}) custom-call(f32[3,2,256,512]{3,2,1,0:T(8,128)S(1)} %get-tuple-element.40.refs_5_.dec, f32[2,2,16,512]{3,2,1,0:T(8,128)S(1)} %get-tuple-element.48.starts, f32[2,2,128,512]{3,2,1,0:T(8,128)S(1)} %get-tuple-element.49.refs_0_, ...), custom_call_target="tpu_custom_call" | custom-call | bytes 4194304 | tf_op jit(solution)/shard_map/states/pallas_call | solution.py:295
  24.3 0.6 %collective-permute-done.6 = f32[8,1,512]{2,1,0:T(1,128)S(1)} collective-permute-done((f32[8,1,512]{2,1,0:T(1,128)S(1)}, f32[8,1,512]{2,1,0:T(1,128)S(1)}, u32[]{:S(2)}, u32[]{:S(2)}) %collective-permute-start.6) | collective-permute-done | bytes 16416 | tf_op jit(solution)/shard_map/ppermute | solution.py:335
  24.9 1.1 %carry_far.1 = (bf16[2,2,256,512]{3,2,1,0:T(8,128)(2,1)S(1)}, bf16[256,512]{1,0:T(8,128)(2,1)S(1)}) custom-call(f32[4,1,512]{2,1,0:T(1,128)S(1)} %broadcast_select_fusion.3.carry, f32[2,2,256,512]{3,2,1,0:T(8,128)S(1)} %get-tuple-element.53.state, f32[2,2,256,512]{3,2,1,0:T(8,128)S(1)} %get-tuple-element.54.cum, bf16[2,512,2048]{2,1,0:T(8,128)(2,1)S(1)} %copy-done.1, ...), custom_call_target="tpu_custom_call" | custom-call | flops 536870912 | bytes 5242880 | tf_op jit(solution)/shard_map/carry_far/pallas_call | solution.py:295
  26.0 1.3 %collective-permute-start.10 = (bf16[256,512]{1,0:T(8,128)(2,1)S(1)}, bf16[256,512]{1,0:T(8,128)(2,1)S(1)}, u32[]{:S(2)}, u32[]{:S(2)}) collective-permute-start(bf16[256,512]{1,0:T(8,128)(2,1)S(1)} %get-tuple-element.62), channel_id=1, source_target_pairs={{0,2},{1,3},{2,0},{3,1},{4,6},{5,7},{6,4},{7,5},{8,10},{9,11},{10,... | collective-permute-start | bytes 786440 | tf_op jit(solution)/shard_map/ppermute | solution.py:335
  27.4 0.7 %far.1 = bf16[256,512]{1,0:T(8,128)(2,1)S(1)} custom-call(bf16[2,2,256,512]{3,2,1,0:T(8,128)(2,1)S(1)} %get-tuple-element.56.states, bf16[2,512,2048]{2,1,0:T(8,128)(2,1)S(1)} %copy-done.1, bf16[2,512,2048]{2,1,0:T(8,128)(2,1)S(1)} %hold.1.w_oth), custom_call_target="tpu_custom_call" | custom-call | flops 536870912 | bytes 5242880 | tf_op jit(solution)/shard_map/far/pallas_call | solution.py:295
  28.1 2.0 %collective-permute-start.9 = (bf16[256,512]{1,0:T(8,128)(2,1)S(1)}, bf16[256,512]{1,0:T(8,128)(2,1)S(1)}, u32[]{:S(2)}, u32[]{:S(2)}) collective-permute-start(bf16[256,512]{1,0:T(8,128)(2,1)S(1)} %far.1), channel_id=1, source_target_pairs={{0,3},{1,2},{2,1},{3,0},{4,7},{5,6},{6,5},{7,4},{8,11},{9,10},{10,... | collective-permute-start | bytes 786440 | tf_op jit(solution)/shard_map/ppermute | solution.py:335
  30.1 1.2 %near.1 = (f32[256,512]{1,0:T(8,128)S(1)}, bf16[128,512]{1,0:T(8,128)(2,1)S(1)}, bf16[128,512]{1,0:T(8,128)(2,1)S(1)}) custom-call(bf16[2,2,256,512]{3,2,1,0:T(8,128)(2,1)S(1)} %get-tuple-element.56.states, bf16[2,512,2048]{2,1,0:T(8,128)(2,1)S(1)} %copy-done.1, bf16[2,512,2048]{2,1,0:T(8,128)(2,1)S(1)} %hold.1.w_oth), custom_call_target="tpu_custom_call" | custom-call | flops 1073741824 | bytes 5242880 | tf_op jit(solution)/shard_map/near/pallas_call | solution.py:295
  31.4 0.1 collective-permute-start.7
  31.5 0.5 %collective-permute-start.8 = (bf16[128,512]{1,0:T(8,128)(2,1)S(1)}, bf16[128,512]{1,0:T(8,128)(2,1)S(1)}, u32[]{:S(2)}, u32[]{:S(2)}) collective-permute-start(bf16[128,512]{1,0:T(8,128)(2,1)S(1)} %get-tuple-element.58), channel_id=1, source_target_pairs={{0,1},{1,0},{2,3},{3,2},{4,5},{5,4},{6,7},{7,6},{8,9},{9,8},{10,11... | collective-permute-start | bytes 393224 | tf_op jit(solution)/shard_map/ppermute | solution.py:335
  32.0 0.8 %collective-permute-done.7.refs_0_ = bf16[128,512]{1,0:T(8,128)(2,1)S(1)} collective-permute-done((bf16[128,512]{1,0:T(8,128)(2,1)S(1)}, bf16[128,512]{1,0:T(8,128)(2,1)S(1)}, u32[]{:S(2)}, u32[]{:S(2)}) %collective-permute-start.7) | collective-permute-done | bytes 131104 | tf_op jit(solution)/shard_map/ppermute | solution.py:335
  32.8 0.2 collective-permute-done.8.refs_1_
  33.0 0.6 %almost.1 = (f32[256,512]{1,0:T(8,128)S(1)}, f32[256,128]{1,0:T(8,128)S(1)}) custom-call(s32[2]{0:T(128)S(1)} %copy-done.3, bf16[2,256,512]{2,1,0:T(8,128)(2,1)S(1)} %constant_dynamic-slice_fusion.events, f32[1,512]{1,0:T(1,128)S(1)} %bitcast.19, bf16[128,512]{1,0:T(8,128)(2,1)S(1)} %collective-permute-done.7.refs_0_, ...), custom_call_target="tpu_custom_call" | custom-call | bytes 1048576 | tf_op jit(solution)/shard_map/almost/pallas_call | solution.py:295
  33.6 1.5 %same.1.done = bf16[2,256,512]{2,1,0:T(8,128)(2,1)} custom-call(s32[2]{0:T(128)S(1)} %copy-done.3, bf16[2,256,512]{2,1,0:T(8,128)(2,1)S(1)} %constant_dynamic-slice_fusion.events, f32[1,512]{1,0:T(1,128)S(1)} %bitcast.20, f32[256,512]{1,0:T(8,128)S(1)} %get-tuple-element.61.refs_0_, bf16[256,512]{1,0:T(8,128)(2,1)S(1)} %collective-permute-done.10.refs_1_), custom_call_target="tpu_custom_call" | custom-call | bytes 1048576 | tf_op jit(solution)/shard_map/same/pallas_call | solution.py:295
  35.2 4.6 %collective-permute-done.9.last = bf16[256,512]{1,0:T(8,128)(2,1)S(1)} collective-permute-done((bf16[256,512]{1,0:T(8,128)(2,1)S(1)}, bf16[256,512]{1,0:T(8,128)(2,1)S(1)}, u32[]{:S(2)}, u32[]{:S(2)}) %collective-permute-start.9) | collective-permute-done | bytes 262176 | tf_op jit(solution)/shard_map/ppermute | solution.py:335
  39.8 0.9 %final.1 = bf16[2,256,512]{2,1,0:T(8,128)(2,1)} custom-call(f32[256,512]{1,0:T(8,128)S(1)} %get-tuple-element.59.total, f32[256,128]{1,0:T(8,128)S(1)} %get-tuple-element.60.keep, bf16[256,512]{1,0:T(8,128)(2,1)S(1)} %collective-permute-done.9.last, bf16[2,256,512]{2,1,0:T(8,128)(2,1)} %same.1.done), custom_call_target="tpu_custom_call", output_to_operand_aliasing={{}: (3, {})} | custom-call | bytes 1048576 | tf_op jit(solution)/shard_map/final/pallas_call | solution.py:295
  (39 shorter events, 0.4 us)
Async XLA Ops:
  0.0 1.2 %copy-start = (bf16[2,256,1024]{2,1,0:T(8,128)(2,1)S(1)}, bf16[2,256,1024]{2,1,0:T(8,128)(2,1)}, u32[]{:S(2)}) copy-start(bf16[2,256,1024]{2,1,0:T(8,128)(2,1)} %param.9) | copy-start | bytes 3145732
  0.0 10.0 %collective-permute-start.2 = (bf16[2048,2,512]{2,1,0:T(2,128)(2,1)}, bf16[2048,2,512]{2,1,0:T(2,128)(2,1)}, u32[]{:S(2)}, u32[]{:S(2)}) collective-permute-start(bf16[2048,2,512]{2,1,0:T(2,128)(2,1)} %param.15), channel_id=1, source_target_pairs={{0,1},{1,0},{2,3},{3,2},{4,5},{5,4},{6,7},{7,6},{8,9},{9,8},{10,11... | collective-permute-start | bytes 12582920 | tf_op jit(solution)/shard_map/ppermute | solution.py:335
  0.1 18.2 %collective-permute-start.5 = (bf16[2,512,2048]{2,1,0:T(8,128)(2,1)}, bf16[2,512,2048]{2,1,0:T(8,128)(2,1)}, u32[]{:S(2)}, u32[]{:S(2)}) collective-permute-start(bf16[2,512,2048]{2,1,0:T(8,128)(2,1)} %w_own.5), channel_id=1, source_target_pairs={{0,1},{1,0},{2,3},{3,2},{4,5},{5,4},{6,7},{7,6},{8,9},{9,8},{10,11... | collective-permute-start | bytes 12582920 | tf_op jit(solution)/shard_map/ppermute | solution.py:335
  1.4 12.4 %collective-permute-start.1 = (bf16[128,1024]{1,0:T(8,128)(2,1)S(1)}, bf16[128,1024]{1,0:T(8,128)(2,1)S(1)}, u32[]{:S(2)}, u32[]{:S(2)}) collective-permute-start(bf16[128,1024]{1,0:T(8,128)(2,1)S(1)} %get-tuple-element.66), channel_id=1, source_target_pairs={{0,2},{2,0},{1,3},{3,1},{4,6},{6,4},{5,7},{7,5},{8,10},{10,8},{9,1... | collective-permute-start | bytes 786440 | tf_op jit(solution)/shard_map/ppermute | solution.py:335
  3.5 13.6 %collective-permute-start.3 = (bf16[128,1024]{1,0:T(8,128)(2,1)S(1)}, bf16[128,1024]{1,0:T(8,128)(2,1)S(1)}, u32[]{:S(2)}, u32[]{:S(2)}) collective-permute-start(bf16[128,1024]{1,0:T(8,128)(2,1)S(1)} %get-tuple-element.65), channel_id=1, source_target_pairs={{0,2},{2,0},{1,3},{3,1},{4,6},{6,4},{5,7},{7,5},{8,10},{10,8},{9,1... | collective-permute-start | bytes 786440 | tf_op jit(solution)/shard_map/ppermute | solution.py:335
  6.4 0.9 %copy-start.5 = (f32[512]{0:T(512)S(1)}, f32[512]{0:T(512)}, u32[]{:S(2)}) copy-start(f32[512]{0:T(512)} %param.14) | copy-start | bytes 6148
  6.4 0.9 %copy-start.6 = (f32[512]{0:T(512)S(1)}, f32[512]{0:T(512)}, u32[]{:S(2)}) copy-start(f32[512]{0:T(512)} %param.13) | copy-start | bytes 6148
  7.3 6.4 %collective-permute-start = (f32[2,512]{1,0:T(2,128)S(1)}, f32[2,512]{1,0:T(2,128)S(1)}, u32[]{:S(2)}, u32[]{:S(2)}) collective-permute-start(f32[2,512]{1,0:T(2,128)S(1)} %pad_maximum_fusion.2), channel_id=1, source_target_pairs={{0,5},{1,4},{4,1},{5,0},{8,13},{9,12},{12,9},{13,8},{2,7},{3,6},{6... | collective-permute-start | bytes 12296 | tf_op jit(solution)/shard_map/ppermute | solution.py:335
  12.9 0.9 %copy-start.8 = (f32[64]{0:T(128)S(1)}, f32[64]{0:T(128)}, u32[]{:S(2)}) copy-start(f32[64]{0:T(128)} %param.12) | copy-start | bytes 772
  12.9 2.1 %copy-start.4 = (s32[2,256]{1,0:T(2,128)S(1)}, s32[2,256]{1,0:T(2,128)}, u32[]{:S(2)}) copy-start(s32[2,256]{1,0:T(2,128)} %bins.1) | copy-start | bytes 6148
  18.1 2.7 %collective-permute-start.4 = (f32[8,1,512]{2,1,0:T(1,128)S(1)}, f32[8,1,512]{2,1,0:T(1,128)S(1)}, u32[]{:S(2)}, u32[]{:S(2)}) collective-permute-start(f32[8,1,512]{2,1,0:T(1,128)S(1)} %pad_maximum_fusion), channel_id=1, source_target_pairs={{0,4},{4,0},{8,12},{12,8},{1,5},{5,1},{9,13},{13,9},{2,6},{6,2},{1... | collective-permute-start | bytes 49160 | tf_op jit(solution)/shard_map/ppermute | solution.py:335
  18.2 2.7 %copy-start.7 = (f32[4,1,512]{2,1,0:T(1,128)S(1)}, f32[4,1,512]{2,1,0:T(1,128)}, u32[]{:S(2)}) copy-start(f32[4,1,512]{2,1,0:T(1,128)} %constant.27.clone.1) | copy-start | bytes 24580
  20.5 4.5 %copy-start.1 = (bf16[2,512,2048]{2,1,0:T(8,128)(2,1)S(1)}, bf16[2,512,2048]{2,1,0:T(8,128)(2,1)}, u32[]{:S(2)}) copy-start(bf16[2,512,2048]{2,1,0:T(8,128)(2,1)} %w_own.5) | copy-start | bytes 12582916
  21.0 3.9 %collective-permute-start.6 = (f32[8,1,512]{2,1,0:T(1,128)S(1)}, f32[8,1,512]{2,1,0:T(1,128)S(1)}, u32[]{:S(2)}, u32[]{:S(2)}) collective-permute-start(f32[8,1,512]{2,1,0:T(1,128)S(1)} %pad_maximum_fusion.1), channel_id=1, source_target_pairs={{0,8},{4,12},{8,0},{12,4},{1,9},{5,13},{9,1},{13,5},{2,10},{6,14},... | collective-permute-start | bytes 49160 | tf_op jit(solution)/shard_map/ppermute | solution.py:335
  26.0 7.6 %collective-permute-start.10 = (bf16[256,512]{1,0:T(8,128)(2,1)S(1)}, bf16[256,512]{1,0:T(8,128)(2,1)S(1)}, u32[]{:S(2)}, u32[]{:S(2)}) collective-permute-start(bf16[256,512]{1,0:T(8,128)(2,1)S(1)} %get-tuple-element.62), channel_id=1, source_target_pairs={{0,2},{1,3},{2,0},{3,1},{4,6},{5,7},{6,4},{7,5},{8,10},{9,11},{10,... | collective-permute-start | bytes 786440 | tf_op jit(solution)/shard_map/ppermute | solution.py:335
  28.1 4.9 %copy-start.2 = (f32[512]{0:T(512)S(1)}, f32[512]{0:T(512)}, u32[]{:S(2)}) copy-start(f32[512]{0:T(512)} %param.17) | copy-start | bytes 6148
  28.1 4.9 %copy-start.3 = (s32[2]{0:T(128)S(1)}, s32[2]{0:T(128)}, u32[]{:S(2)}) copy-start(s32[2]{0:T(128)} %lengths.3) | copy-start | bytes 28
  28.1 11.6 %collective-permute-start.9 = (bf16[256,512]{1,0:T(8,128)(2,1)S(1)}, bf16[256,512]{1,0:T(8,128)(2,1)S(1)}, u32[]{:S(2)}, u32[]{:S(2)}) collective-permute-start(bf16[256,512]{1,0:T(8,128)(2,1)S(1)} %far.1), channel_id=1, source_target_pairs={{0,3},{1,2},{2,1},{3,0},{4,7},{5,6},{6,5},{7,4},{8,11},{9,10},{10,... | collective-permute-start | bytes 786440 | tf_op jit(solution)/shard_map/ppermute | solution.py:335
  31.4 1.4 %collective-permute-start.7 = (bf16[128,512]{1,0:T(8,128)(2,1)S(1)}, bf16[128,512]{1,0:T(8,128)(2,1)S(1)}, u32[]{:S(2)}, u32[]{:S(2)}) collective-permute-start(bf16[128,512]{1,0:T(8,128)(2,1)S(1)} %get-tuple-element.57), channel_id=1, source_target_pairs={{0,1},{1,0},{2,3},{3,2},{4,5},{5,4},{6,7},{7,6},{8,9},{9,8},{10,11... | collective-permute-start | bytes 393224 | tf_op jit(solution)/shard_map/ppermute | solution.py:335
  31.5 1.5 %collective-permute-start.8 = (bf16[128,512]{1,0:T(8,128)(2,1)S(1)}, bf16[128,512]{1,0:T(8,128)(2,1)S(1)}, u32[]{:S(2)}, u32[]{:S(2)}) collective-permute-start(bf16[128,512]{1,0:T(8,128)(2,1)S(1)} %get-tuple-element.58), channel_id=1, source_target_pairs={{0,1},{1,0},{2,3},{3,2},{4,5},{5,4},{6,7},{7,6},{8,9},{9,8},{10,11... | collective-permute-start | bytes 393224 | tf_op jit(solution)/shard_map/ppermute | solution.py:335

commit v8 on v7

--- a/solution.py
+++ b/solution.py
@@ -122,16 +122,20 @@
                 state[1, h, at, :] = si
 
 
-def own_kernel(tokens, events, w, out):
+def own_kernel(tokens, ordered, events, w, out, *rows):
     chan = lax.axis_index("chan")
     seg_rows, width = events.shape
-    order = order_matrix(tokens)
-    rows = jnp.concatenate(
-        [dot(order, events[u : u + tokens, :]).astype(BF16) for u in range(0, seg_rows, tokens)], 0
-    )
+    if ordered:
+        moved = events[...]
+    else:
+        order = order_matrix(tokens)
+        moved = jnp.concatenate(
+            [dot(order, events[u : u + tokens, :]).astype(BF16) for u in range(0, seg_rows, tokens)], 0
+        )
+        rows[0][...] = moved
     start = pl.ds(pl.multiple_of(chan * width, width), width)
     for c in range(2):
-        out[c] = dot(rows, w[c, start, :])
+        out[c] = dot(moved, w[c, start, :])
 
 
 def scan_kernel(tokens, peers, chunk, *refs):
@@ -349,17 +353,18 @@
     w_own = jnp.transpose(in_proj, (1, 0, 2))
     w_oth = jnp.transpose(raw_oth, (1, 0, 2))
 
-    parts = [
-        call(
-            functools.partial(own_kernel, tokens),
+    def own_drive(h, given, w, more):
+        return call(
+            functools.partial(own_kernel, tokens, h > 0),
             "own_drive_%d" % h,
-            (own_rows, w),
-            shape((2, rows, q), F32),
+            (given, w),
+            (shape((2, rows, q), F32),) + more,
             flops=2 * rows * width * 2 * q,
             bytes_=2 * width * q * 2 + 2 * rows * q * 4,
         )
-        for h, w in enumerate((w_own, w_oth))
-    ]
+
+    part, ordered = own_drive(0, own_rows, w_own, (shape((rows, width), BF16),))
+    parts = [part, own_drive(1, ordered, w_oth, ())[0]]
     rates, _ = lax.optimization_barrier((jnp.stack([decay_rate, frequency]), parts[0]))
     rates_oth = swap(rates, ("ctx", "grp"), ctxs * grps, 3 if ctxs > 1 else 1)
     rates_oth, peer_rows[0], _ = lax.optimization_barrier((rates_oth, peer_rows[0], parts[1]))

time: 40.9 us -> 40.7 us (level)
  starting transfers between devices: 12.1 us -> 11.6 us
  waiting for transfers between devices: 6.58 us -> 6.99 us
    ppermute x11, starting transfers between devices: 12.1 us -> 11.6 us  [swap(): return lax.ppermute(array, axes, [(i, i ^ k) for i in range(size)])]
  transfers between devices with their start and end apart: 11 -> 11, of which waited for: 5 -> 5; matrix products, arithmetic and copies ran while one was open for 17% -> 18% of each run, Pallas kernels for 29% -> 28%
where the time goes in v8:
time: 40.7 us; the launch traced here: 40.4 us
  Pallas kernels  13.5 us (33%)
  starting transfers between devices  11.6 us (29%)
  waiting for transfers between devices  6.99 us (17%)
  local copies, waits for them, and re-layouts  6.61 us (16%)
  other arithmetic  1.37 us (3%)
    pallas_call x13, Pallas kernels, call(): pl.pallas_call(body, name=name, out_shape=out_shape, in_specs=in_specs or...  13.5 us
    ppermute x11, starting transfers between devices, swap(): return lax.ppermute(array, axes, [(i, i ^ k) for i in range(size)])  11.6 us
    ppermute x11, waiting for transfers between devices, swap(): return lax.ppermute(array, axes, [(i, i ^ k) for i in range(size)])  6.99 us
    unnamed x19, local copies, waits for them, and re-layouts  3.63 us
    another operation x1, local copies, waits for them, and re-layouts, local(): raw_oth = with_layout_constraint(raw_oth, stored)  2.86 us
    mul x1, other arithmetic, tables(): magnitude * jnp.sin(turned)  1.17 us
  transfers between devices with their start and end apart: 11, of which 5 were waited for; matrix products, arithmetic and copies ran while one was open for 18% of the time, Pallas kernels for 28%

profile of v8, /device:TPU:1, one launch (start us, length us, event | category | flops | bytes accessed | tf_op | source)
XLA Modules:
  0.0 40.4 jit_solution(10967020476482106585)
XLA Ops:
  0.1 0.5 %collective-permute-start.5 = (bf16[2,512,2048]{2,1,0:T(8,128)(2,1)}, bf16[2,512,2048]{2,1,0:T(8,128)(2,1)}, u32[]{:S(2)}, u32[]{:S(2)}) collective-permute-start(bf16[2,512,2048]{2,1,0:T(8,128)(2,1)} %w_own.5), channel_id=1, source_target_pairs={{0,1},{1,0},{2,3},{3,2},{4,5},{5,4},{6,7},{7,6},{8,9},{9,8},{10,11... | collective-permute-start | bytes 12582920 | tf_op jit(solution)/shard_map/ppermute | solution.py:339
  0.5 0.7 %copy-done = bf16[2,256,1024]{2,1,0:T(8,128)(2,1)S(1)} copy-done((bf16[2,256,1024]{2,1,0:T(8,128)(2,1)S(1)}, bf16[2,256,1024]{2,1,0:T(8,128)(2,1)}, u32[]{:S(2)}) %copy-start) | copy-done | bytes 1048600
  1.4 2.1 %collective-permute-start.1 = (bf16[128,1024]{1,0:T(8,128)(2,1)S(1)}, bf16[128,1024]{1,0:T(8,128)(2,1)S(1)}, u32[]{:S(2)}, u32[]{:S(2)}) collective-permute-start(bf16[128,1024]{1,0:T(8,128)(2,1)S(1)} %get-tuple-element.70), channel_id=1, source_target_pairs={{0,2},{2,0},{1,3},{3,1},{4,6},{6,4},{5,7},{7,5},{8,10},{10,8},{9,1... | collective-permute-start | bytes 786440 | tf_op jit(solution)/shard_map/ppermute | solution.py:339
  3.5 0.1 collective-permute-start.3
  3.5 2.9 %copy.16 = bf16[2048,2,512]{2,0,1:T(8,128)(2,1)S(1)} copy(bf16[2048,2,512]{2,1,0:T(2,128)(2,1)} %param.15) | data formatting | bytes 8388608 | tf_op args[6]
  6.4 0.9 %own_drive_0.1 = (f32[2,256,512]{2,1,0:T(8,128)S(1)}, bf16[256,1024]{1,0:T(8,128)(2,1)S(1)}) custom-call(bf16[256,1024]{1,0:T(8,128)(2,1)S(1)} %dynamic-slice_bitcast_fusion.events, bf16[2,2048,512]{2,1,0:T(8,128)(2,1)S(1)} %bitcast.13), custom_call_target="tpu_custom_call" | custom-call | flops 536870912 | bytes 3145728 | tf_op jit(solution)/shard_map/own_drive_0/pallas_call | solution.py:299
  7.3 2.7 %collective-permute-start = (f32[2,512]{1,0:T(2,128)S(1)}, f32[2,512]{1,0:T(2,128)S(1)}, u32[]{:S(2)}, u32[]{:S(2)}) collective-permute-start(f32[2,512]{1,0:T(2,128)S(1)} %pad_maximum_fusion.2), channel_id=1, source_target_pairs={{0,5},{1,4},{4,1},{5,0},{8,13},{9,12},{12,9},{13,8},{2,7},{3,6},{6... | collective-permute-start | bytes 12296 | tf_op jit(solution)/shard_map/ppermute | solution.py:339
  10.0 2.9 %copy.15 = bf16[2048,2,512]{2,0,1:T(8,128)(2,1)S(1)} copy(bf16[2048,2,512]{2,1,0:T(2,128)(2,1)} %collective-permute-done.2) | data formatting | bytes 8388608 | tf_op jit(solution)/shard_map/layout_constraint | solution.py:351
  12.9 0.7 %own_drive_1.1.refs_4_ = f32[2,256,512]{2,1,0:T(8,128)S(1)} custom-call(bf16[256,1024]{1,0:T(8,128)(2,1)S(1)} %get-tuple-element.40.events, bf16[2,2048,512]{2,1,0:T(8,128)(2,1)S(1)} %bitcast.16), custom_call_target="tpu_custom_call" | custom-call | flops 536870912 | bytes 3145728 | tf_op jit(solution)/shard_map/own_drive_1/pallas_call | solution.py:299
  13.7 1.2 %fusion.7 = (f32[64,512]{1,0:T(8,128)S(1)}, f32[64,512]{1,0:T(8,128)S(1)}, f32[64,512]{1,0:T(8,128)S(1)}, f32[64,512]{1,0:T(8,128)S(1)}, f32[64,512]{1,0:T(8,128)S(1)}, /*index=5*/f32[64,512]{1,0:T(8,128)S(1)}) fusion(f32[512]{0:T(512)S(1)} %bitcast.24, f32[512]{0:T(512)S(1)} %bitcast.23, f32[64]{0:T(128)S(1)} %copy-done.8, f32[512]{0:T(512)S(1)} %copy-done.6, ...), kind=kLoop, calls=%fused_computation.18 | loop fusion | flops 458752 | bytes 794880 | tf_op jit(solution)/shard_map/mul | solution.py:378
  14.8 1.0 %decays.1 = (f32[3,2,256,512]{3,2,1,0:T(8,128)S(1)}, f32[4,1,512]{2,1,0:T(1,128)S(1)}, f32[2,2,16,512]{3,2,1,0:T(8,128)S(1)}, f32[2,2,16,512]{3,2,1,0:T(8,128)S(1)}, s32[2,1,512]{2,1,0:T(1,128)S(1)}) custom-call(s32[2,256]{1,0:T(2,128)S(1)} %copy-done.4, f32[64,512]{1,0:T(8,128)S(1)} %get-tuple-element.97.refs_0_, f32[64,512]{1,0:T(8,128)S(1)} %get-tuple-element.98.refs_1_, ...), custom_call_target="tpu_custom_call" | custom-call | flops 301989888 | bytes 5242880 | tf_op jit(solution)/shard_map/decays/pallas_call | solution.py:299
  15.8 1.1 %drive_scan_0.1 = (f32[2,2,128,512]{3,2,1,0:T(8,128)S(1)}, f32[2,2,8,512]{3,2,1,0:T(8,128)S(1)}, f32[4,1,512]{2,1,0:T(1,128)S(1)}) custom-call(bf16[128,1024]{1,0:T(8,128)(2,1)S(1)} %collective-permute-done.1.refs_0_, bf16[2,2048,512]{2,1,0:T(8,128)(2,1)S(1)} %bitcast.14, bf16[2,2048,512]{2,1,0:T(8,128)(2,1)S(1)} %bitcast.17, ...), custom_call_target="tpu_custom_call" | custom-call | flops 536870912 | bytes 7340032 | tf_op jit(solution)/shard_map/drive_scan_0/pallas_call | solution.py:299
  16.9 1.1 %drive_scan_1.1 = (f32[2,2,128,512]{3,2,1,0:T(8,128)S(1)}, f32[2,2,8,512]{3,2,1,0:T(8,128)S(1)}, f32[4,1,512]{2,1,0:T(1,128)S(1)}) custom-call(bf16[128,1024]{1,0:T(8,128)(2,1)S(1)} %collective-permute-done.3.refs_0_, bf16[2,2048,512]{2,1,0:T(8,128)(2,1)S(1)} %bitcast.15, bf16[2,2048,512]{2,1,0:T(8,128)(2,1)S(1)} %bitcast.18, ...), custom_call_target="tpu_custom_call" | custom-call | flops 536870912 | bytes 7340032 | tf_op jit(solution)/shard_map/drive_scan_1/pallas_call | solution.py:299
  18.0 0.1 collective-permute-start.4
  18.1 2.2 %hold.1.w_oth = bf16[2,512,2048]{2,1,0:T(8,128)(2,1)S(1)} custom-call(bf16[2,512,2048]{2,1,0:T(8,128)(2,1)} %collective-permute-done.5.source), custom_call_target="tpu_custom_call" | custom-call | bytes 8388608 | tf_op jit(solution)/shard_map/hold/pallas_call | solution.py:299
  20.3 0.6 %collective-permute-done.4 = f32[8,1,512]{2,1,0:T(1,128)S(1)} collective-permute-done((f32[8,1,512]{2,1,0:T(1,128)S(1)}, f32[8,1,512]{2,1,0:T(1,128)S(1)}, u32[]{:S(2)}, u32[]{:S(2)}) %collective-permute-start.4) | collective-permute-done | bytes 16416 | tf_op jit(solution)/shard_map/ppermute | solution.py:339
  21.1 2.0 %collective-permute-start.6 = (f32[8,1,512]{2,1,0:T(1,128)S(1)}, f32[8,1,512]{2,1,0:T(1,128)S(1)}, u32[]{:S(2)}, u32[]{:S(2)}) collective-permute-start(f32[8,1,512]{2,1,0:T(1,128)S(1)} %pad_maximum_fusion.1), channel_id=1, source_target_pairs={{0,8},{4,12},{8,0},{12,4},{1,9},{5,13},{9,1},{13,5},{2,10},{6,14},... | collective-permute-start | bytes 49160 | tf_op jit(solution)/shard_map/ppermute | solution.py:339
  23.2 0.6 %states.1 = (f32[2,2,256,512]{3,2,1,0:T(8,128)S(1)}, f32[2,2,256,512]{3,2,1,0:T(8,128)S(1)}) custom-call(f32[3,2,256,512]{3,2,1,0:T(8,128)S(1)} %get-tuple-element.44.refs_5_.dec, f32[2,2,16,512]{3,2,1,0:T(8,128)S(1)} %get-tuple-element.52.starts, f32[2,2,128,512]{3,2,1,0:T(8,128)S(1)} %get-tuple-element.53.refs_0_, ...), custom_call_target="tpu_custom_call" | custom-call | bytes 4194304 | tf_op jit(solution)/shard_map/states/pallas_call | solution.py:299
  23.7 1.0 %collective-permute-done.6 = f32[8,1,512]{2,1,0:T(1,128)S(1)} collective-permute-done((f32[8,1,512]{2,1,0:T(1,128)S(1)}, f32[8,1,512]{2,1,0:T(1,128)S(1)}, u32[]{:S(2)}, u32[]{:S(2)}) %collective-permute-start.6) | collective-permute-done | bytes 16416 | tf_op jit(solution)/shard_map/ppermute | solution.py:339
  24.7 1.1 %carry_far.1 = (bf16[2,2,256,512]{3,2,1,0:T(8,128)(2,1)S(1)}, bf16[256,512]{1,0:T(8,128)(2,1)S(1)}) custom-call(f32[4,1,512]{2,1,0:T(1,128)S(1)} %broadcast_select_fusion.3.carry, f32[2,2,256,512]{3,2,1,0:T(8,128)S(1)} %get-tuple-element.57.state, f32[2,2,256,512]{3,2,1,0:T(8,128)S(1)} %get-tuple-element.58.cum, bf16[2,512,2048]{2,1,0:T(8,128)(2,1)S(1)} %copy-done.1, ...), custom_call_target="tpu_custom_call" | custom-call | flops 536870912 | bytes 5242880 | tf_op jit(solution)/shard_map/carry_far/pallas_call | solution.py:299
  25.8 0.9 %collective-permute-start.10 = (bf16[256,512]{1,0:T(8,128)(2,1)S(1)}, bf16[256,512]{1,0:T(8,128)(2,1)S(1)}, u32[]{:S(2)}, u32[]{:S(2)}) collective-permute-start(bf16[256,512]{1,0:T(8,128)(2,1)S(1)} %get-tuple-element.66), channel_id=1, source_target_pairs={{0,2},{1,3},{2,0},{3,1},{4,6},{5,7},{6,4},{7,5},{8,10},{9,11},{10,... | collective-permute-start | bytes 786440 | tf_op jit(solution)/shard_map/ppermute | solution.py:339
  26.8 0.7 %far.1 = bf16[256,512]{1,0:T(8,128)(2,1)S(1)} custom-call(bf16[2,2,256,512]{3,2,1,0:T(8,128)(2,1)S(1)} %get-tuple-element.60.states, bf16[2,512,2048]{2,1,0:T(8,128)(2,1)S(1)} %copy-done.1, bf16[2,512,2048]{2,1,0:T(8,128)(2,1)S(1)} %hold.1.w_oth), custom_call_target="tpu_custom_call" | custom-call | flops 536870912 | bytes 5242880 | tf_op jit(solution)/shard_map/far/pallas_call | solution.py:299
  27.5 2.6 %collective-permute-start.9 = (bf16[256,512]{1,0:T(8,128)(2,1)S(1)}, bf16[256,512]{1,0:T(8,128)(2,1)S(1)}, u32[]{:S(2)}, u32[]{:S(2)}) collective-permute-start(bf16[256,512]{1,0:T(8,128)(2,1)S(1)} %far.1), channel_id=1, source_target_pairs={{0,3},{1,2},{2,1},{3,0},{4,7},{5,6},{6,5},{7,4},{8,11},{9,10},{10,... | collective-permute-start | bytes 786440 | tf_op jit(solution)/shard_map/ppermute | solution.py:339
  30.2 1.2 %near.1 = (f32[256,512]{1,0:T(8,128)S(1)}, bf16[128,512]{1,0:T(8,128)(2,1)S(1)}, bf16[128,512]{1,0:T(8,128)(2,1)S(1)}) custom-call(bf16[2,2,256,512]{3,2,1,0:T(8,128)(2,1)S(1)} %get-tuple-element.60.states, bf16[2,512,2048]{2,1,0:T(8,128)(2,1)S(1)} %copy-done.1, bf16[2,512,2048]{2,1,0:T(8,128)(2,1)S(1)} %hold.1.w_oth), custom_call_target="tpu_custom_call" | custom-call | flops 1073741824 | bytes 5242880 | tf_op jit(solution)/shard_map/near/pallas_call | solution.py:299
  31.4 0.1 collective-permute-start.7
  31.5 0.5 %collective-permute-start.8 = (bf16[128,512]{1,0:T(8,128)(2,1)S(1)}, bf16[128,512]{1,0:T(8,128)(2,1)S(1)}, u32[]{:S(2)}, u32[]{:S(2)}) collective-permute-start(bf16[128,512]{1,0:T(8,128)(2,1)S(1)} %get-tuple-element.62), channel_id=1, source_target_pairs={{0,1},{1,0},{2,3},{3,2},{4,5},{5,4},{6,7},{7,6},{8,9},{9,8},{10,11... | collective-permute-start | bytes 393224 | tf_op jit(solution)/shard_map/ppermute | solution.py:339
  32.0 0.8 %collective-permute-done.7.refs_0_ = bf16[128,512]{1,0:T(8,128)(2,1)S(1)} collective-permute-done((bf16[128,512]{1,0:T(8,128)(2,1)S(1)}, bf16[128,512]{1,0:T(8,128)(2,1)S(1)}, u32[]{:S(2)}, u32[]{:S(2)}) %collective-permute-start.7) | collective-permute-done | bytes 131104 | tf_op jit(solution)/shard_map/ppermute | solution.py:339
  32.8 0.2 collective-permute-done.8.refs_1_
  33.0 0.6 %almost.1 = (f32[256,512]{1,0:T(8,128)S(1)}, f32[256,128]{1,0:T(8,128)S(1)}) custom-call(s32[2]{0:T(128)S(1)} %copy-done.3, bf16[2,256,512]{2,1,0:T(8,128)(2,1)S(1)} %constant_dynamic-slice_fusion.events, f32[1,512]{1,0:T(1,128)S(1)} %bitcast.19, bf16[128,512]{1,0:T(8,128)(2,1)S(1)} %collective-permute-done.7.refs_0_, ...), custom_call_target="tpu_custom_call" | custom-call | bytes 1048576 | tf_op jit(solution)/shard_map/almost/pallas_call | solution.py:299
  33.7 1.5 %same.1.done = bf16[2,256,512]{2,1,0:T(8,128)(2,1)} custom-call(s32[2]{0:T(128)S(1)} %copy-done.3, bf16[2,256,512]{2,1,0:T(8,128)(2,1)S(1)} %constant_dynamic-slice_fusion.events, f32[1,512]{1,0:T(1,128)S(1)} %bitcast.20, f32[256,512]{1,0:T(8,128)S(1)} %get-tuple-element.65.refs_0_, bf16[256,512]{1,0:T(8,128)(2,1)S(1)} %collective-permute-done.10.refs_1_), custom_call_target="tpu_custom_call" | custom-call | bytes 1048576 | tf_op jit(solution)/shard_map/same/pallas_call | solution.py:299
  35.2 4.4 %collective-permute-done.9.last = bf16[256,512]{1,0:T(8,128)(2,1)S(1)} collective-permute-done((bf16[256,512]{1,0:T(8,128)(2,1)S(1)}, bf16[256,512]{1,0:T(8,128)(2,1)S(1)}, u32[]{:S(2)}, u32[]{:S(2)}) %collective-permute-start.9) | collective-permute-done | bytes 262176 | tf_op jit(solution)/shard_map/ppermute | solution.py:339
  39.5 0.9 %final.1 = bf16[2,256,512]{2,1,0:T(8,128)(2,1)} custom-call(f32[256,512]{1,0:T(8,128)S(1)} %get-tuple-element.63.total, f32[256,128]{1,0:T(8,128)S(1)} %get-tuple-element.64.keep, bf16[256,512]{1,0:T(8,128)(2,1)S(1)} %collective-permute-done.9.last, bf16[2,256,512]{2,1,0:T(8,128)(2,1)} %same.1.done), custom_call_target="tpu_custom_call", output_to_operand_aliasing={{}: (3, {})} | custom-call | bytes 1048576 | tf_op jit(solution)/shard_map/final/pallas_call | solution.py:299
  (39 shorter events, 0.4 us)
Async XLA Ops:
  0.0 1.2 %copy-start = (bf16[2,256,1024]{2,1,0:T(8,128)(2,1)S(1)}, bf16[2,256,1024]{2,1,0:T(8,128)(2,1)}, u32[]{:S(2)}) copy-start(bf16[2,256,1024]{2,1,0:T(8,128)(2,1)} %param.9) | copy-start | bytes 3145732
  0.0 10.0 %collective-permute-start.2 = (bf16[2048,2,512]{2,1,0:T(2,128)(2,1)}, bf16[2048,2,512]{2,1,0:T(2,128)(2,1)}, u32[]{:S(2)}, u32[]{:S(2)}) collective-permute-start(bf16[2048,2,512]{2,1,0:T(2,128)(2,1)} %param.15), channel_id=1, source_target_pairs={{0,1},{1,0},{2,3},{3,2},{4,5},{5,4},{6,7},{7,6},{8,9},{9,8},{10,11... | collective-permute-start | bytes 12582920 | tf_op jit(solution)/shard_map/ppermute | solution.py:339
  0.1 18.0 %collective-permute-start.5 = (bf16[2,512,2048]{2,1,0:T(8,128)(2,1)}, bf16[2,512,2048]{2,1,0:T(8,128)(2,1)}, u32[]{:S(2)}, u32[]{:S(2)}) collective-permute-start(bf16[2,512,2048]{2,1,0:T(8,128)(2,1)} %w_own.5), channel_id=1, source_target_pairs={{0,1},{1,0},{2,3},{3,2},{4,5},{5,4},{6,7},{7,6},{8,9},{9,8},{10,11... | collective-permute-start | bytes 12582920 | tf_op jit(solution)/shard_map/ppermute | solution.py:339
  1.4 12.3 %collective-permute-start.1 = (bf16[128,1024]{1,0:T(8,128)(2,1)S(1)}, bf16[128,1024]{1,0:T(8,128)(2,1)S(1)}, u32[]{:S(2)}, u32[]{:S(2)}) collective-permute-start(bf16[128,1024]{1,0:T(8,128)(2,1)S(1)} %get-tuple-element.70), channel_id=1, source_target_pairs={{0,2},{2,0},{1,3},{3,1},{4,6},{6,4},{5,7},{7,5},{8,10},{10,8},{9,1... | collective-permute-start | bytes 786440 | tf_op jit(solution)/shard_map/ppermute | solution.py:339
  3.5 13.4 %collective-permute-start.3 = (bf16[128,1024]{1,0:T(8,128)(2,1)S(1)}, bf16[128,1024]{1,0:T(8,128)(2,1)S(1)}, u32[]{:S(2)}, u32[]{:S(2)}) collective-permute-start(bf16[128,1024]{1,0:T(8,128)(2,1)S(1)} %get-tuple-element.69), channel_id=1, source_target_pairs={{0,2},{2,0},{1,3},{3,1},{4,6},{6,4},{5,7},{7,5},{8,10},{10,8},{9,1... | collective-permute-start | bytes 786440 | tf_op jit(solution)/shard_map/ppermute | solution.py:339
  6.4 0.9 %copy-start.5 = (f32[512]{0:T(512)S(1)}, f32[512]{0:T(512)}, u32[]{:S(2)}) copy-start(f32[512]{0:T(512)} %param.14) | copy-start | bytes 6148
  6.4 0.9 %copy-start.6 = (f32[512]{0:T(512)S(1)}, f32[512]{0:T(512)}, u32[]{:S(2)}) copy-start(f32[512]{0:T(512)} %param.13) | copy-start | bytes 6148
  7.3 6.3 %collective-permute-start = (f32[2,512]{1,0:T(2,128)S(1)}, f32[2,512]{1,0:T(2,128)S(1)}, u32[]{:S(2)}, u32[]{:S(2)}) collective-permute-start(f32[2,512]{1,0:T(2,128)S(1)} %pad_maximum_fusion.2), channel_id=1, source_target_pairs={{0,5},{1,4},{4,1},{5,0},{8,13},{9,12},{12,9},{13,8},{2,7},{3,6},{6... | collective-permute-start | bytes 12296 | tf_op jit(solution)/shard_map/ppermute | solution.py:339
  12.9 0.8 %copy-start.8 = (f32[64]{0:T(128)S(1)}, f32[64]{0:T(128)}, u32[]{:S(2)}) copy-start(f32[64]{0:T(128)} %param.12) | copy-start | bytes 772
  12.9 2.0 %copy-start.4 = (s32[2,256]{1,0:T(2,128)S(1)}, s32[2,256]{1,0:T(2,128)}, u32[]{:S(2)}) copy-start(s32[2,256]{1,0:T(2,128)} %bins.1) | copy-start | bytes 6148
  18.0 3.0 %collective-permute-start.4 = (f32[8,1,512]{2,1,0:T(1,128)S(1)}, f32[8,1,512]{2,1,0:T(1,128)S(1)}, u32[]{:S(2)}, u32[]{:S(2)}) collective-permute-start(f32[8,1,512]{2,1,0:T(1,128)S(1)} %pad_maximum_fusion), channel_id=1, source_target_pairs={{0,4},{4,0},{8,12},{12,8},{1,5},{5,1},{9,13},{13,9},{2,6},{6,2},{1... | collective-permute-start | bytes 49160 | tf_op jit(solution)/shard_map/ppermute | solution.py:339
  18.1 2.9 %copy-start.7 = (f32[4,1,512]{2,1,0:T(1,128)S(1)}, f32[4,1,512]{2,1,0:T(1,128)}, u32[]{:S(2)}) copy-start(f32[4,1,512]{2,1,0:T(1,128)} %constant.27.clone.1) | copy-start | bytes 24580
  20.3 4.4 %copy-start.1 = (bf16[2,512,2048]{2,1,0:T(8,128)(2,1)S(1)}, bf16[2,512,2048]{2,1,0:T(8,128)(2,1)}, u32[]{:S(2)}) copy-start(bf16[2,512,2048]{2,1,0:T(8,128)(2,1)} %w_own.5) | copy-start | bytes 12582916
  21.1 3.6 %collective-permute-start.6 = (f32[8,1,512]{2,1,0:T(1,128)S(1)}, f32[8,1,512]{2,1,0:T(1,128)S(1)}, u32[]{:S(2)}, u32[]{:S(2)}) collective-permute-start(f32[8,1,512]{2,1,0:T(1,128)S(1)} %pad_maximum_fusion.1), channel_id=1, source_target_pairs={{0,8},{4,12},{8,0},{12,4},{1,9},{5,13},{9,1},{13,5},{2,10},{6,14},... | collective-permute-start | bytes 49160 | tf_op jit(solution)/shard_map/ppermute | solution.py:339
  25.8 7.8 %collective-permute-start.10 = (bf16[256,512]{1,0:T(8,128)(2,1)S(1)}, bf16[256,512]{1,0:T(8,128)(2,1)S(1)}, u32[]{:S(2)}, u32[]{:S(2)}) collective-permute-start(bf16[256,512]{1,0:T(8,128)(2,1)S(1)} %get-tuple-element.66), channel_id=1, source_target_pairs={{0,2},{1,3},{2,0},{3,1},{4,6},{5,7},{6,4},{7,5},{8,10},{9,11},{10,... | collective-permute-start | bytes 786440 | tf_op jit(solution)/shard_map/ppermute | solution.py:339
  27.5 5.5 %copy-start.2 = (f32[512]{0:T(512)S(1)}, f32[512]{0:T(512)}, u32[]{:S(2)}) copy-start(f32[512]{0:T(512)} %param.17) | copy-start | bytes 6148
  27.5 5.5 %copy-start.3 = (s32[2]{0:T(128)S(1)}, s32[2]{0:T(128)}, u32[]{:S(2)}) copy-start(s32[2]{0:T(128)} %lengths.3) | copy-start | bytes 28
  27.5 12.0 %collective-permute-start.9 = (bf16[256,512]{1,0:T(8,128)(2,1)S(1)}, bf16[256,512]{1,0:T(8,128)(2,1)S(1)}, u32[]{:S(2)}, u32[]{:S(2)}) collective-permute-start(bf16[256,512]{1,0:T(8,128)(2,1)S(1)} %far.1), channel_id=1, source_target_pairs={{0,3},{1,2},{2,1},{3,0},{4,7},{5,6},{6,5},{7,4},{8,11},{9,10},{10,... | collective-permute-start | bytes 786440 | tf_op jit(solution)/shard_map/ppermute | solution.py:339
  31.4 1.4 %collective-permute-start.7 = (bf16[128,512]{1,0:T(8,128)(2,1)S(1)}, bf16[128,512]{1,0:T(8,128)(2,1)S(1)}, u32[]{:S(2)}, u32[]{:S(2)}) collective-permute-start(bf16[128,512]{1,0:T(8,128)(2,1)S(1)} %get-tuple-element.61), channel_id=1, source_target_pairs={{0,1},{1,0},{2,3},{3,2},{4,5},{5,4},{6,7},{7,6},{8,9},{9,8},{10,11... | collective-permute-start | bytes 393224 | tf_op jit(solution)/shard_map/ppermute | solution.py:339
  31.5 1.5 %collective-permute-start.8 = (bf16[128,512]{1,0:T(8,128)(2,1)S(1)}, bf16[128,512]{1,0:T(8,128)(2,1)S(1)}, u32[]{:S(2)}, u32[]{:S(2)}) collective-permute-start(bf16[128,512]{1,0:T(8,128)(2,1)S(1)} %get-tuple-element.62), channel_id=1, source_target_pairs={{0,1},{1,0},{2,3},{3,2},{4,5},{5,4},{6,7},{7,6},{8,9},{9,8},{10,11... | collective-permute-start | bytes 393224 | tf_op jit(solution)/shard_map/ppermute | solution.py:339
